TPU v7x, 32 devices: a whole 2x2x4 slice. The times are simulated.
32 devices in a mesh: seq: 8 (over z, x), head: 4 (over y, core).
Axes of the slice: x: 2, y: 2, z: 4, core: 2. Of those that a mesh axis runs over, the one named last changes fastest.
Arguments:
- queries: bfloat16 [8192, 8192], P('seq', 'head'), may hold values from -6 to 6
- key_vectors: bfloat16 [8192, 8192], P('seq', 'head'), may hold values from -6 to 6
- value_vectors: bfloat16 [8192, 8192], P('seq', 'head'), may hold values from -6 to 6
- level_weight: float32 [8192, 1024], P('seq', 'head'), may hold values from 0.02 to 1
- gate_values: bfloat16 [8192, 8192], P(('seq', 'head')), may hold values from -6 to 6
- norm_gain: float32 [8192], replicated, may hold values from 0.5 to 1.5
Outputs:
- normed: bfloat16 [8192, 8192], P(('seq', 'head'))
All inputs are finite; a program needn't handle non-finite values.
Results may differ from a plain program's by a relative error of at most 0.012.
Values may be sent and summed in bfloat16 or wider, within the bound.
No kernel may reach another device: no remote copies, remote signals or barrier semaphores. Data moves between devices by JAX's collectives and lax.ppermute only.
A program may use at most 128 MiB of HBM per device.

v0:
```python
import jax
import jax.numpy as jnp
from jax import lax
from jax.sharding import PartitionSpec as P

HEAD_DIM = 128
LEVELS = 16


def bit_levels(count):
    indices = jnp.arange(count, dtype=jnp.int32)
    mixed = jnp.bitwise_xor(indices[:, None], indices[None, :])
    levels = jnp.zeros((count, count), jnp.int32)
    for height in range(count.bit_length() - 1):
        levels = levels + (mixed >= 1 << height).astype(jnp.int32)
    causal = indices[None, :] <= indices[:, None]
    return (levels, causal)


def local_attention(query_head, key_head, value_head, weight_head, levels, causal):
    scores = jnp.dot(query_head, key_head.T, preferred_element_type=jnp.float32)
    factor = jnp.zeros(scores.shape, jnp.float32)
    for height in range(query_head.shape[0].bit_length()):
        factor = factor + jnp.where(
            levels == height, weight_head[:, height : height + 1], jnp.float32(0.0)
        )
    weighted = jnp.where(causal, scores * factor, jnp.float32(0.0)).astype(jnp.bfloat16)
    return jnp.dot(weighted, value_head, preferred_element_type=jnp.float32)


def per_device(queries, key_vectors, value_vectors, level_weight, gate_values, norm_gain):
    count, features = queries.shape
    heads_here = features // HEAD_DIM
    query_rows = queries.reshape(count, heads_here, HEAD_DIM)
    key_rows = key_vectors.reshape(count, heads_here, HEAD_DIM)
    value_rows = value_vectors.reshape(count, heads_here, HEAD_DIM)
    weight_rows = level_weight.reshape(count, heads_here, LEVELS)
    states = jnp.einsum("che,chf->hef", key_rows, value_rows, preferred_element_type=jnp.float32)
    position = lax.axis_index("seq")
    seq_bits = lax.axis_size("seq").bit_length() - 1
    local_bits = count.bit_length() - 1
    empty = jnp.zeros((seq_bits, heads_here, HEAD_DIM, HEAD_DIM), jnp.float32)
    portion = lax.all_gather(states[None].astype(jnp.bfloat16), "seq", axis=0, tiled=True).astype(
        jnp.float32
    )
    sources = jnp.arange(portion.shape[0], dtype=jnp.int32)
    flags = []
    for add_height in range(1, seq_bits + 1):
        same_parent = jnp.right_shift(sources, add_height) == jnp.right_shift(position, add_height)
        left_side = jnp.right_shift(sources, add_height - 1) & 1 == 0
        right_self = jnp.right_shift(position, add_height - 1) & 1 == 1
        flags.append((same_parent & left_side & right_self).astype(jnp.float32))
    selector = jnp.stack(flags, axis=1)
    level_sums = empty + jnp.einsum(
        "rm,rhef->mhef", selector, portion, precision=lax.Precision.HIGHEST
    )
    rounded = level_sums.astype(jnp.bfloat16)
    cross = jnp.zeros((count, heads_here, HEAD_DIM), jnp.float32)
    for height in range(seq_bits):
        term = jnp.einsum(
            "che,hef->chf", query_rows, rounded[height], preferred_element_type=jnp.float32
        )
        cross = cross + weight_rows[:, :, local_bits + 1 + height, None] * term
    levels, causal = bit_levels(count)

    def per_head(head_inputs):
        return local_attention(
            head_inputs[0], head_inputs[1], head_inputs[2], head_inputs[3], levels, causal
        )

    inner = lax.map(
        per_head,
        (
            query_rows.transpose(1, 0, 2),
            key_rows.transpose(1, 0, 2),
            value_rows.transpose(1, 0, 2),
            weight_rows.transpose(1, 0, 2),
        ),
    )
    inner = inner.transpose(1, 0, 2)
    attended = (inner + cross).reshape(count, features).astype(jnp.bfloat16)
    token_rows = lax.all_to_all(attended, "head", split_axis=0, concat_axis=1, tiled=True).astype(
        jnp.float32
    )
    mean_square = jnp.mean(token_rows * token_rows, axis=1, keepdims=True)
    gating = jax.nn.silu(gate_values.astype(jnp.float32))
    return (token_rows * lax.rsqrt(mean_square + 1e-06) * norm_gain[None, :] * gating).astype(
        jnp.bfloat16
    )


def solution(mesh):
    placed = (
        P("seq", "head"),
        P("seq", "head"),
        P("seq", "head"),
        P("seq", "head"),
        P(("seq", "head"), None),
        P(),
    )
    return jax.shard_map(
        per_device, mesh=mesh, in_specs=placed, out_specs=P(("seq", "head"), None), check_vma=False
    )
```

profile of v0, /device:TPU:1, one launch (start us, length us, event | category | flops | bytes accessed | tf_op | source)
XLA Modules:
  0.0 219.9 jit_solution(5368130220149001610)
XLA Ops:
  6.5 0.0 all-gather.3.cloned.1.call-start
  6.5 6.4 %copy.50 = bf16[1024,2048]{0,1:T(8,128)(2,1)} copy(bf16[1024,2048]{1,0:T(8,128)(2,1)} %param.9) | data formatting | bytes 8388608 | tf_op args[1]
  12.9 6.4 %copy.52 = bf16[1024,2048]{0,1:T(8,128)(2,1)} copy(bf16[1024,2048]{1,0:T(8,128)(2,1)} %param.10) | data formatting | bytes 8388608 | tf_op args[2]
  19.3 5.5 %convolution_convert_fusion = bf16[16,128,128]{2,1,0:T(8,128)(2,1)} fusion(bf16[1024,16,128]{0,2,1:T(8,128)(2,1)} %bitcast.136, bf16[1024,16,128]{0,2,1:T(8,128)(2,1)} %bitcast.138), kind=kOutput, calls=%fused_computation.62 | convolution fusion | flops 537133056 | bytes 8912896 | tf_op jit(solution)/shard_map/che,chf->hef/dot_general | solution.py:38
  24.8 0.0 all-gather.3.cloned.1.call-update
  24.9 0.0 copy-start.3
  24.9 6.5 %copy.49 = bf16[1024,2048]{0,1:T(8,128)(2,1)} copy(bf16[1024,2048]{1,0:T(8,128)(2,1)} %param.8) | data formatting | bytes 8388608 | tf_op args[0]
  31.4 0.0 copy-done.3
  31.4 0.3 copy.51
  31.7 61.2 %while.12 = (s32[]{:T(128)}, f32[16,1024,128]{1,2,0:T(8,128)}, bf16[16,1024,128]{1,2,0:T(8,128)(2,1)}, bf16[16,1024,128]{1,2,0:T(8,128)(2,1)}, f32[16,1024,16]{1...) while((s32[]{:T(128)}, f32[16,1024,128]{1,2,0:T(8,128)}, ...), condition=%wide.region_1.2_spmd.clone.clone, body=%wide.region_0.1_spmd.clone.clone.sunk | while | flops 606076928 | bytes 1579097 | solution.py:71
  31.8 3.8 %fusion.90 = f32[16,1024,128]{1,2,0:T(8,128)} fusion(f32[16,1024,128]{1,2,0:T(8,128)} %get-tuple-element.240, s32[]{:T(128)S(6)} %copy.113, f32[1024]{0:T(1024)S(1)} %bitcast.145, f32[1024]{0:T(1024)S(1)} %bitcast.146, f32[1024]{0:T(1024)S(1)} %bitcast.147, f32[1024]{0:T(1024)S(1)} %bitcast.148, f32[1024]{0:T(1024)S(1)} %bitcast.149, ...), kind=kOutput, calls=%fused_computation.18.clone.1 | convolution fusion | flops 606076928 | bytes 1357824 | tf_op jit(solution)/shard_map/while/body/eval_jaxpr/dot_general | solution.py:28
  35.6 3.8 %fusion.90 = f32[16,1024,128]{1,2,0:T(8,128)} fusion(f32[16,1024,128]{1,2,0:T(8,128)} %get-tuple-element.240, s32[]{:T(128)S(6)} %copy.113, f32[1024]{0:T(1024)S(1)} %bitcast.145, f32[1024]{0:T(1024)S(1)} %bitcast.146, f32[1024]{0:T(1024)S(1)} %bitcast.147, f32[1024]{0:T(1024)S(1)} %bitcast.148, f32[1024]{0:T(1024)S(1)} %bitcast.149, ...), kind=kOutput, calls=%fused_computation.18.clone.1 | convolution fusion | flops 606076928 | bytes 1357824 | tf_op jit(solution)/shard_map/while/body/eval_jaxpr/dot_general | solution.py:28
  39.4 3.8 %fusion.90 = f32[16,1024,128]{1,2,0:T(8,128)} fusion(f32[16,1024,128]{1,2,0:T(8,128)} %get-tuple-element.240, s32[]{:T(128)S(6)} %copy.113, f32[1024]{0:T(1024)S(1)} %bitcast.145, f32[1024]{0:T(1024)S(1)} %bitcast.146, f32[1024]{0:T(1024)S(1)} %bitcast.147, f32[1024]{0:T(1024)S(1)} %bitcast.148, f32[1024]{0:T(1024)S(1)} %bitcast.149, ...), kind=kOutput, calls=%fused_computation.18.clone.1 | convolution fusion | flops 606076928 | bytes 1357824 | tf_op jit(solution)/shard_map/while/body/eval_jaxpr/dot_general | solution.py:28
  43.3 3.8 %fusion.90 = f32[16,1024,128]{1,2,0:T(8,128)} fusion(f32[16,1024,128]{1,2,0:T(8,128)} %get-tuple-element.240, s32[]{:T(128)S(6)} %copy.113, f32[1024]{0:T(1024)S(1)} %bitcast.145, f32[1024]{0:T(1024)S(1)} %bitcast.146, f32[1024]{0:T(1024)S(1)} %bitcast.147, f32[1024]{0:T(1024)S(1)} %bitcast.148, f32[1024]{0:T(1024)S(1)} %bitcast.149, ...), kind=kOutput, calls=%fused_computation.18.clone.1 | convolution fusion | flops 606076928 | bytes 1357824 | tf_op jit(solution)/shard_map/while/body/eval_jaxpr/dot_general | solution.py:28
  47.1 3.8 %fusion.90 = f32[16,1024,128]{1,2,0:T(8,128)} fusion(f32[16,1024,128]{1,2,0:T(8,128)} %get-tuple-element.240, s32[]{:T(128)S(6)} %copy.113, f32[1024]{0:T(1024)S(1)} %bitcast.145, f32[1024]{0:T(1024)S(1)} %bitcast.146, f32[1024]{0:T(1024)S(1)} %bitcast.147, f32[1024]{0:T(1024)S(1)} %bitcast.148, f32[1024]{0:T(1024)S(1)} %bitcast.149, ...), kind=kOutput, calls=%fused_computation.18.clone.1 | convolution fusion | flops 606076928 | bytes 1357824 | tf_op jit(solution)/shard_map/while/body/eval_jaxpr/dot_general | solution.py:28
  50.9 3.8 %fusion.90 = f32[16,1024,128]{1,2,0:T(8,128)} fusion(f32[16,1024,128]{1,2,0:T(8,128)} %get-tuple-element.240, s32[]{:T(128)S(6)} %copy.113, f32[1024]{0:T(1024)S(1)} %bitcast.145, f32[1024]{0:T(1024)S(1)} %bitcast.146, f32[1024]{0:T(1024)S(1)} %bitcast.147, f32[1024]{0:T(1024)S(1)} %bitcast.148, f32[1024]{0:T(1024)S(1)} %bitcast.149, ...), kind=kOutput, calls=%fused_computation.18.clone.1 | convolution fusion | flops 606076928 | bytes 1357824 | tf_op jit(solution)/shard_map/while/body/eval_jaxpr/dot_general | solution.py:28
  54.7 3.8 %fusion.90 = f32[16,1024,128]{1,2,0:T(8,128)} fusion(f32[16,1024,128]{1,2,0:T(8,128)} %get-tuple-element.240, s32[]{:T(128)S(6)} %copy.113, f32[1024]{0:T(1024)S(1)} %bitcast.145, f32[1024]{0:T(1024)S(1)} %bitcast.146, f32[1024]{0:T(1024)S(1)} %bitcast.147, f32[1024]{0:T(1024)S(1)} %bitcast.148, f32[1024]{0:T(1024)S(1)} %bitcast.149, ...), kind=kOutput, calls=%fused_computation.18.clone.1 | convolution fusion | flops 606076928 | bytes 1357824 | tf_op jit(solution)/shard_map/while/body/eval_jaxpr/dot_general | solution.py:28
  58.6 3.8 %fusion.90 = f32[16,1024,128]{1,2,0:T(8,128)} fusion(f32[16,1024,128]{1,2,0:T(8,128)} %get-tuple-element.240, s32[]{:T(128)S(6)} %copy.113, f32[1024]{0:T(1024)S(1)} %bitcast.145, f32[1024]{0:T(1024)S(1)} %bitcast.146, f32[1024]{0:T(1024)S(1)} %bitcast.147, f32[1024]{0:T(1024)S(1)} %bitcast.148, f32[1024]{0:T(1024)S(1)} %bitcast.149, ...), kind=kOutput, calls=%fused_computation.18.clone.1 | convolution fusion | flops 606076928 | bytes 1357824 | tf_op jit(solution)/shard_map/while/body/eval_jaxpr/dot_general | solution.py:28
  62.4 3.8 %fusion.90 = f32[16,1024,128]{1,2,0:T(8,128)} fusion(f32[16,1024,128]{1,2,0:T(8,128)} %get-tuple-element.240, s32[]{:T(128)S(6)} %copy.113, f32[1024]{0:T(1024)S(1)} %bitcast.145, f32[1024]{0:T(1024)S(1)} %bitcast.146, f32[1024]{0:T(1024)S(1)} %bitcast.147, f32[1024]{0:T(1024)S(1)} %bitcast.148, f32[1024]{0:T(1024)S(1)} %bitcast.149, ...), kind=kOutput, calls=%fused_computation.18.clone.1 | convolution fusion | flops 606076928 | bytes 1357824 | tf_op jit(solution)/shard_map/while/body/eval_jaxpr/dot_general | solution.py:28
  66.2 3.8 %fusion.90 = f32[16,1024,128]{1,2,0:T(8,128)} fusion(f32[16,1024,128]{1,2,0:T(8,128)} %get-tuple-element.240, s32[]{:T(128)S(6)} %copy.113, f32[1024]{0:T(1024)S(1)} %bitcast.145, f32[1024]{0:T(1024)S(1)} %bitcast.146, f32[1024]{0:T(1024)S(1)} %bitcast.147, f32[1024]{0:T(1024)S(1)} %bitcast.148, f32[1024]{0:T(1024)S(1)} %bitcast.149, ...), kind=kOutput, calls=%fused_computation.18.clone.1 | convolution fusion | flops 606076928 | bytes 1357824 | tf_op jit(solution)/shard_map/while/body/eval_jaxpr/dot_general | solution.py:28
  70.0 3.8 %fusion.90 = f32[16,1024,128]{1,2,0:T(8,128)} fusion(f32[16,1024,128]{1,2,0:T(8,128)} %get-tuple-element.240, s32[]{:T(128)S(6)} %copy.113, f32[1024]{0:T(1024)S(1)} %bitcast.145, f32[1024]{0:T(1024)S(1)} %bitcast.146, f32[1024]{0:T(1024)S(1)} %bitcast.147, f32[1024]{0:T(1024)S(1)} %bitcast.148, f32[1024]{0:T(1024)S(1)} %bitcast.149, ...), kind=kOutput, calls=%fused_computation.18.clone.1 | convolution fusion | flops 606076928 | bytes 1357824 | tf_op jit(solution)/shard_map/while/body/eval_jaxpr/dot_general | solution.py:28
  73.9 3.8 %fusion.90 = f32[16,1024,128]{1,2,0:T(8,128)} fusion(f32[16,1024,128]{1,2,0:T(8,128)} %get-tuple-element.240, s32[]{:T(128)S(6)} %copy.113, f32[1024]{0:T(1024)S(1)} %bitcast.145, f32[1024]{0:T(1024)S(1)} %bitcast.146, f32[1024]{0:T(1024)S(1)} %bitcast.147, f32[1024]{0:T(1024)S(1)} %bitcast.148, f32[1024]{0:T(1024)S(1)} %bitcast.149, ...), kind=kOutput, calls=%fused_computation.18.clone.1 | convolution fusion | flops 606076928 | bytes 1357824 | tf_op jit(solution)/shard_map/while/body/eval_jaxpr/dot_general | solution.py:28
  77.7 3.8 %fusion.90 = f32[16,1024,128]{1,2,0:T(8,128)} fusion(f32[16,1024,128]{1,2,0:T(8,128)} %get-tuple-element.240, s32[]{:T(128)S(6)} %copy.113, f32[1024]{0:T(1024)S(1)} %bitcast.145, f32[1024]{0:T(1024)S(1)} %bitcast.146, f32[1024]{0:T(1024)S(1)} %bitcast.147, f32[1024]{0:T(1024)S(1)} %bitcast.148, f32[1024]{0:T(1024)S(1)} %bitcast.149, ...), kind=kOutput, calls=%fused_computation.18.clone.1 | convolution fusion | flops 606076928 | bytes 1357824 | tf_op jit(solution)/shard_map/while/body/eval_jaxpr/dot_general | solution.py:28
  81.5 3.8 %fusion.90 = f32[16,1024,128]{1,2,0:T(8,128)} fusion(f32[16,1024,128]{1,2,0:T(8,128)} %get-tuple-element.240, s32[]{:T(128)S(6)} %copy.113, f32[1024]{0:T(1024)S(1)} %bitcast.145, f32[1024]{0:T(1024)S(1)} %bitcast.146, f32[1024]{0:T(1024)S(1)} %bitcast.147, f32[1024]{0:T(1024)S(1)} %bitcast.148, f32[1024]{0:T(1024)S(1)} %bitcast.149, ...), kind=kOutput, calls=%fused_computation.18.clone.1 | convolution fusion | flops 606076928 | bytes 1357824 | tf_op jit(solution)/shard_map/while/body/eval_jaxpr/dot_general | solution.py:28
  85.3 3.8 %fusion.90 = f32[16,1024,128]{1,2,0:T(8,128)} fusion(f32[16,1024,128]{1,2,0:T(8,128)} %get-tuple-element.240, s32[]{:T(128)S(6)} %copy.113, f32[1024]{0:T(1024)S(1)} %bitcast.145, f32[1024]{0:T(1024)S(1)} %bitcast.146, f32[1024]{0:T(1024)S(1)} %bitcast.147, f32[1024]{0:T(1024)S(1)} %bitcast.148, f32[1024]{0:T(1024)S(1)} %bitcast.149, ...), kind=kOutput, calls=%fused_computation.18.clone.1 | convolution fusion | flops 606076928 | bytes 1357824 | tf_op jit(solution)/shard_map/while/body/eval_jaxpr/dot_general | solution.py:28
  89.1 3.8 %fusion.90 = f32[16,1024,128]{1,2,0:T(8,128)} fusion(f32[16,1024,128]{1,2,0:T(8,128)} %get-tuple-element.240, s32[]{:T(128)S(6)} %copy.113, f32[1024]{0:T(1024)S(1)} %bitcast.145, f32[1024]{0:T(1024)S(1)} %bitcast.146, f32[1024]{0:T(1024)S(1)} %bitcast.147, f32[1024]{0:T(1024)S(1)} %bitcast.148, f32[1024]{0:T(1024)S(1)} %bitcast.149, ...), kind=kOutput, calls=%fused_computation.18.clone.1 | convolution fusion | flops 606076928 | bytes 1357824 | tf_op jit(solution)/shard_map/while/body/eval_jaxpr/dot_general | solution.py:28
  93.0 0.2 fusion.75
  93.2 6.1 %all-gather.3.cloned.1.call-done = bf16[128,128,128]{2,1,0:T(8,128)(2,1)} async-done(((bf16[16,128,128]{2,1,0:T(8,128)(2,1)}), bf16[128,128,128]{2,1,0:T(8,128)(2,1)}) %all-gather.3.cloned.1.call-update) | async-done | bytes 4194320 | tf_op jit(solution)/shard_map/all_gather | solution.py:43
  99.3 5.0 %fusion.57 = bf16[3,16,128,128]{3,0,2,1:T(4,128)(2,1)S(1)} fusion(bf16[8,16,128,128]{3,2,1,0:T(8,128)(2,1)} %bitcast.140, pred[8,1]{0,1:T(4,128)(4,1)S(1)} %get-tuple-element.169, pred[8,1]{0,1:T(4,128)(4,1)S(1)} %get-tuple-element.170, pred[8,1]{0,1:T(4,128)(4,1)S(1)} %and_and_fusion.2), kind=kOutput, calls=%fused_computation.61 | convolution fusion | flops 13369392 | bytes 5767192 | tf_op jit(solution)/shard_map/rm,rhef->mhef/dot_general | solution.py:54
  104.3 0.0 copy-start
  104.3 2.3 %fusion.74 = (bf16[1,16,128,128]{3,0,2,1:T(2,128)(2,1)S(1)}, bf16[1,16,128,128]{3,0,2,1:T(2,128)(2,1)S(1)}, bf16[1,16,128,128]{3,0,2,1:T(2,128)(2,1)S(1)}) fusion(bf16[3,16,128,128]{3,0,2,1:T(4,128)(2,1)S(1)} %fusion.57), kind=kLoop, calls=%fused_computation.87 | loop fusion | bytes 3145728 | tf_op jit(solution)/shard_map/slice | solution.py:61
  106.6 0.0 copy-done
  106.6 4.5 %fusion.62 = f32[16,128,1024]{2,1,0:T(8,128)} fusion(bf16[1024,16,128]{0,2,1:T(8,128)(2,1)S(1)} %bitcast.132, bf16[1,16,128,128]{3,0,2,1:T(2,128)(2,1)S(1)} %get-tuple-element.164), kind=kOutput, calls=%fused_computation.65 | convolution fusion | flops 536870912 | bytes 13107200 | tf_op jit(solution)/shard_map/che,hef->chf/dot_general | solution.py:60
  111.1 4.5 %fusion.65 = f32[16,128,1024]{2,1,0:T(8,128)} fusion(bf16[1024,16,128]{0,2,1:T(8,128)(2,1)S(1)} %bitcast.133, bf16[1,16,128,128]{3,0,2,1:T(2,128)(2,1)S(1)} %get-tuple-element.165), kind=kOutput, calls=%fused_computation.68 | convolution fusion | flops 536870912 | bytes 13107200 | tf_op jit(solution)/shard_map/che,hef->chf/dot_general | solution.py:60
  115.7 11.8 %fusion.52 = bf16[1024,16,128]{0,2,1:T(8,128)(2,1)} fusion(f32[16,128,1024]{2,1,0:T(8,128)} %fusion.62, f32[16,128,1024]{2,1,0:T(8,128)} %fusion.65, f32[16,1024,128]{1,2,0:T(8,128)} %get-tuple-element.77, f32[1024,16]{0,1:T(8,128)S(1)} %get-tuple-element.171, f32[1024,16]{0,1:T(8,128)S(1)} %get-tuple-element.172, f32[1024,16]{0,1:T(8,128)S(1)} %bitcast.143, ...), kind=kOutput, calls=%fused_computation.53 | convolution fusion | flops 551550976 | bytes 34275328 | tf_op jit(solution)/shard_map/che,hef->chf/dot_general | solution.py:60
  127.5 7.8 %convert_element_type.307 = bf16[4,256,2048]{1,0,2:T(4,128)(2,1)} reshape(bf16[1024,16,128]{0,2,1:T(8,128)(2,1)} %fusion.52) | data formatting | bytes 8388608 | tf_op jit(solution)/shard_map/convert_element_type | solution.py:81
  135.3 2.7 %copy.65 = bf16[4,256,2048]{1,2,0:T(8,128)(2,1)S(1)} copy(bf16[4,256,2048]{1,0,2:T(4,128)(2,1)} %convert_element_type.307) | data formatting | bytes 8388608 | tf_op jit(solution)/shard_map/convert_element_type | solution.py:81
  138.1 51.6 %all_to_all.10 = bf16[4,256,2048]{1,2,0:T(8,128)(2,1)S(1)} all-to-all(bf16[4,256,2048]{1,2,0:T(8,128)(2,1)S(1)} %copy.65), channel_id=1, replica_groups=mesh['seq'=8,'head'=4] {'head'}, dimensions={0} | all-to-all | bytes 8388608 | tf_op jit(solution)/shard_map/all_to_all | solution.py:82
  189.6 0.0 copy-start.1
  189.6 4.3 %convert_element_type.316 = f32[4,256,2048]{1,2,0:T(8,128)} convert(bf16[4,256,2048]{1,2,0:T(8,128)(2,1)S(1)} %all_to_all.10) | non-fusion elementwise | flops 2097152 | bytes 12582912 | tf_op jit(solution)/shard_map/convert_element_type | solution.py:82
  193.9 0.2 copy-done.1
  194.1 0.0 copy-start.4
  194.1 9.0 %copy.66 = f32[256,8192]{1,0:T(8,128)} copy(f32[256,8192]{0,1:T(8,128)} %bitcast.135) | data formatting | bytes 16777216 | tf_op jit(solution)/shard_map/convert_element_type | solution.py:82
  203.1 0.0 copy-start.2
  203.1 3.5 %multiply_reduce_fusion = f32[256]{0:T(256)S(1)} fusion(bf16[4,256,2048]{1,2,0:T(8,128)(2,1)} %copy-done.1), kind=kLoop, calls=%fused_computation.57 | loop fusion | flops 6291200 | bytes 4195328 | tf_op jit(solution)/shard_map/reduce_sum | solution.py:85
  206.6 0.0 copy-done.4
  206.6 0.0 copy-done.2
  206.6 6.5 %fusion.54 = bf16[256,8192]{1,0:T(8,128)(2,1)} fusion(bf16[256,8192]{1,0:T(8,128)(2,1)S(1)} %copy-done.2, f32[256,8192]{1,0:T(8,128)} %copy.66, f32[8192]{0:T(1024)S(1)} %copy-done.4, f32[256]{0:T(256)S(1)} %add_rsqrt_fusion), kind=kLoop, calls=%fused_computation.58 | loop fusion | flops 18874368 | bytes 16811008 | tf_op jit(solution)/shard_map/convert_element_type | solution.py:87
  (38 shorter events, 0.7 us)
Async XLA Ops:
  6.5 92.8 %all-gather.3.cloned.1.call-start = ((), (), s32[]{:S(2)}) async-start(), calls=%async_computation.1 | async-start | bytes 4718592 | tf_op jit(solution)/shard_map/all_gather | solution.py:43
  24.9 6.5 %copy-start.3 = (f32[1024,256]{1,0:T(8,128)S(1)}, f32[1024,256]{1,0:T(8,128)}, u32[]{:S(2)}) copy-start(f32[1024,256]{1,0:T(8,128)} %param.11) | copy-start | bytes 3145732
  104.3 2.3 %copy-start = (bf16[16,1024,128]{1,2,0:T(8,128)(2,1)S(1)}, bf16[16,1024,128]{1,2,0:T(8,128)(2,1)}, u32[]{:S(2)}) copy-start(bf16[16,1024,128]{1,2,0:T(8,128)(2,1)} %get-tuple-element.254) | copy-start | bytes 12582916
  189.6 4.5 %copy-start.1 = (bf16[4,256,2048]{1,2,0:T(8,128)(2,1)}, bf16[4,256,2048]{1,2,0:T(8,128)(2,1)S(1)}, u32[]{:S(2)}) copy-start(bf16[4,256,2048]{1,2,0:T(8,128)(2,1)S(1)} %all_to_all.10) | copy-start | bytes 12582916
  194.1 12.4 %copy-start.4 = (f32[8192]{0:T(1024)S(1)}, f32[8192]{0:T(1024)}, u32[]{:S(2)}) copy-start(f32[8192]{0:T(1024)} %param.13) | copy-start | bytes 98308
  203.1 3.5 %copy-start.2 = (bf16[256,8192]{1,0:T(8,128)(2,1)S(1)}, bf16[256,8192]{1,0:T(8,128)(2,1)}, u32[]{:S(2)}) copy-start(bf16[256,8192]{1,0:T(8,128)(2,1)} %param.12) | copy-start | bytes 12582916
Sparse Core Ops, SparseCore 0:
  25.0 74.2 all-gather.2
where the time goes:
time: 222 us; the launch traced here: 220 us
  matrix products  91.9 us (41%)
  blocking collectives  51.6 us (23%)
  local copies, waits for them, and re-layouts  42.4 us (19%)
  other arithmetic  14.3 us (6%)
  between operations  13.5 us (6%)
  waiting for transfers between devices  6.12 us (3%)
    dot_general x16, matrix products, local_attention(): return jnp.dot(weighted, value_head, preferred_element_type=jnp.float32)  60.6 us
    all_to_all x1, blocking collectives, per_device(): lax.all_to_all(attended, 'head', split_axis=0, concat_axis=1, tiled=True)  51.6 us
    dot_general x3, matrix products, per_device(): jnp.einsum('che,hef->chf', query_rows, rounded[height], preferred_element...  20.9 us
    unnamed x16, local copies, waits for them, and re-layouts  19.9 us
    convert_element_type x2, local copies, waits for them, and re-layouts, per_device(): attended = (inner + cross).reshape(count, features).astype(jnp.bfloat16)  10.6 us
    convert_element_type x1, local copies, waits for them, and re-layouts, per_device(): lax.all_to_all(attended, 'head', split_axis=0, concat_axis=1, tiled=True)  8.95 us
    convert_element_type x1, other arithmetic, per_device(): (token_rows * lax.rsqrt(mean_square + 1e-06) * norm_gain[None, :] * gatin...  6.47 us
    all_gather x1, waiting for transfers between devices, per_device(): lax.all_gather(states[None].astype(jnp.bfloat16), 'seq', axis=0, tiled=True)  6.1 us
  transfers between devices with their start and end apart: 1, of which 1 were waited for; matrix products, arithmetic and copies ran while one was open for 31% of the time, Pallas kernels for 0%

commit v1 on v0

v1 whole, which is shorter than its diff:
```python
import functools

import jax
import jax.numpy as jnp
from jax import lax
from jax.experimental import pallas as pl
from jax.experimental.pallas import tpu as pltpu
from jax.sharding import PartitionSpec as P

HEAD_DIM = 128
LEVELS = 16
CHUNK = 128
LANES = 128
SUB = 8
SUB_BITS = 3
GROUP = 2
PER_TILE = LANES // LEVELS
SIZES = (4, 4)
ORDER = (
    ("S", 0),
    ("S", 1),
    ("A", 0),
    ("S", 2),
    ("A", 0),
    ("A", 1),
    ("I", 0),
    ("F", 0),
    ("A", 1),
    ("A", 2),
    ("I", 1),
    ("F", 1),
    ("A", 2),
    ("I", 2),
    ("I", 2),
    ("F", 2),
    ("N", 0),
    ("N", 1),
    ("N", 2),
)
LONG = pl.CostEstimate(flops=3 * 10**9, bytes_accessed=10**6, transcendentals=0)


def dot(a, b, dims=((1,), (0,))):
    return lax.dot_general(a, b, (dims, ((), ())), preferred_element_type=jnp.float32)


def anywhere():
    return pl.BlockSpec(memory_space=pl.ANY)


def local():
    return pl.BlockSpec(memory_space=pltpu.VMEM)


def params(mebibytes):
    return pltpu.CompilerParams(vmem_limit_bytes=mebibytes * 1024 * 1024)


def hbm():
    return pl.BlockSpec(memory_space=pltpu.HBM)


def in_hbm(array):
    return pltpu.with_memory_space_constraint(array, pltpu.HBM)


def in_vmem(array):
    return pltpu.with_memory_space_constraint(array, pltpu.VMEM)


def fetches(source_ref, held_ref, first, heads, sems):
    copies = []
    for n in range(heads // GROUP):
        source = pl.ds((first + n * GROUP) * HEAD_DIM, GROUP * HEAD_DIM)
        target = pl.ds(n * GROUP * HEAD_DIM, GROUP * HEAD_DIM)
        copies.append(
            pltpu.make_async_copy(source_ref.at[:, source], held_ref.at[:, target], sems.at[n])
        )
    return copies


def state_kernel(first, heads, k_ref, v_ref, *refs):
    state_ref, rounded_ref, k_held, v_held, k_sems, v_sems = refs[-6:]
    k_copies = fetches(k_ref, k_held, first, heads, k_sems)
    v_copies = fetches(v_ref, v_held, first, heads, v_sems)
    for n in range(heads // GROUP):
        k_copies[n].start()
        v_copies[n].start()
    for n in range(heads // GROUP):
        k_copies[n].wait()
        v_copies[n].wait()
        for i in range(n * GROUP, (n + 1) * GROUP):
            here = slice(i * HEAD_DIM, (i + 1) * HEAD_DIM)
            state = dot(k_held[:, here], v_held[:, here], ((0,), (0,)))
            state_ref[i] = state
            rounded_ref[i] = state.astype(jnp.bfloat16)


def block_states(keys, values, first, heads, after):
    count = keys.shape[0]
    shape = (heads, HEAD_DIM, HEAD_DIM)
    held = jax.ShapeDtypeStruct((count, heads * HEAD_DIM), keys.dtype)
    return pl.pallas_call(
        functools.partial(state_kernel, first, heads),
        in_specs=[hbm(), hbm()] + [anywhere() for _ in after],
        out_specs=[local()] * 4,
        out_shape=[
            jax.ShapeDtypeStruct(shape, jnp.float32),
            jax.ShapeDtypeStruct(shape, jnp.bfloat16),
            held,
            held,
        ],
        scratch_shapes=[pltpu.SemaphoreType.DMA((heads // GROUP,))] * 2,
        compiler_params=params(8),
        cost_estimate=LONG,
        name="block_states",
    )(in_hbm(keys), in_hbm(values), *after)


def add_kernel(total_ref, held_ref, *refs):
    sum_ref, rounded_ref = refs[-2:]
    total = total_ref[...] + held_ref[...].astype(jnp.float32)
    sum_ref[...] = total
    rounded_ref[...] = total.astype(jnp.bfloat16)


def add_states(total, held, after):
    return pl.pallas_call(
        add_kernel,
        in_specs=[local()] * 2 + [anywhere() for _ in after],
        out_specs=[local(), local()],
        out_shape=[
            jax.ShapeDtypeStruct(total.shape, jnp.float32),
            jax.ShapeDtypeStruct(total.shape, jnp.bfloat16),
        ],
        compiler_params=params(8),
        cost_estimate=LONG,
        name="add_states",
    )(in_vmem(total), held, *after)


def factor_rows(weights, near_mix, far_mix):
    chunk = weights.shape[1]
    bits = chunk.bit_length() - 1
    row = [jnp.broadcast_to(weights[l : l + 1], (SUB, chunk)) for l in range(bits + 1)]
    near = row[0]
    for level in range(1, SUB_BITS + 1):
        near = jnp.where(near_mix >= 1 << (level - 1), row[level], near)
    near = jnp.where(near_mix >= SUB, jnp.float32(0.0), near)
    far = []
    for mix in far_mix:
        value = jnp.zeros((SUB, chunk), jnp.float32)
        for level in range(SUB_BITS + 1, bits + 1):
            value = jnp.where(mix >= 1 << (level - SUB_BITS - 1), row[level], value)
        far.append(value)
    return near, far


def inner_kernel(first, start, heads, q_source, k_ref, v_ref, w_ref, *refs):
    out_ref, q_ref, wt_ref, sems = refs[-4:]
    copies = fetches(q_source, q_ref, first, heads, sems)
    for copy in copies:
        copy.start()
    count = q_ref.shape[0]
    chunk = min(CHUNK, count)
    chunks = count // chunk
    chunk_bits = chunk.bit_length() - 1
    groups = chunk // SUB
    low_tile = first // PER_TILE
    tiles = (first + heads - 1) // PER_TILE + 1 - low_tile

    for tile in range(tiles):
        lanes = slice((low_tile + tile) * LANES, (low_tile + tile + 1) * LANES)
        for c in range(chunks):
            here = slice(c * chunk, (c + 1) * chunk)
            wt_ref[tile * LANES : (tile + 1) * LANES, here] = w_ref[here, lanes].T

    t = lax.broadcasted_iota(jnp.int32, (SUB, chunk), 1)
    s = lax.broadcasted_iota(jnp.int32, (SUB, chunk), 0)
    t_low, t_high = t & (SUB - 1), t >> SUB_BITS
    near_mix = jnp.where(s <= t_low, s ^ t_low, SUB)
    far_mix = []
    for a in range(max(1, groups // SUB)):
        s_high = s + SUB * a
        far_mix.append(jnp.where(t_high > s_high, t_high ^ s_high, 0))

    def group(step, carry):
        wide = GROUP * HEAD_DIM
        source = pl.ds(pl.multiple_of((first + step * GROUP) * HEAD_DIM, HEAD_DIM), wide)
        target = pl.ds(pl.multiple_of(step * wide, wide), wide)
        pltpu.make_async_copy(
            q_source.at[:, source], q_ref.at[:, target], sems.at[step]
        ).wait()
        head = first + step * GROUP
        lane = pl.multiple_of(head // PER_TILE * LANES, LANES)
        base = head % PER_TILE * LEVELS
        weights = pltpu.roll(w_ref[:, pl.ds(lane, LANES)], (LANES - base) % LANES, 1)
        rows_base = lane - low_tile * LANES + base
        sums = {}

        def columns(i, offset=0):
            place = (offset + step * GROUP + i) * HEAD_DIM
            return pl.ds(pl.multiple_of(place, HEAD_DIM), HEAD_DIM)

        def scores_of(i, c):
            here = slice(c * chunk, (c + 1) * chunk)
            held = columns(i, start)
            q, k, v = q_ref[here, columns(i)], k_ref[here, held], v_ref[here, held]
            scores = dot(k, q, ((1,), (1,)))
            terms = []
            for bit in range(chunks.bit_length() - 1):
                if c >> bit & 1:
                    terms.append((bit, dot(q, sums[i, bit].astype(jnp.bfloat16))))
            if c + 1 < chunks:
                state = dot(k, v, ((0,), (0,)))
                for bit in range(chunks.bit_length() - 1):
                    if not c >> bit & 1:
                        fresh = c % (1 << bit) == 0
                        sums[i, bit] = state if fresh else sums[i, bit] + state
            return scores, terms

        def store(i, c, scores, terms):
            here = slice(c * chunk, (c + 1) * chunk)
            own_rows = pl.ds(pl.multiple_of(rows_base + i * LEVELS, LEVELS), LEVELS)
            near, far = factor_rows(wt_ref[own_rows, here], near_mix, far_mix)
            parts = []
            for r in range(groups):
                line = jnp.broadcast_to(far[r // SUB][r % SUB : r % SUB + 1], (SUB, chunk))
                factor = jnp.where(t_high == r, near, line)
                parts.append(scores[r * SUB : (r + 1) * SUB] * factor)
            weighted = jnp.concatenate(parts, axis=0).astype(jnp.bfloat16)
            total = dot(weighted, v_ref[here, columns(i, start)], ((0,), (0,)))
            for bit, term in terms:
                level = i * LEVELS + chunk_bits + 1 + bit
                total += weights[here, level : level + 1] * term
            out_ref[here, columns(i)] = total

        waiting = []
        for i in range(GROUP):
            for c in range(chunks):
                waiting.append((i, c) + scores_of(i, c))
                if len(waiting) > 2:
                    store(*waiting.pop(0))
        for unit in waiting:
            store(*unit)
        return carry

    lax.fori_loop(0, heads // GROUP, group, 0)


def inner_part(queries, keys, values, weights, chunk_first, start, heads, after):
    count = queries.shape[0]
    first = chunk_first + start
    tiles = (first + heads - 1) // PER_TILE + 1 - first // PER_TILE
    shape = (count, heads * HEAD_DIM)
    return pl.pallas_call(
        functools.partial(inner_kernel, first, start, heads),
        in_specs=[hbm()] + [local()] * 3 + [anywhere() for _ in after],
        out_specs=[local()] * 2,
        out_shape=[
            jax.ShapeDtypeStruct(shape, jnp.float32),
            jax.ShapeDtypeStruct(shape, queries.dtype),
        ],
        scratch_shapes=[
            pltpu.VMEM((tiles * LANES, count), jnp.float32),
            pltpu.SemaphoreType.DMA((heads // GROUP,)),
        ],
        compiler_params=params(8),
        cost_estimate=LONG,
        name="inner_part",
    )(in_hbm(queries), in_vmem(keys), in_vmem(values), weights, *after)


def finish_kernel(first, start, heads, pairs, levels, place_ref, q_ref, w_ref, inner_ref, *refs):
    tiers = refs[:levels]
    outs = refs[len(refs) - 2 * len(pairs) :]
    count = q_ref.shape[0]
    rows = outs[0].shape[0]
    local_bits = count.bit_length() - 1
    flip = (place_ref[0] & 1) == 1

    def group(step, carry):
        head = first + step * GROUP
        lane = pl.multiple_of(head // PER_TILE * LANES, LANES)
        base = head % PER_TILE * LEVELS
        for n, pair in enumerate(pairs):
            spot = jnp.bitwise_xor(jnp.right_shift(place_ref[0], 1), pair)
            here = pl.ds(pl.multiple_of(spot * (2 * rows), 2 * rows), 2 * rows)
            weights = pltpu.roll(w_ref[here, pl.ds(lane, LANES)], (LANES - base) % LANES, 1)
            for i in range(GROUP):
                cols = pl.ds(pl.multiple_of((step * GROUP + i) * HEAD_DIM, HEAD_DIM), HEAD_DIM)
                q = q_ref[here, cols]
                total = inner_ref[here, cols]
                for m in range(levels):
                    level = i * LEVELS + local_bits + 1 + m
                    held = place_ref[1 + m].astype(jnp.float32)
                    tier = tiers[m][start + step * GROUP + i]
                    total += (weights[:, level : level + 1] * held) * dot(q, tier)
                upper, lower = total[:rows], total[rows:]
                outs[2 * n][:, cols] = jnp.where(flip, lower, upper).astype(jnp.bfloat16)
                outs[2 * n + 1][:, cols] = jnp.where(flip, upper, lower).astype(jnp.bfloat16)
        return carry

    lax.fori_loop(0, heads // GROUP, group, 0)


def finish(place, tiers, queries, inner, weights, chunk_first, start, heads, pairs, parts, after):
    rows = queries.shape[0] // parts
    outs = 2 * len(pairs)
    return pl.pallas_call(
        functools.partial(
            finish_kernel, chunk_first + start, start, heads, tuple(pairs), len(tiers)
        ),
        in_specs=[pl.BlockSpec(memory_space=pltpu.SMEM)]
        + [local()] * (3 + len(tiers))
        + [anywhere() for _ in after],
        out_specs=[local()] * outs,
        out_shape=[
            jax.ShapeDtypeStruct((rows, heads * HEAD_DIM), jnp.bfloat16) for _ in range(outs)
        ],
        compiler_params=params(8),
        cost_estimate=LONG,
        name="finish",
    )(place, queries, weights, inner, *tiers, *after)


def norm_kernel(layout, width, place_ref, gain_ref, gate_ref, *refs):
    out_ref = refs[-1]
    pieces = refs[:-1]
    tile = out_ref.shape[0]
    rows = pl.ds(pl.multiple_of(pl.program_id(0) * tile, tile), tile)
    square = None
    for ref in pieces:
        x = ref[rows, :].astype(jnp.float32)
        part = jnp.sum(x * x, axis=1, keepdims=True)
        square = part if square is None else square + part
    scale = lax.rsqrt(square / out_ref.shape[1] + 1e-06)
    for (step, start), ref in zip(layout, pieces):
        offset = pl.multiple_of(jnp.bitwise_xor(place_ref[0], step) * width + start, LANES)
        here = pl.ds(offset, ref.shape[1])
        half = gate_ref[rows, here].astype(jnp.float32) * 0.5
        gating = half + half * jnp.tanh(half)
        x = ref[rows, :].astype(jnp.float32) * scale
        out_ref[:, here] = (x * gain_ref[:, here] * gating).astype(jnp.bfloat16)


def normalize(place, gain, gate, layout, pieces, width):
    rows, features = gate.shape
    tile = min(64, rows)
    return pl.pallas_call(
        functools.partial(norm_kernel, layout, width),
        grid=(rows // tile,),
        in_specs=[pl.BlockSpec(memory_space=pltpu.SMEM)] + [local()] * (2 + len(pieces)),
        out_specs=pl.BlockSpec((tile, features), lambda i: (i, 0)),
        out_shape=jax.ShapeDtypeStruct((rows, features), jnp.bfloat16),
        compiler_params=params(8),
        cost_estimate=LONG,
        name="normalize",
    )(place, gain.reshape(1, features), gate, *pieces)


def cut(heads):
    sizes = []
    for size in SIZES:
        if heads - sum(sizes) > size:
            sizes.append(size)
    return sizes + [heads - sum(sizes)]


def per_device(queries, key_vectors, value_vectors, level_weight, gate_values, norm_gain):
    count, width = queries.shape
    heads = width // HEAD_DIM
    blocks = lax.axis_size("seq")
    parts = lax.axis_size("head")
    seq_bits = blocks.bit_length() - 1
    block = lax.axis_index("seq")
    flags = [jnp.right_shift(block, m) & 1 for m in range(seq_bits)]
    place = jnp.stack([lax.axis_index("head")] + flags).astype(jnp.int32)

    sizes = cut(heads)
    chunks = range(len(sizes))
    firsts = [sum(sizes[:g]) for g in chunks]

    inner_sizes = []
    for size in sizes:
        inner_sizes.append([min(4, size - start) for start in range(0, size, 4)])

    totals, sends, tiers, inner, keys, values = {}, {}, {}, {}, {}, {}
    pieces, layout = [], []
    last = {}

    def hop(g):
        m = len(tiers[g])
        pairs = [(i, i ^ 1 << m) for i in range(blocks)]
        tiers[g].append(lax.ppermute(sends[g], "seq", pairs))

    def state_step(g):
        totals[g], sends[g], keys[g], values[g] = block_states(
            key_vectors, value_vectors, firsts[g], sizes[g], tuple(last.values())
        )
        tiers[g] = []
        last["kernel"] = sends[g]
        hop(g)

    def add_step(g):
        if len(tiers[g]) < seq_bits:
            totals[g], sends[g] = add_states(totals[g], tiers[g][-1], tuple(last.values()))
            last["kernel"] = sends[g]
            hop(g)

    def inner_step(g):
        done = inner.setdefault(g, [])
        if len(done) < len(inner_sizes[g]):
            start = sum(inner_sizes[g][: len(done)])
            done.append(
                inner_part(
                    queries,
                    keys[g],
                    values[g],
                    level_weight,
                    firsts[g],
                    start,
                    inner_sizes[g][len(done)],
                    tuple(last.values()),
                )
            )
            last["kernel"] = done[-1][0]

    def finish_step(g, pairs):
        start = 0
        for (part, q_part), size in zip(inner[g], inner_sizes[g]):
            outs = finish(
                place,
                tiers[g],
                q_part,
                part,
                level_weight,
                firsts[g],
                start,
                size,
                pairs,
                parts,
                tuple(last.values()),
            )
            last["kernel"] = outs[-1]
            for offset, out in enumerate(outs):
                step = 2 * pairs[0] + offset
                if step:
                    out = lax.ppermute(out, "head", [(i, i ^ step) for i in range(parts)])
                pieces.append(out)
                layout.append((step, (firsts[g] + start) * HEAD_DIM))
            start += size

    far, near = range(1, parts // 2), range(1)
    for kind, g in ORDER:
        if g >= len(sizes):
            continue
        if kind == "S":
            state_step(g)
        if kind == "A":
            add_step(g)
        if kind == "I":
            inner_step(g)
        if kind == "F":
            for _ in range(seq_bits):
                add_step(g)
            finish_step(g, far)
        if kind == "N":
            finish_step(g, near)
    return normalize(place, norm_gain, gate_values, layout, pieces, width)


def solution(mesh):
    placed = (
        P("seq", "head"),
        P("seq", "head"),
        P("seq", "head"),
        P("seq", "head"),
        P(("seq", "head"), None),
        P(),
    )
    return jax.shard_map(
        per_device, mesh=mesh, in_specs=placed, out_specs=P(("seq", "head"), None), check_vma=False
    )
```

time: 222 us -> 93.6 us (0.42)
  matrix products: 91.9 us -> 0 us
  blocking collectives: 51.6 us -> 0 us
  Pallas kernels: 0 us -> 50.4 us
  local copies, waits for them, and re-layouts: 42.4 us -> 2.55 us
  starting transfers between devices: 0.01 us -> 21.3 us
  other arithmetic: 14.3 us -> 0.08 us
  between operations: 13.5 us -> 0.23 us
  waiting for transfers between devices: 6.12 us -> 18.6 us
    dot_general x21 -> x0, matrix products: 91.9 us -> none  [the longest x16 60.6 us: local_attention(): return jnp.dot(weighted, value_head, preferred_element_type=jnp.float32)]
    all_to_all x1 -> x0, blocking collectives: 51.6 us -> none  [per_device(): lax.all_to_all(attended, 'head', split_axis=0, concat_axis=1, tiled=True)]
    pallas_call x0 -> x22, Pallas kernels: none -> 50.4 us  [the longest x4 19.9 us: inner_part(): pl.pallas_call(functools.partial(inner_kernel, first, start, heads), in_s...]
    ppermute x0 -> x21, starting transfers between devices: none -> 21.3 us  [the longest x12 13.3 us: finish_step(): out = lax.ppermute(out, 'head', [(i, i ^ step) for i in range(parts)])]
    convert_element_type x3 -> x0, local copies, waits for them, and re-layouts: 19.5 us -> none  [the longest x2 10.6 us: per_device(): attended = (inner + cross).reshape(count, features).astype(jnp.bfloat16)]
    ppermute x0 -> x21, waiting for transfers between devices: none -> 18.6 us  [the longest x12 11.6 us: finish_step(): out = lax.ppermute(out, 'head', [(i, i ^ step) for i in range(parts)])]
    unnamed x16 -> x14, local copies, waits for them, and re-layouts: 19.9 us -> 2.55 us
    convert_element_type x2 -> x0, other arithmetic: 10.8 us -> none  [the longest x1 6.47 us: per_device(): (token_rows * lax.rsqrt(mean_square + 1e-06) * norm_gain[None, :] * gatin...]
  transfers between devices with their start and end apart: 1 -> 21, of which waited for: 1 -> 6; matrix products, arithmetic and copies ran while one was open for 31% -> 0% of each run, Pallas kernels for 0% -> 45%
where the time goes in v1:
time: 93.6 us; the launch traced here: 93.2 us
  Pallas kernels  50.4 us (54%)
  starting transfers between devices  21.3 us (23%)
  waiting for transfers between devices  18.6 us (20%)
  local copies, waits for them, and re-layouts  2.55 us (3%)
    pallas_call x4, Pallas kernels, inner_part(): pl.pallas_call(functools.partial(inner_kernel, first, start, heads), in_s...  19.9 us
    pallas_call x8, Pallas kernels, finish(): pl.pallas_call(functools.partial(finish_kernel, chunk_first + start, star...  14.6 us
    ppermute x12, starting transfers between devices, finish_step(): out = lax.ppermute(out, 'head', [(i, i ^ step) for i in range(parts)])  13.3 us
    ppermute x12, waiting for transfers between devices, finish_step(): out = lax.ppermute(out, 'head', [(i, i ^ step) for i in range(parts)])  11.6 us
    ppermute x9, starting transfers between devices, hop(): tiers[g].append(lax.ppermute(sends[g], 'seq', pairs))  7.99 us
    ppermute x9, waiting for transfers between devices, hop(): tiers[g].append(lax.ppermute(sends[g], 'seq', pairs))  7.06 us
    pallas_call x3, Pallas kernels, block_states(): pl.pallas_call(functools.partial(state_kernel, first, heads), in_specs=[h...  6.76 us
    pallas_call x1, Pallas kernels, normalize(): pl.pallas_call(functools.partial(norm_kernel, layout, width), grid=(rows...  6.61 us
  transfers between devices with their start and end apart: 21, of which 6 were waited for; matrix products, arithmetic and copies ran while one was open for 0% of the time, Pallas kernels for 45%

profile of v1, /device:TPU:1, one launch (start us, length us, event | category | flops | bytes accessed | tf_op | source)
XLA Modules:
  0.0 93.2 jit_solution(3862162331119262534)
XLA Ops:
  0.0 1.9 %block_states.3 = (f32[4,128,128]{2,1,0:T(8,128)S(1)}, bf16[4,128,128]{2,1,0:T(8,128)(2,1)S(1)}, bf16[1024,512]{1,0:T(8,128)(2,1)S(1)}, bf16[1024,512]{1,0:T(8,128)(2,1)S(1)}) custom-call(bf16[1024,2048]{1,0:T(8,128)(2,1)} %k_ref.5, bf16[1024,2048]{1,0:T(8,128)(2,1)} %v_ref.5), custom_call_target="tpu_custom_call" | custom-call | flops 3000000000 | bytes 1000000 | tf_op jit(solution)/shard_map/block_states/pallas_call | solution.py:103
  1.9 1.0 %copy-done.3 = bf16[1024,512]{1,0:T(8,128)(2,1)} copy-done((bf16[1024,512]{1,0:T(8,128)(2,1)}, bf16[1024,512]{1,0:T(8,128)(2,1)S(1)}, u32[]{:S(2)}) %copy-start.3) | copy-done | bytes 1048600
  2.9 2.0 %collective-permute-start.1 = (bf16[4,128,128]{2,1,0:T(8,128)(2,1)S(1)}, bf16[4,128,128]{2,1,0:T(8,128)(2,1)S(1)}, u32[]{:S(2)}, u32[]{:S(2)}) collective-permute-start(bf16[4,128,128]{2,1,0:T(8,128)(2,1)S(1)} %get-tuple-element.52.refs_0_), channel_id=1, source_target_pairs={{0,4},{4,0},{8,12},{12,8},{16,20},{20,16},{24,28},{28,24},{1,5},{5... | collective-permute-start | bytes 393224 | tf_op jit(solution)/shard_map/ppermute | solution.py:395
  5.0 1.9 %block_states.4 = (f32[4,128,128]{2,1,0:T(8,128)S(1)}, bf16[4,128,128]{2,1,0:T(8,128)(2,1)S(1)}, bf16[1024,512]{1,0:T(8,128)(2,1)S(1)}, bf16[1024,512]{1,0:T(8,128)(2,1)S(1)}) custom-call(bf16[1024,2048]{1,0:T(8,128)(2,1)} %k_ref.5, bf16[1024,2048]{1,0:T(8,128)(2,1)} %v_ref.5, bf16[4,128,128]{2,1,0:T(8,128)(2,1)S(1)} %get-tuple-element.52.refs_0_), custom_call_target="tpu_custom_call" | custom-call | flops 3000000000 | bytes 1000000 | tf_op jit(solution)/shard_map/block_states/pallas_call | solution.py:103
  6.9 0.4 collective-permute-start
  7.3 0.1 pad_add_fusion.place_ref
  7.4 0.8 collective-permute-done.1.held_ref.refs_0_
  8.2 1.3 %collective-permute-start.2 = (bf16[4,128,128]{2,1,0:T(8,128)(2,1)S(1)}, bf16[4,128,128]{2,1,0:T(8,128)(2,1)S(1)}, u32[]{:S(2)}, u32[]{:S(2)}) collective-permute-start(bf16[4,128,128]{2,1,0:T(8,128)(2,1)S(1)} %get-tuple-element.57.refs_0_), channel_id=1, source_target_pairs={{0,8},{4,12},{8,0},{12,4},{16,24},{20,28},{24,16},{28,20},{1,9},{5... | collective-permute-start | bytes 393224 | tf_op jit(solution)/shard_map/ppermute | solution.py:395
  9.5 2.9 %block_states.5 = (f32[8,128,128]{2,1,0:T(8,128)S(1)}, bf16[8,128,128]{2,1,0:T(8,128)(2,1)S(1)}, bf16[1024,1024]{1,0:T(8,128)(2,1)S(1)}, bf16[1024,1024]{1,0:T(8,128)(2,1)S(1)}) custom-call(bf16[1024,2048]{1,0:T(8,128)(2,1)} %k_ref.5, bf16[1024,2048]{1,0:T(8,128)(2,1)} %v_ref.5, bf16[4,128,128]{2,1,0:T(8,128)(2,1)S(1)} %get-tuple-element.57.refs_0_), custom_call_target="tpu_custom_call" | custom-call | flops 3000000000 | bytes 1000000 | tf_op jit(solution)/shard_map/block_states/pallas_call | solution.py:103
  12.4 1.3 %collective-permute-start.6 = (bf16[8,128,128]{2,1,0:T(8,128)(2,1)S(1)}, bf16[8,128,128]{2,1,0:T(8,128)(2,1)S(1)}, u32[]{:S(2)}, u32[]{:S(2)}) collective-permute-start(bf16[8,128,128]{2,1,0:T(8,128)(2,1)S(1)} %get-tuple-element.58.refs_0_), channel_id=1, source_target_pairs={{0,4},{4,0},{8,12},{12,8},{16,20},{20,16},{24,28},{28,24},{1,5},{5... | collective-permute-start | bytes 786440 | tf_op jit(solution)/shard_map/ppermute | solution.py:395
  13.7 0.7 add_states.7
  14.4 2.3 %collective-permute-start.3 = (bf16[4,128,128]{2,1,0:T(8,128)(2,1)S(1)}, bf16[4,128,128]{2,1,0:T(8,128)(2,1)S(1)}, u32[]{:S(2)}, u32[]{:S(2)}) collective-permute-start(bf16[4,128,128]{2,1,0:T(8,128)(2,1)S(1)} %get-tuple-element.59.refs_0_), channel_id=1, source_target_pairs={{0,16},{4,20},{8,24},{12,28},{16,0},{20,4},{24,8},{28,12},{1,17},{... | collective-permute-start | bytes 393224 | tf_op jit(solution)/shard_map/ppermute | solution.py:395
  16.8 0.2 collective-permute-start.7
  17.0 0.9 %copy-done.1 = f32[1024,256]{1,0:T(8,128)S(1)} copy-done((f32[1024,256]{1,0:T(8,128)S(1)}, f32[1024,256]{1,0:T(8,128)}, u32[]{:S(2)}) %copy-start.1) | copy-done | bytes 1048600
  18.0 0.3 copy-done.4
  18.3 0.3 copy-done.6
  18.6 5.0 %inner_part.4 = (f32[1024,512]{1,0:T(8,128)S(1)}, bf16[1024,512]{1,0:T(8,128)(2,1)S(1)}) custom-call(bf16[1024,2048]{1,0:T(8,128)(2,1)} %q_source.7, bf16[1024,512]{1,0:T(8,128)(2,1)S(1)} %copy-done.4, bf16[1024,512]{1,0:T(8,128)(2,1)S(1)} %copy-done.6, f32[1024,256]{1,0:T(8,128)S(1)} %copy-done.1, bf16[4,128,128]{2,1,0:T(8,128)(2,1)S(1)} %get-tuple-element.60.refs_0_), custom_call_target="tpu_custom_call" | custom-call | flops 3000000000 | bytes 1000000 | tf_op jit(solution)/shard_map/inner_part/pallas_call | solution.py:256
  23.6 1.8 %finish.8 = (bf16[256,512]{1,0:T(8,128)(2,1)S(1)}, bf16[256,512]{1,0:T(8,128)(2,1)S(1)}) custom-call(s32[4]{0:T(128)S(1)} %pad_add_fusion.place_ref, bf16[1024,512]{1,0:T(8,128)(2,1)S(1)} %get-tuple-element.61.q_ref, f32[1024,256]{1,0:T(8,128)S(1)} %copy-done.1, f32[1024,512]{1,0:T(8,128)S(1)} %get-tuple-element.62.inner_ref.refs_3_, ...), custom_call_target="tpu_custom_call" | custom-call | flops 3000000000 | bytes 1000000 | tf_op jit(solution)/shard_map/finish/pallas_call | solution.py:310
  25.4 1.3 %collective-permute-start.4 = (bf16[256,512]{1,0:T(8,128)(2,1)S(1)}, bf16[256,512]{1,0:T(8,128)(2,1)S(1)}, u32[]{:S(2)}, u32[]{:S(2)}) collective-permute-start(bf16[256,512]{1,0:T(8,128)(2,1)S(1)} %get-tuple-element.63), channel_id=1, source_target_pairs={{0,2},{1,3},{2,0},{3,1},{4,6},{5,7},{6,4},{7,5},{8,10},{9,11},{10,... | collective-permute-start | bytes 786440 | tf_op jit(solution)/shard_map/ppermute | solution.py:449
  26.7 3.2 %collective-permute-start.5 = (bf16[256,512]{1,0:T(8,128)(2,1)S(1)}, bf16[256,512]{1,0:T(8,128)(2,1)S(1)}, u32[]{:S(2)}, u32[]{:S(2)}) collective-permute-start(bf16[256,512]{1,0:T(8,128)(2,1)S(1)} %get-tuple-element.64.refs_0_), channel_id=1, source_target_pairs={{0,3},{1,2},{2,1},{3,0},{4,7},{5,6},{6,5},{7,4},{8,11},{9,10},{10,... | collective-permute-start | bytes 786440 | tf_op jit(solution)/shard_map/ppermute | solution.py:449
  29.9 0.7 add_states.9
  30.7 0.1 add_states.10
  30.8 0.3 collective-permute-start.11
  31.1 5.0 %inner_part.5 = (f32[1024,512]{1,0:T(8,128)S(1)}, bf16[1024,512]{1,0:T(8,128)(2,1)S(1)}) custom-call(bf16[1024,2048]{1,0:T(8,128)(2,1)} %q_source.7, bf16[1024,512]{1,0:T(8,128)(2,1)S(1)} %get-tuple-element.65.k_ref, bf16[1024,512]{1,0:T(8,128)(2,1)S(1)} %get-tuple-element.66.v_ref, f32[1024,256]{1,0:T(8,128)S(1)} %copy-done.1, ...), custom_call_target="tpu_custom_call" | custom-call | flops 3000000000 | bytes 1000000 | tf_op jit(solution)/shard_map/inner_part/pallas_call | solution.py:256
  36.1 3.7 %collective-permute-done.8.refs_2_ = bf16[4,128,128]{2,1,0:T(8,128)(2,1)S(1)} collective-permute-done((bf16[4,128,128]{2,1,0:T(8,128)(2,1)S(1)}, bf16[4,128,128]{2,1,0:T(8,128)(2,1)S(1)}, u32[]{:S(2)}, u32[]{:S(2)}) %collective-permute-start.8) | collective-permute-done | bytes 131104 | tf_op jit(solution)/shard_map/ppermute | solution.py:395
  39.7 1.8 %finish.9 = (bf16[256,512]{1,0:T(8,128)(2,1)S(1)}, bf16[256,512]{1,0:T(8,128)(2,1)S(1)}) custom-call(s32[4]{0:T(128)S(1)} %pad_add_fusion.place_ref, bf16[1024,512]{1,0:T(8,128)(2,1)S(1)} %get-tuple-element.71.q_ref, f32[1024,256]{1,0:T(8,128)S(1)} %copy-done.1, f32[1024,512]{1,0:T(8,128)S(1)} %get-tuple-element.72.inner_ref.refs_3_, ...), custom_call_target="tpu_custom_call" | custom-call | flops 3000000000 | bytes 1000000 | tf_op jit(solution)/shard_map/finish/pallas_call | solution.py:310
  41.5 0.6 collective-permute-start.9
  42.1 1.6 %collective-permute-start.10 = (bf16[256,512]{1,0:T(8,128)(2,1)S(1)}, bf16[256,512]{1,0:T(8,128)(2,1)S(1)}, u32[]{:S(2)}, u32[]{:S(2)}) collective-permute-start(bf16[256,512]{1,0:T(8,128)(2,1)S(1)} %get-tuple-element.74.refs_0_), channel_id=1, source_target_pairs={{0,3},{1,2},{2,1},{3,0},{4,7},{5,6},{6,5},{7,4},{8,11},{9,10},{10,... | collective-permute-start | bytes 786440 | tf_op jit(solution)/shard_map/ppermute | solution.py:449
  43.7 0.9 add_states.11
  44.6 5.0 %inner_part.6 = (f32[1024,512]{1,0:T(8,128)S(1)}, bf16[1024,512]{1,0:T(8,128)(2,1)S(1)}) custom-call(bf16[1024,2048]{1,0:T(8,128)(2,1)} %q_source.7, bf16[1024,1024]{1,0:T(8,128)(2,1)S(1)} %get-tuple-element.75.k_ref, bf16[1024,1024]{1,0:T(8,128)(2,1)S(1)} %get-tuple-element.76.v_ref, f32[1024,256]{1,0:T(8,128)S(1)} %copy-done.1, ...), custom_call_target="tpu_custom_call" | custom-call | flops 3000000000 | bytes 1000000 | tf_op jit(solution)/shard_map/inner_part/pallas_call | solution.py:256
  49.6 5.0 %inner_part.7 = (f32[1024,512]{1,0:T(8,128)S(1)}, bf16[1024,512]{1,0:T(8,128)(2,1)S(1)}) custom-call(bf16[1024,2048]{1,0:T(8,128)(2,1)} %q_source.7, bf16[1024,1024]{1,0:T(8,128)(2,1)S(1)} %get-tuple-element.75.k_ref, bf16[1024,1024]{1,0:T(8,128)(2,1)S(1)} %get-tuple-element.76.v_ref, f32[1024,256]{1,0:T(8,128)S(1)} %copy-done.1, ...), custom_call_target="tpu_custom_call" | custom-call | flops 3000000000 | bytes 1000000 | tf_op jit(solution)/shard_map/inner_part/pallas_call | solution.py:256
  54.6 2.6 %collective-permute-done.12.refs_2_ = bf16[8,128,128]{2,1,0:T(8,128)(2,1)S(1)} collective-permute-done((bf16[8,128,128]{2,1,0:T(8,128)(2,1)S(1)}, bf16[8,128,128]{2,1,0:T(8,128)(2,1)S(1)}, u32[]{:S(2)}, u32[]{:S(2)}) %collective-permute-start.12) | collective-permute-done | bytes 262176 | tf_op jit(solution)/shard_map/ppermute | solution.py:395
  57.2 1.8 %finish.10 = (bf16[256,512]{1,0:T(8,128)(2,1)S(1)}, bf16[256,512]{1,0:T(8,128)(2,1)S(1)}) custom-call(s32[4]{0:T(128)S(1)} %pad_add_fusion.place_ref, bf16[1024,512]{1,0:T(8,128)(2,1)S(1)} %get-tuple-element.79.q_ref, f32[1024,256]{1,0:T(8,128)S(1)} %copy-done.1, f32[1024,512]{1,0:T(8,128)S(1)} %get-tuple-element.80.refs_0_.inner_ref, ...), custom_call_target="tpu_custom_call" | custom-call | flops 3000000000 | bytes 1000000 | tf_op jit(solution)/shard_map/finish/pallas_call | solution.py:310
  59.0 0.7 collective-permute-start.14
  59.7 1.8 %finish.11 = (bf16[256,512]{1,0:T(8,128)(2,1)S(1)}, bf16[256,512]{1,0:T(8,128)(2,1)S(1)}) custom-call(s32[4]{0:T(128)S(1)} %pad_add_fusion.place_ref, bf16[1024,512]{1,0:T(8,128)(2,1)S(1)} %get-tuple-element.84.q_ref, f32[1024,256]{1,0:T(8,128)S(1)} %copy-done.1, f32[1024,512]{1,0:T(8,128)S(1)} %get-tuple-element.81.refs_3_.inner_ref, ...), custom_call_target="tpu_custom_call" | custom-call | flops 3000000000 | bytes 1000000 | tf_op jit(solution)/shard_map/finish/pallas_call | solution.py:310
  61.5 1.8 %finish.12 = (bf16[256,512]{1,0:T(8,128)(2,1)S(1)}, bf16[256,512]{1,0:T(8,128)(2,1)S(1)}) custom-call(s32[4]{0:T(128)S(1)} %pad_add_fusion.place_ref, bf16[1024,512]{1,0:T(8,128)(2,1)S(1)} %get-tuple-element.61.q_ref, f32[1024,256]{1,0:T(8,128)S(1)} %copy-done.1, f32[1024,512]{1,0:T(8,128)S(1)} %get-tuple-element.62.inner_ref.refs_3_, ...), custom_call_target="tpu_custom_call" | custom-call | flops 3000000000 | bytes 1000000 | tf_op jit(solution)/shard_map/finish/pallas_call | solution.py:310
  63.3 1.8 %finish.13 = (bf16[256,512]{1,0:T(8,128)(2,1)S(1)}, bf16[256,512]{1,0:T(8,128)(2,1)S(1)}) custom-call(s32[4]{0:T(128)S(1)} %pad_add_fusion.place_ref, bf16[1024,512]{1,0:T(8,128)(2,1)S(1)} %get-tuple-element.71.q_ref, f32[1024,256]{1,0:T(8,128)S(1)} %copy-done.1, f32[1024,512]{1,0:T(8,128)S(1)} %get-tuple-element.72.inner_ref.refs_3_, ...), custom_call_target="tpu_custom_call" | custom-call | flops 3000000000 | bytes 1000000 | tf_op jit(solution)/shard_map/finish/pallas_call | solution.py:310
  65.1 2.0 %finish.14 = (bf16[256,512]{1,0:T(8,128)(2,1)S(1)}, bf16[256,512]{1,0:T(8,128)(2,1)S(1)}) custom-call(s32[4]{0:T(128)S(1)} %pad_add_fusion.place_ref, bf16[1024,512]{1,0:T(8,128)(2,1)S(1)} %get-tuple-element.79.q_ref, f32[1024,256]{1,0:T(8,128)S(1)} %copy-done.1, f32[1024,512]{1,0:T(8,128)S(1)} %get-tuple-element.80.refs_0_.inner_ref, ...), custom_call_target="tpu_custom_call" | custom-call | flops 3000000000 | bytes 1000000 | tf_op jit(solution)/shard_map/finish/pallas_call | solution.py:310
  67.2 1.2 %collective-permute-start.13 = (bf16[256,512]{1,0:T(8,128)(2,1)S(1)}, bf16[256,512]{1,0:T(8,128)(2,1)S(1)}, u32[]{:S(2)}, u32[]{:S(2)}) collective-permute-start(bf16[256,512]{1,0:T(8,128)(2,1)S(1)} %get-tuple-element.82), channel_id=1, source_target_pairs={{0,2},{1,3},{2,0},{3,1},{4,6},{5,7},{6,4},{7,5},{8,10},{9,11},{10,... | collective-permute-start | bytes 786440 | tf_op jit(solution)/shard_map/ppermute | solution.py:449
  68.4 0.3 collective-permute-start.15
  68.7 1.8 %finish.15 = (bf16[256,512]{1,0:T(8,128)(2,1)S(1)}, bf16[256,512]{1,0:T(8,128)(2,1)S(1)}) custom-call(s32[4]{0:T(128)S(1)} %pad_add_fusion.place_ref, bf16[1024,512]{1,0:T(8,128)(2,1)S(1)} %get-tuple-element.84.q_ref, f32[1024,256]{1,0:T(8,128)S(1)} %copy-done.1, f32[1024,512]{1,0:T(8,128)S(1)} %get-tuple-element.81.refs_3_.inner_ref, ...), custom_call_target="tpu_custom_call" | custom-call | flops 3000000000 | bytes 1000000 | tf_op jit(solution)/shard_map/finish/pallas_call | solution.py:310
  70.5 1.7 %collective-permute-start.16 = (bf16[256,512]{1,0:T(8,128)(2,1)S(1)}, bf16[256,512]{1,0:T(8,128)(2,1)S(1)}, u32[]{:S(2)}, u32[]{:S(2)}) collective-permute-start(bf16[256,512]{1,0:T(8,128)(2,1)S(1)} %get-tuple-element.86.refs_3_), channel_id=1, source_target_pairs={{0,3},{1,2},{2,1},{3,0},{4,7},{5,6},{6,5},{7,4},{8,11},{9,10},{10,... | collective-permute-start | bytes 786440 | tf_op jit(solution)/shard_map/ppermute | solution.py:449
  72.3 2.8 %collective-permute-done.13.refs_4_ = bf16[256,512]{1,0:T(8,128)(2,1)S(1)} collective-permute-done((bf16[256,512]{1,0:T(8,128)(2,1)S(1)}, bf16[256,512]{1,0:T(8,128)(2,1)S(1)}, u32[]{:S(2)}, u32[]{:S(2)}) %collective-permute-start.13) | collective-permute-done | bytes 262176 | tf_op jit(solution)/shard_map/ppermute | solution.py:449
  75.1 1.3 %collective-permute-start.18 = (bf16[256,512]{1,0:T(8,128)(2,1)S(1)}, bf16[256,512]{1,0:T(8,128)(2,1)S(1)}, u32[]{:S(2)}, u32[]{:S(2)}) collective-permute-start(bf16[256,512]{1,0:T(8,128)(2,1)S(1)} %get-tuple-element.90.refs_3_), channel_id=1, source_target_pairs={{0,1},{1,0},{2,3},{3,2},{4,5},{5,4},{6,7},{7,6},{8,9},{9,8},{10,11... | collective-permute-start | bytes 786440 | tf_op jit(solution)/shard_map/ppermute | solution.py:449
  76.4 4.3 %collective-permute-done.15.refs_6_ = bf16[256,512]{1,0:T(8,128)(2,1)S(1)} collective-permute-done((bf16[256,512]{1,0:T(8,128)(2,1)S(1)}, bf16[256,512]{1,0:T(8,128)(2,1)S(1)}, u32[]{:S(2)}, u32[]{:S(2)}) %collective-permute-start.15) | collective-permute-done | bytes 262176 | tf_op jit(solution)/shard_map/ppermute | solution.py:449
  80.7 1.3 %collective-permute-start.20 = (bf16[256,512]{1,0:T(8,128)(2,1)S(1)}, bf16[256,512]{1,0:T(8,128)(2,1)S(1)}, u32[]{:S(2)}, u32[]{:S(2)}) collective-permute-start(bf16[256,512]{1,0:T(8,128)(2,1)S(1)} %get-tuple-element.94), channel_id=1, source_target_pairs={{0,1},{1,0},{2,3},{3,2},{4,5},{5,4},{6,7},{7,6},{8,9},{9,8},{10,11... | collective-permute-start | bytes 786440 | tf_op jit(solution)/shard_map/ppermute | solution.py:449
  82.1 4.5 %collective-permute-done.16.refs_7_ = bf16[256,512]{1,0:T(8,128)(2,1)S(1)} collective-permute-done((bf16[256,512]{1,0:T(8,128)(2,1)S(1)}, bf16[256,512]{1,0:T(8,128)(2,1)S(1)}, u32[]{:S(2)}, u32[]{:S(2)}) %collective-permute-start.16) | collective-permute-done | bytes 262176 | tf_op jit(solution)/shard_map/ppermute | solution.py:449
  86.6 6.6 %normalize.1 = bf16[256,8192]{1,0:T(8,128)(2,1)} custom-call(s32[4]{0:T(128)S(1)} %pad_add_fusion.place_ref, f32[1,8192]{1,0:T(1,128)S(1)} %bitcast.5, bf16[256,8192]{1,0:T(8,128)(2,1)S(1)} %copy-done, bf16[256,512]{1,0:T(8,128)(2,1)S(1)} %collective-permute-done.4.refs_0_, bf16[256,512]{1,0:T(8,128)(2,1)S(1)} %collective-permute-done.5.refs_1_, ...), custom_call_target="tpu_custom_call" | custom-call | flops 3000000000 | bytes 1000000 | tf_op jit(solution)/shard_map/normalize/pallas_call | solution.py:350
  (31 shorter events, 0.2 us)
Async XLA Ops:
  1.9 1.0 %copy-start.3 = (bf16[1024,512]{1,0:T(8,128)(2,1)}, bf16[1024,512]{1,0:T(8,128)(2,1)S(1)}, u32[]{:S(2)}) copy-start(bf16[1024,512]{1,0:T(8,128)(2,1)S(1)} %get-tuple-element.50.k_ref) | copy-start | bytes 3145732
  2.9 4.0 %copy-start.5 = (bf16[1024,512]{1,0:T(8,128)(2,1)}, bf16[1024,512]{1,0:T(8,128)(2,1)S(1)}, u32[]{:S(2)}) copy-start(bf16[1024,512]{1,0:T(8,128)(2,1)S(1)} %get-tuple-element.51.v_ref) | copy-start | bytes 3145732
  2.9 5.3 %collective-permute-start.1 = (bf16[4,128,128]{2,1,0:T(8,128)(2,1)S(1)}, bf16[4,128,128]{2,1,0:T(8,128)(2,1)S(1)}, u32[]{:S(2)}, u32[]{:S(2)}) collective-permute-start(bf16[4,128,128]{2,1,0:T(8,128)(2,1)S(1)} %get-tuple-element.52.refs_0_), channel_id=1, source_target_pairs={{0,4},{4,0},{8,12},{12,8},{16,20},{20,16},{24,28},{28,24},{1,5},{5... | collective-permute-start | bytes 393224 | tf_op jit(solution)/shard_map/ppermute | solution.py:395
  6.9 9.8 %collective-permute-start = (bf16[4,128,128]{2,1,0:T(8,128)(2,1)S(1)}, bf16[4,128,128]{2,1,0:T(8,128)(2,1)S(1)}, u32[]{:S(2)}, u32[]{:S(2)}) collective-permute-start(bf16[4,128,128]{2,1,0:T(8,128)(2,1)S(1)} %get-tuple-element.54.refs_0_), channel_id=1, source_target_pairs={{0,4},{4,0},{8,12},{12,8},{16,20},{20,16},{24,28},{28,24},{1,5},{5... | collective-permute-start | bytes 393224 | tf_op jit(solution)/shard_map/ppermute | solution.py:395
  8.2 5.5 %collective-permute-start.2 = (bf16[4,128,128]{2,1,0:T(8,128)(2,1)S(1)}, bf16[4,128,128]{2,1,0:T(8,128)(2,1)S(1)}, u32[]{:S(2)}, u32[]{:S(2)}) collective-permute-start(bf16[4,128,128]{2,1,0:T(8,128)(2,1)S(1)} %get-tuple-element.57.refs_0_), channel_id=1, source_target_pairs={{0,8},{4,12},{8,0},{12,4},{16,24},{20,28},{24,16},{28,20},{1,9},{5... | collective-permute-start | bytes 393224 | tf_op jit(solution)/shard_map/ppermute | solution.py:395
  12.4 18.2 %collective-permute-start.6 = (bf16[8,128,128]{2,1,0:T(8,128)(2,1)S(1)}, bf16[8,128,128]{2,1,0:T(8,128)(2,1)S(1)}, u32[]{:S(2)}, u32[]{:S(2)}) collective-permute-start(bf16[8,128,128]{2,1,0:T(8,128)(2,1)S(1)} %get-tuple-element.58.refs_0_), channel_id=1, source_target_pairs={{0,4},{4,0},{8,12},{12,8},{16,20},{20,16},{24,28},{28,24},{1,5},{5... | collective-permute-start | bytes 786440 | tf_op jit(solution)/shard_map/ppermute | solution.py:395
  14.4 9.1 %collective-permute-start.3 = (bf16[4,128,128]{2,1,0:T(8,128)(2,1)S(1)}, bf16[4,128,128]{2,1,0:T(8,128)(2,1)S(1)}, u32[]{:S(2)}, u32[]{:S(2)}) collective-permute-start(bf16[4,128,128]{2,1,0:T(8,128)(2,1)S(1)} %get-tuple-element.59.refs_0_), channel_id=1, source_target_pairs={{0,16},{4,20},{8,24},{12,28},{16,0},{20,4},{24,8},{28,12},{1,17},{... | collective-permute-start | bytes 393224 | tf_op jit(solution)/shard_map/ppermute | solution.py:395
  16.8 1.2 %copy-start.1 = (f32[1024,256]{1,0:T(8,128)S(1)}, f32[1024,256]{1,0:T(8,128)}, u32[]{:S(2)}) copy-start(f32[1024,256]{1,0:T(8,128)} %w_ref.23) | copy-start | bytes 3145732
  16.8 1.5 %copy-start.4 = (bf16[1024,512]{1,0:T(8,128)(2,1)S(1)}, bf16[1024,512]{1,0:T(8,128)(2,1)}, u32[]{:S(2)}) copy-start(bf16[1024,512]{1,0:T(8,128)(2,1)} %copy-done.3) | copy-start | bytes 3145732
  16.8 1.9 %copy-start.6 = (bf16[1024,512]{1,0:T(8,128)(2,1)S(1)}, bf16[1024,512]{1,0:T(8,128)(2,1)}, u32[]{:S(2)}) copy-start(bf16[1024,512]{1,0:T(8,128)(2,1)} %copy-done.5) | copy-start | bytes 3145732
  16.8 13.1 %collective-permute-start.7 = (bf16[4,128,128]{2,1,0:T(8,128)(2,1)S(1)}, bf16[4,128,128]{2,1,0:T(8,128)(2,1)S(1)}, u32[]{:S(2)}, u32[]{:S(2)}) collective-permute-start(bf16[4,128,128]{2,1,0:T(8,128)(2,1)S(1)} %get-tuple-element.60.refs_0_), channel_id=1, source_target_pairs={{0,8},{4,12},{8,0},{12,4},{16,24},{20,28},{24,16},{28,20},{1,9},{5... | collective-permute-start | bytes 393224 | tf_op jit(solution)/shard_map/ppermute | solution.py:395
  25.4 41.8 %collective-permute-start.4 = (bf16[256,512]{1,0:T(8,128)(2,1)S(1)}, bf16[256,512]{1,0:T(8,128)(2,1)S(1)}, u32[]{:S(2)}, u32[]{:S(2)}) collective-permute-start(bf16[256,512]{1,0:T(8,128)(2,1)S(1)} %get-tuple-element.63), channel_id=1, source_target_pairs={{0,2},{1,3},{2,0},{3,1},{4,6},{5,7},{6,4},{7,5},{8,10},{9,11},{10,... | collective-permute-start | bytes 786440 | tf_op jit(solution)/shard_map/ppermute | solution.py:449
  26.7 41.7 %collective-permute-start.5 = (bf16[256,512]{1,0:T(8,128)(2,1)S(1)}, bf16[256,512]{1,0:T(8,128)(2,1)S(1)}, u32[]{:S(2)}, u32[]{:S(2)}) collective-permute-start(bf16[256,512]{1,0:T(8,128)(2,1)S(1)} %get-tuple-element.64.refs_0_), channel_id=1, source_target_pairs={{0,3},{1,2},{2,1},{3,0},{4,7},{5,6},{6,5},{7,4},{8,11},{9,10},{10,... | collective-permute-start | bytes 786440 | tf_op jit(solution)/shard_map/ppermute | solution.py:449
  30.6 9.1 %collective-permute-start.8 = (bf16[4,128,128]{2,1,0:T(8,128)(2,1)S(1)}, bf16[4,128,128]{2,1,0:T(8,128)(2,1)S(1)}, u32[]{:S(2)}, u32[]{:S(2)}) collective-permute-start(bf16[4,128,128]{2,1,0:T(8,128)(2,1)S(1)} %get-tuple-element.69.refs_0_), channel_id=1, source_target_pairs={{0,16},{4,20},{8,24},{12,28},{16,0},{20,4},{24,8},{28,12},{1,17},{... | collective-permute-start | bytes 393224 | tf_op jit(solution)/shard_map/ppermute | solution.py:395
  30.8 13.0 %collective-permute-start.11 = (bf16[8,128,128]{2,1,0:T(8,128)(2,1)S(1)}, bf16[8,128,128]{2,1,0:T(8,128)(2,1)S(1)}, u32[]{:S(2)}, u32[]{:S(2)}) collective-permute-start(bf16[8,128,128]{2,1,0:T(8,128)(2,1)S(1)} %get-tuple-element.70.refs_0_), channel_id=1, source_target_pairs={{0,8},{4,12},{8,0},{12,4},{16,24},{20,28},{24,16},{28,20},{1,9},{5... | collective-permute-start | bytes 786440 | tf_op jit(solution)/shard_map/ppermute | solution.py:395
  41.5 29.0 %collective-permute-start.9 = (bf16[256,512]{1,0:T(8,128)(2,1)S(1)}, bf16[256,512]{1,0:T(8,128)(2,1)S(1)}, u32[]{:S(2)}, u32[]{:S(2)}) collective-permute-start(bf16[256,512]{1,0:T(8,128)(2,1)S(1)} %get-tuple-element.73), channel_id=1, source_target_pairs={{0,2},{1,3},{2,0},{3,1},{4,6},{5,7},{6,4},{7,5},{8,10},{9,11},{10,... | collective-permute-start | bytes 786440 | tf_op jit(solution)/shard_map/ppermute | solution.py:449
  42.1 30.1 %collective-permute-start.10 = (bf16[256,512]{1,0:T(8,128)(2,1)S(1)}, bf16[256,512]{1,0:T(8,128)(2,1)S(1)}, u32[]{:S(2)}, u32[]{:S(2)}) collective-permute-start(bf16[256,512]{1,0:T(8,128)(2,1)S(1)} %get-tuple-element.74.refs_0_), channel_id=1, source_target_pairs={{0,3},{1,2},{2,1},{3,0},{4,7},{5,6},{6,5},{7,4},{8,11},{9,10},{10,... | collective-permute-start | bytes 786440 | tf_op jit(solution)/shard_map/ppermute | solution.py:449
  44.6 12.6 %collective-permute-start.12 = (bf16[8,128,128]{2,1,0:T(8,128)(2,1)S(1)}, bf16[8,128,128]{2,1,0:T(8,128)(2,1)S(1)}, u32[]{:S(2)}, u32[]{:S(2)}) collective-permute-start(bf16[8,128,128]{2,1,0:T(8,128)(2,1)S(1)} %get-tuple-element.78.refs_0_), channel_id=1, source_target_pairs={{0,16},{4,20},{8,24},{12,28},{16,0},{20,4},{24,8},{28,12},{1,17},{... | collective-permute-start | bytes 786440 | tf_op jit(solution)/shard_map/ppermute | solution.py:395
  59.0 17.4 %collective-permute-start.14 = (bf16[256,512]{1,0:T(8,128)(2,1)S(1)}, bf16[256,512]{1,0:T(8,128)(2,1)S(1)}, u32[]{:S(2)}, u32[]{:S(2)}) collective-permute-start(bf16[256,512]{1,0:T(8,128)(2,1)S(1)} %get-tuple-element.83.refs_3_), channel_id=1, source_target_pairs={{0,3},{1,2},{2,1},{3,0},{4,7},{5,6},{6,5},{7,4},{8,11},{9,10},{10,... | collective-permute-start | bytes 786440 | tf_op jit(solution)/shard_map/ppermute | solution.py:449
  67.2 7.9 %collective-permute-start.13 = (bf16[256,512]{1,0:T(8,128)(2,1)S(1)}, bf16[256,512]{1,0:T(8,128)(2,1)S(1)}, u32[]{:S(2)}, u32[]{:S(2)}) collective-permute-start(bf16[256,512]{1,0:T(8,128)(2,1)S(1)} %get-tuple-element.82), channel_id=1, source_target_pairs={{0,2},{1,3},{2,0},{3,1},{4,6},{5,7},{6,4},{7,5},{8,10},{9,11},{10,... | collective-permute-start | bytes 786440 | tf_op jit(solution)/shard_map/ppermute | solution.py:449
  68.4 12.3 %collective-permute-start.15 = (bf16[256,512]{1,0:T(8,128)(2,1)S(1)}, bf16[256,512]{1,0:T(8,128)(2,1)S(1)}, u32[]{:S(2)}, u32[]{:S(2)}) collective-permute-start(bf16[256,512]{1,0:T(8,128)(2,1)S(1)} %get-tuple-element.85), channel_id=1, source_target_pairs={{0,2},{1,3},{2,0},{3,1},{4,6},{5,7},{6,4},{7,5},{8,10},{9,11},{10,... | collective-permute-start | bytes 786440 | tf_op jit(solution)/shard_map/ppermute | solution.py:449
  68.7 17.8 %copy-start = (bf16[256,8192]{1,0:T(8,128)(2,1)S(1)}, bf16[256,8192]{1,0:T(8,128)(2,1)}, u32[]{:S(2)}) copy-start(bf16[256,8192]{1,0:T(8,128)(2,1)} %gate_ref.1) | copy-start | bytes 12582916
  68.7 17.8 %copy-start.2 = (f32[8192]{0:T(1024)S(1)}, f32[8192]{0:T(1024)}, u32[]{:S(2)}) copy-start(f32[8192]{0:T(1024)} %param.11) | copy-start | bytes 98308
  70.5 16.0 %collective-permute-start.16 = (bf16[256,512]{1,0:T(8,128)(2,1)S(1)}, bf16[256,512]{1,0:T(8,128)(2,1)S(1)}, u32[]{:S(2)}, u32[]{:S(2)}) collective-permute-start(bf16[256,512]{1,0:T(8,128)(2,1)S(1)} %get-tuple-element.86.refs_3_), channel_id=1, source_target_pairs={{0,3},{1,2},{2,1},{3,0},{4,7},{5,6},{6,5},{7,4},{8,11},{9,10},{10,... | collective-permute-start | bytes 786440 | tf_op jit(solution)/shard_map/ppermute | solution.py:449
  72.3 14.2 %collective-permute-start.17 = (bf16[256,512]{1,0:T(8,128)(2,1)S(1)}, bf16[256,512]{1,0:T(8,128)(2,1)S(1)}, u32[]{:S(2)}, u32[]{:S(2)}) collective-permute-start(bf16[256,512]{1,0:T(8,128)(2,1)S(1)} %get-tuple-element.88.refs_3_), channel_id=1, source_target_pairs={{0,1},{1,0},{2,3},{3,2},{4,5},{5,4},{6,7},{7,6},{8,9},{9,8},{10,11... | collective-permute-start | bytes 786440 | tf_op jit(solution)/shard_map/ppermute | solution.py:449
  75.1 11.4 %collective-permute-start.18 = (bf16[256,512]{1,0:T(8,128)(2,1)S(1)}, bf16[256,512]{1,0:T(8,128)(2,1)S(1)}, u32[]{:S(2)}, u32[]{:S(2)}) collective-permute-start(bf16[256,512]{1,0:T(8,128)(2,1)S(1)} %get-tuple-element.90.refs_3_), channel_id=1, source_target_pairs={{0,1},{1,0},{2,3},{3,2},{4,5},{5,4},{6,7},{7,6},{8,9},{9,8},{10,11... | collective-permute-start | bytes 786440 | tf_op jit(solution)/shard_map/ppermute | solution.py:449
  76.4 10.1 %collective-permute-start.19 = (bf16[256,512]{1,0:T(8,128)(2,1)S(1)}, bf16[256,512]{1,0:T(8,128)(2,1)S(1)}, u32[]{:S(2)}, u32[]{:S(2)}) collective-permute-start(bf16[256,512]{1,0:T(8,128)(2,1)S(1)} %get-tuple-element.92.refs_3_), channel_id=1, source_target_pairs={{0,1},{1,0},{2,3},{3,2},{4,5},{5,4},{6,7},{7,6},{8,9},{9,8},{10,11... | collective-permute-start | bytes 786440 | tf_op jit(solution)/shard_map/ppermute | solution.py:449
  80.7 5.8 %collective-permute-start.20 = (bf16[256,512]{1,0:T(8,128)(2,1)S(1)}, bf16[256,512]{1,0:T(8,128)(2,1)S(1)}, u32[]{:S(2)}, u32[]{:S(2)}) collective-permute-start(bf16[256,512]{1,0:T(8,128)(2,1)S(1)} %get-tuple-element.94), channel_id=1, source_target_pairs={{0,1},{1,0},{2,3},{3,2},{4,5},{5,4},{6,7},{7,6},{8,9},{9,8},{10,11... | collective-permute-start | bytes 786440 | tf_op jit(solution)/shard_map/ppermute | solution.py:449

commit v2 on v1

v2 whole, which is shorter than its diff:
```python
import functools

import jax
import jax.numpy as jnp
from jax import lax
from jax.experimental import pallas as pl
from jax.experimental.pallas import tpu as pltpu
from jax.sharding import PartitionSpec as P

HEAD_DIM = 128
LEVELS = 16
CHUNK = 128
LANES = 128
SUB = 8
SUB_BITS = 3
GROUP = 2
PER_TILE = LANES // LEVELS
SIZES = (4, 4)
ORDER = (
    ("S", 0),
    ("S", 1),
    ("A", 0),
    ("S", 2),
    ("A", 0),
    ("A", 1),
    ("I", 0),
    ("A", 2),
    ("F", 0),
    ("A", 1),
    ("I", 1),
    ("A", 2),
    ("F", 1),
    ("I", 2),
    ("N", 0),
    ("F", 2),
    ("N", 1),
    ("N", 2),
)
TINY = pl.CostEstimate(flops=1024, bytes_accessed=1024, transcendentals=0)
LONG = pl.CostEstimate(flops=3 * 10**9, bytes_accessed=10**6, transcendentals=0)


def dot(a, b, dims=((1,), (0,))):
    return lax.dot_general(a, b, (dims, ((), ())), preferred_element_type=jnp.float32)


def anywhere():
    return pl.BlockSpec(memory_space=pl.ANY)


def cost(pairs):
    return LONG if pairs[0] else TINY


def local():
    return pl.BlockSpec(memory_space=pltpu.VMEM)


def params(mebibytes):
    return pltpu.CompilerParams(vmem_limit_bytes=mebibytes * 1024 * 1024)


def hbm():
    return pl.BlockSpec(memory_space=pltpu.HBM)


def in_hbm(array):
    return pltpu.with_memory_space_constraint(array, pltpu.HBM)


def in_vmem(array):
    return pltpu.with_memory_space_constraint(array, pltpu.VMEM)


def fetches(source_ref, held_ref, first, heads, sems):
    copies = []
    for n in range(heads // GROUP):
        source = pl.ds((first + n * GROUP) * HEAD_DIM, GROUP * HEAD_DIM)
        target = pl.ds(n * GROUP * HEAD_DIM, GROUP * HEAD_DIM)
        copies.append(
            pltpu.make_async_copy(source_ref.at[:, source], held_ref.at[:, target], sems.at[n])
        )
    return copies


def state_kernel(first, heads, k_ref, v_ref, *refs):
    rounded_ref, k_held, v_held, k_sems, v_sems = refs[-5:]
    k_copies = fetches(k_ref, k_held, first, heads, k_sems)
    v_copies = fetches(v_ref, v_held, first, heads, v_sems)
    for n in range(heads // GROUP):
        k_copies[n].start()
        v_copies[n].start()
    for n in range(heads // GROUP):
        k_copies[n].wait()
        v_copies[n].wait()
        for i in range(n * GROUP, (n + 1) * GROUP):
            here = slice(i * HEAD_DIM, (i + 1) * HEAD_DIM)
            state = dot(k_held[:, here], v_held[:, here], ((0,), (0,)))
            rounded_ref[i] = state.astype(jnp.bfloat16)


def block_states(keys, values, first, heads, after):
    held = pltpu.VMEM((keys.shape[0], heads * HEAD_DIM), keys.dtype)
    return pl.pallas_call(
        functools.partial(state_kernel, first, heads),
        in_specs=[hbm(), hbm()] + [anywhere() for _ in after],
        out_specs=local(),
        out_shape=jax.ShapeDtypeStruct((heads, HEAD_DIM, HEAD_DIM), jnp.bfloat16),
        scratch_shapes=[held, held] + [pltpu.SemaphoreType.DMA((heads // GROUP,))] * 2,
        compiler_params=params(12),
        cost_estimate=LONG,
        name="block_states",
    )(in_hbm(keys), in_hbm(values), *after)


def add_kernel(total_ref, held_ref, *refs):
    sum_ref = refs[-1]
    total = total_ref[...].astype(jnp.float32) + held_ref[...].astype(jnp.float32)
    sum_ref[...] = total.astype(jnp.bfloat16)


def add_states(total, held, after):
    return pl.pallas_call(
        add_kernel,
        in_specs=[local()] * 2 + [anywhere() for _ in after],
        out_specs=local(),
        out_shape=jax.ShapeDtypeStruct(total.shape, jnp.bfloat16),
        compiler_params=params(4),
        cost_estimate=LONG,
        name="add_states",
    )(in_vmem(total), held, *after)


def factor_rows(weights, near_mix, far_mix):
    chunk = weights.shape[1]
    bits = chunk.bit_length() - 1
    row = [jnp.broadcast_to(weights[l : l + 1], (SUB, chunk)) for l in range(bits + 1)]
    near = row[0]
    for level in range(1, SUB_BITS + 1):
        near = jnp.where(near_mix >= 1 << (level - 1), row[level], near)
    near = jnp.where(near_mix >= SUB, jnp.float32(0.0), near)
    far = []
    for mix in far_mix:
        value = jnp.zeros((SUB, chunk), jnp.float32)
        for level in range(SUB_BITS + 1, bits + 1):
            value = jnp.where(mix >= 1 << (level - SUB_BITS - 1), row[level], value)
        far.append(value)
    return near, far


def inner_kernel(
    first, heads, pairs, rows, place_ref, q_source, k_source, v_source, w_ref, *refs
):
    out_ref, q_ref, k_ref, v_ref, wt_ref, sems, kv_sems = refs[-7:]
    wide = GROUP * HEAD_DIM
    spots = [jnp.bitwise_xor(jnp.right_shift(place_ref[0], 1), pair) for pair in pairs]

    def fetch(step, n):
        source = pl.ds(pl.multiple_of((first + step * GROUP) * HEAD_DIM, HEAD_DIM), wide)
        target = pl.ds(pl.multiple_of(step * wide, wide), wide)
        above = pl.ds(pl.multiple_of(spots[n] * rows, rows), rows)
        return pltpu.make_async_copy(
            q_source.at[above, source],
            q_ref.at[n * rows : (n + 1) * rows, target],
            sems.at[n, step],
        )

    def fetch_whole(step, m):
        source = pl.ds(pl.multiple_of((first + step * GROUP) * HEAD_DIM, HEAD_DIM), wide)
        target = pl.ds(pl.multiple_of(step * wide, wide), wide)
        return pltpu.make_async_copy(
            (k_source, v_source)[m].at[:, source],
            (k_ref, v_ref)[m].at[:, target],
            kv_sems.at[m, step],
        )

    for step in range(heads // GROUP):
        for m in range(2):
            fetch_whole(step, m).start()
        for n in range(len(pairs)):
            fetch(step, n).start()
    count = k_ref.shape[0]
    chunk = min(CHUNK, rows)
    chunks = rows // chunk
    chunk_bits = chunk.bit_length() - 1
    row_bits = rows.bit_length() - 1
    blocks = count // rows
    groups = chunk // SUB
    low_tile = first // PER_TILE
    tiles = (first + heads - 1) // PER_TILE + 1 - low_tile

    def span(n, c):
        return pl.ds(pl.multiple_of(spots[n] * rows + c * chunk, chunk), chunk)

    for tile in range(tiles):
        lanes = slice((low_tile + tile) * LANES, (low_tile + tile + 1) * LANES)
        for n in range(len(pairs)):
            for c in range(chunks):
                here = slice(n * rows + c * chunk, n * rows + (c + 1) * chunk)
                wt_ref[tile * LANES : (tile + 1) * LANES, here] = w_ref[span(n, c), lanes].T

    t = lax.broadcasted_iota(jnp.int32, (SUB, chunk), 1)
    s = lax.broadcasted_iota(jnp.int32, (SUB, chunk), 0)
    t_low, t_high = t & (SUB - 1), t >> SUB_BITS
    near_mix = jnp.where(s <= t_low, s ^ t_low, SUB)
    far_mix = []
    for a in range(max(1, groups // SUB)):
        s_high = s + SUB * a
        far_mix.append(jnp.where(t_high > s_high, t_high ^ s_high, 0))

    def group(step, carry):
        for m in range(2):
            fetch_whole(step, m).wait()
        for n in range(len(pairs)):
            fetch(step, n).wait()
        head = first + step * GROUP
        lane = pl.multiple_of(head // PER_TILE * LANES, LANES)
        base = head % PER_TILE * LEVELS
        rows_base = lane - low_tile * LANES + base
        shift = (LANES - base) % LANES
        weights = []
        for n in range(len(pairs)):
            above = pl.ds(pl.multiple_of(spots[n] * rows, rows), rows)
            weights.append(pltpu.roll(w_ref[above, pl.ds(lane, LANES)], shift, 1))
        sums, outer = {}, {}

        def columns(i):
            place = (step * GROUP + i) * HEAD_DIM
            return pl.ds(pl.multiple_of(place, HEAD_DIM), HEAD_DIM)

        def outer_tiers(i):
            held = columns(i)
            states = []
            for block in range(blocks - 1):
                here = slice(block * rows, (block + 1) * rows)
                states.append(dot(k_ref[here, held], v_ref[here, held], ((0,), (0,))))
            for n, spot in enumerate(spots):
                for bit in range(blocks.bit_length() - 1):
                    tier = jnp.zeros((HEAD_DIM, HEAD_DIM), jnp.float32)
                    for block, state in enumerate(states):
                        if not block >> bit & 1:
                            same = jnp.right_shift(spot, bit + 1) == block >> (bit + 1)
                            upper = (jnp.right_shift(spot, bit) & 1) == 1
                            tier += jnp.where(same & upper, state, jnp.float32(0.0))
                    outer[i, n, bit] = tier.astype(jnp.bfloat16)

        def scores_of(i, n, c):
            held = columns(i)
            here = slice(n * rows + c * chunk, n * rows + (c + 1) * chunk)
            q, k, v = q_ref[here, columns(i)], k_ref[span(n, c), held], v_ref[span(n, c), held]
            scores = dot(k, q, ((1,), (1,)))
            terms = []
            for bit in range(chunks.bit_length() - 1):
                if c >> bit & 1:
                    tier = sums[i, n, bit].astype(jnp.bfloat16)
                    terms.append((chunk_bits + 1 + bit, dot(q, tier)))
            for bit in range(blocks.bit_length() - 1):
                terms.append((row_bits + 1 + bit, dot(q, outer[i, n, bit])))
            if c + 1 < chunks:
                state = dot(k, v, ((0,), (0,)))
                for bit in range(chunks.bit_length() - 1):
                    if not c >> bit & 1:
                        fresh = c % (1 << bit) == 0
                        sums[i, n, bit] = state if fresh else sums[i, n, bit] + state
            return scores, terms

        def store(i, n, c, scores, terms):
            here = slice(n * rows + c * chunk, n * rows + (c + 1) * chunk)
            own_rows = pl.ds(pl.multiple_of(rows_base + i * LEVELS, LEVELS), LEVELS)
            near, far = factor_rows(wt_ref[own_rows, here], near_mix, far_mix)
            parts = []
            for r in range(groups):
                line = jnp.broadcast_to(far[r // SUB][r % SUB : r % SUB + 1], (SUB, chunk))
                factor = jnp.where(t_high == r, near, line)
                parts.append(scores[r * SUB : (r + 1) * SUB] * factor)
            weighted = jnp.concatenate(parts, axis=0).astype(jnp.bfloat16)
            total = dot(weighted, v_ref[span(n, c), columns(i)], ((0,), (0,)))
            for level, term in terms:
                column = i * LEVELS + level
                scale = weights[n][c * chunk : (c + 1) * chunk, column : column + 1]
                total += scale * term
            out_ref[here, columns(i)] = total

        waiting = []
        for i in range(GROUP):
            outer_tiers(i)
            for n in range(len(pairs)):
                for c in range(chunks):
                    waiting.append((i, n, c) + scores_of(i, n, c))
                    if len(waiting) > 2:
                        store(*waiting.pop(0))
        for unit in waiting:
            store(*unit)
        return carry

    lax.fori_loop(0, heads // GROUP, group, 0)


def inner_part(
    place, queries, keys, values, weights, chunk_first, start, heads, pairs, parts, after
):
    rows = 2 * queries.shape[0] // parts
    first = chunk_first + start
    tiles = (first + heads - 1) // PER_TILE + 1 - first // PER_TILE
    shape = (len(pairs) * rows, heads * HEAD_DIM)
    return pl.pallas_call(
        functools.partial(inner_kernel, first, heads, tuple(pairs), rows),
        in_specs=[pl.BlockSpec(memory_space=pltpu.SMEM), hbm(), hbm(), hbm(), local()]
        + [anywhere() for _ in after],
        out_specs=[local()] * 2,
        out_shape=[
            jax.ShapeDtypeStruct(shape, jnp.float32),
            jax.ShapeDtypeStruct(shape, queries.dtype),
        ],
        scratch_shapes=[
            pltpu.VMEM((queries.shape[0], shape[1]), keys.dtype),
            pltpu.VMEM((queries.shape[0], shape[1]), values.dtype),
            pltpu.VMEM((tiles * LANES, shape[0]), jnp.float32),
            pltpu.SemaphoreType.DMA((len(pairs), heads // GROUP)),
            pltpu.SemaphoreType.DMA((2, heads // GROUP)),
        ],
        compiler_params=params(12),
        cost_estimate=cost(pairs),
        name="inner_part",
    )(place, in_hbm(queries), in_hbm(keys), in_hbm(values), weights, *after)


def finish_kernel(first, start, heads, pairs, levels, place_ref, q_ref, w_ref, inner_ref, *refs):
    tiers = refs[:levels]
    outs = refs[len(refs) - 2 * len(pairs) :]
    local_bits = w_ref.shape[0].bit_length() - 1
    rows = outs[0].shape[0]
    flip = (place_ref[0] & 1) == 1

    def group(step, carry):
        head = first + step * GROUP
        lane = pl.multiple_of(head // PER_TILE * LANES, LANES)
        base = head % PER_TILE * LEVELS
        for n, pair in enumerate(pairs):
            spot = jnp.bitwise_xor(jnp.right_shift(place_ref[0], 1), pair)
            here = pl.ds(pl.multiple_of(spot * (2 * rows), 2 * rows), 2 * rows)
            weights = pltpu.roll(w_ref[here, pl.ds(lane, LANES)], (LANES - base) % LANES, 1)
            for i in range(GROUP):
                cols = pl.ds(pl.multiple_of((step * GROUP + i) * HEAD_DIM, HEAD_DIM), HEAD_DIM)
                own = slice(2 * n * rows, 2 * (n + 1) * rows)
                q = q_ref[own, cols]
                total = inner_ref[own, cols]
                for m in range(levels):
                    level = i * LEVELS + local_bits + 1 + m
                    held = place_ref[1 + m].astype(jnp.float32)
                    tier = tiers[m][start + step * GROUP + i]
                    total += (weights[:, level : level + 1] * held) * dot(q, tier)
                upper, lower = total[:rows], total[rows:]
                outs[2 * n][:, cols] = jnp.where(flip, lower, upper).astype(jnp.bfloat16)
                outs[2 * n + 1][:, cols] = jnp.where(flip, upper, lower).astype(jnp.bfloat16)
        return carry

    lax.fori_loop(0, heads // GROUP, group, 0)


def finish(place, tiers, queries, inner, weights, chunk_first, start, heads, pairs, parts, after):
    rows = weights.shape[0] // parts
    outs = 2 * len(pairs)
    return pl.pallas_call(
        functools.partial(
            finish_kernel, chunk_first + start, start, heads, tuple(pairs), len(tiers)
        ),
        in_specs=[pl.BlockSpec(memory_space=pltpu.SMEM)]
        + [local()] * (3 + len(tiers))
        + [anywhere() for _ in after],
        out_specs=[local()] * outs,
        out_shape=[
            jax.ShapeDtypeStruct((rows, heads * HEAD_DIM), jnp.bfloat16) for _ in range(outs)
        ],
        compiler_params=params(8),
        cost_estimate=cost(pairs),
        name="finish",
    )(place, queries, weights, inner, *tiers, *after)


def gate_kernel(gain_ref, gate_ref, *refs):
    out_ref = refs[-1]
    tile = min(LANES * SUB, out_ref.shape[1])

    def columns(j, carry):
        here = pl.ds(pl.multiple_of(j * tile, tile), tile)
        half = gate_ref[:, here].astype(jnp.float32) * 0.5
        out_ref[:, here] = (half + half * jnp.tanh(half)) * gain_ref[:, here]
        return carry

    lax.fori_loop(0, out_ref.shape[1] // tile, columns, 0)


def gating(gain, gate, after):
    return pl.pallas_call(
        gate_kernel,
        in_specs=[local()] * 2 + [anywhere() for _ in after],
        out_specs=local(),
        out_shape=jax.ShapeDtypeStruct(gate.shape, jnp.float32),
        compiler_params=params(8),
        cost_estimate=TINY,
        name="gating",
    )(gain.reshape(1, gain.shape[0]), gate, *after)


def norm_kernel(layout, width, place_ref, gating_ref, *refs):
    out_ref = refs[-1]
    pieces = refs[:-1]
    tile = out_ref.shape[0]
    rows = pl.ds(pl.multiple_of(pl.program_id(0) * tile, tile), tile)
    square = None
    for ref in pieces:
        x = ref[rows, :].astype(jnp.float32)
        part = jnp.sum(x * x, axis=1, keepdims=True)
        square = part if square is None else square + part
    scale = lax.rsqrt(square / out_ref.shape[1] + 1e-06)
    for (step, start), ref in zip(layout, pieces):
        offset = pl.multiple_of(jnp.bitwise_xor(place_ref[0], step) * width + start, LANES)
        here = pl.ds(offset, ref.shape[1])
        x = ref[rows, :].astype(jnp.float32) * scale
        out_ref[:, here] = (x * gating_ref[rows, here]).astype(jnp.bfloat16)


def normalize(place, gated, layout, pieces, width):
    rows, features = gated.shape
    tile = min(64, rows)
    return pl.pallas_call(
        functools.partial(norm_kernel, layout, width),
        grid=(rows // tile,),
        in_specs=[pl.BlockSpec(memory_space=pltpu.SMEM)] + [local()] * (1 + len(pieces)),
        out_specs=pl.BlockSpec((tile, features), lambda i: (i, 0)),
        out_shape=jax.ShapeDtypeStruct((rows, features), jnp.bfloat16),
        compiler_params=params(8),
        cost_estimate=LONG,
        name="normalize",
    )(place, in_vmem(gated), *pieces)


def cut(heads):
    sizes = []
    for size in SIZES:
        if heads - sum(sizes) > size:
            sizes.append(size)
    return sizes + [heads - sum(sizes)]


def per_device(queries, key_vectors, value_vectors, level_weight, gate_values, norm_gain):
    count, width = queries.shape
    heads = width // HEAD_DIM
    blocks = lax.axis_size("seq")
    parts = lax.axis_size("head")
    seq_bits = blocks.bit_length() - 1
    block = lax.axis_index("seq")
    flags = [jnp.right_shift(block, m) & 1 for m in range(seq_bits)]
    place = jnp.stack([lax.axis_index("head")] + flags).astype(jnp.int32)

    sizes = cut(heads)
    chunks = range(len(sizes))
    firsts = [sum(sizes[:g]) for g in chunks]

    sends, tiers, inner = {}, {}, {}
    pieces, layout, arrived = [], [], {}
    last = {}

    def hop(g):
        m = len(tiers[g])
        pairs = [(i, i ^ 1 << m) for i in range(blocks)]
        tiers[g].append(lax.ppermute(sends[g], "seq", pairs))

    def state_step(g):
        sends[g] = block_states(
            key_vectors, value_vectors, firsts[g], sizes[g], tuple(last.values())
        )
        tiers[g] = []
        last["kernel"] = sends[g]
        hop(g)

    def add_step(g):
        if len(tiers[g]) < seq_bits:
            sends[g] = add_states(sends[g], tiers[g][-1], tuple(last.values()))
            last["kernel"] = sends[g]
            hop(g)

    def inner_step(g, pairs, start, size):
        inner[g] = inner_part(
            place,
            queries,
            key_vectors,
            value_vectors,
            level_weight,
            firsts[g],
            start,
            size,
            pairs,
            parts,
            tuple(last.values()),
        )
        last["kernel"] = inner[g][0]

    def finish_step(g, pairs, start, size):
        part, q_part = inner[g]
        behind = g - 2 if pairs[0] else g - 1 if g == len(sizes) - 1 else -1
        before = tuple(arrived.get(behind, ()))
        outs = finish(
            place,
            tiers[g],
            q_part,
            part,
            level_weight,
            firsts[g],
            start,
            size,
            pairs,
            parts,
            tuple(last.values()) + before,
        )
        last["kernel"] = outs[-1]
        for step, out in enumerate(outs, 2 * pairs[0]):
            if step:
                out = lax.ppermute(out, "head", [(i, i ^ step) for i in range(parts)])
            pieces.append(out)
            layout.append((step, (firsts[g] + start) * HEAD_DIM))
            if pairs[0]:
                arrived.setdefault(g, []).append(out)

    far, near = range(1, parts // 2), range(1)
    for kind, g in ORDER:
        if g >= len(sizes):
            continue
        if kind == "S":
            state_step(g)
        if kind == "A":
            add_step(g)
        if kind == "I":
            inner_step(g, far, 0, sizes[g])
        if kind == "F":
            for _ in range(seq_bits):
                add_step(g)
            finish_step(g, far, 0, sizes[g])
        if kind == "N":
            for start in range(0, sizes[g], SIZES[0]):
                size = min(SIZES[0], sizes[g] - start)
                inner_step(g, near, start, size)
                finish_step(g, near, start, size)
    gated = gating(norm_gain, gate_values, tuple(last.values()))
    return normalize(place, gated, layout, pieces, width)


def solution(mesh):
    placed = (
        P("seq", "head"),
        P("seq", "head"),
        P("seq", "head"),
        P("seq", "head"),
        P(("seq", "head"), None),
        P(),
    )
    return jax.shard_map(
        per_device, mesh=mesh, in_specs=placed, out_specs=P(("seq", "head"), None), check_vma=False
    )
```

time: 93.6 us -> 85.3 us (0.911)
  waiting for transfers between devices: 18.6 us -> 4.58 us
  Pallas kernels: 50.4 us -> 58.6 us
  local copies, waits for them, and re-layouts: 2.55 us -> 0.27 us
    pallas_call x4 -> x8, Pallas kernels: 19.9 us -> 33.6 us  [the longest x7 31.9 us: inner_part(): pl.pallas_call(functools.partial(inner_kernel, first, heads, tuple(pairs)...]
    ppermute x12 -> x10, waiting for transfers between devices: 11.6 us -> 1.98 us  [finish_step(): out = lax.ppermute(out, 'head', [(i, i ^ step) for i in range(parts)])]
    ppermute x9, waiting for transfers between devices: 7.06 us -> 2.61 us  [hop(): tiers[g].append(lax.ppermute(sends[g], 'seq', pairs))]
    ppermute x12 -> x10, starting transfers between devices: 13.3 us -> 9.96 us  [finish_step(): out = lax.ppermute(out, 'head', [(i, i ^ step) for i in range(parts)])]
    ppermute x9, starting transfers between devices: 7.99 us -> 11.2 us  [hop(): tiers[g].append(lax.ppermute(sends[g], 'seq', pairs))]
    pallas_call x1, Pallas kernels: 6.61 us -> 4.17 us  [normalize(): pl.pallas_call(functools.partial(norm_kernel, layout, width), grid=(rows...]
    unnamed x14 -> x6, local copies, waits for them, and re-layouts: 2.55 us -> 0.27 us
    pallas_call x6, Pallas kernels: 2.48 us -> 0.26 us  [add_states(): pl.pallas_call(add_kernel, in_specs=[local()] * 2 + [anywhere() for _ in...]
  transfers between devices with their start and end apart: 21 -> 19, of which waited for: 6 -> 3; matrix products, arithmetic and copies ran while one was open for 0% -> 0% of each run, Pallas kernels for 45% -> 62%
where the time goes in v2:
time: 85.3 us; the launch traced here: 85 us
  Pallas kernels  58.6 us (69%)
  starting transfers between devices  21.2 us (25%)
  waiting for transfers between devices  4.58 us (5%)
    pallas_call x7, Pallas kernels, inner_part(): pl.pallas_call(functools.partial(inner_kernel, first, heads, tuple(pairs)...  31.9 us
    pallas_call x7, Pallas kernels, finish(): pl.pallas_call(functools.partial(finish_kernel, chunk_first + start, star...  13.8 us
    ppermute x9, starting transfers between devices, hop(): tiers[g].append(lax.ppermute(sends[g], 'seq', pairs))  11.2 us
    ppermute x10, starting transfers between devices, finish_step(): out = lax.ppermute(out, 'head', [(i, i ^ step) for i in range(parts)])  9.96 us
    pallas_call x3, Pallas kernels, block_states(): pl.pallas_call(functools.partial(state_kernel, first, heads), in_specs=[h...  6.78 us
    pallas_call x1, Pallas kernels, normalize(): pl.pallas_call(functools.partial(norm_kernel, layout, width), grid=(rows...  4.17 us
    ppermute x9, waiting for transfers between devices, hop(): tiers[g].append(lax.ppermute(sends[g], 'seq', pairs))  2.61 us
    ppermute x10, waiting for transfers between devices, finish_step(): out = lax.ppermute(out, 'head', [(i, i ^ step) for i in range(parts)])  1.98 us
  transfers between devices with their start and end apart: 19, of which 3 were waited for; matrix products, arithmetic and copies ran while one was open for 0% of the time, Pallas kernels for 62%

profile of v2, /device:TPU:1, one launch (start us, length us, event | category | flops | bytes accessed | tf_op | source)
XLA Modules:
  0.0 85.0 jit_solution(17819937078282011100)
XLA Ops:
  0.0 1.9 %block_states.3.refs_0_.total_ref = bf16[4,128,128]{2,1,0:T(8,128)(2,1)S(1)} custom-call(bf16[1024,2048]{1,0:T(8,128)(2,1)} %k_source.13, bf16[1024,2048]{1,0:T(8,128)(2,1)} %v_source.13), custom_call_target="tpu_custom_call" | custom-call | flops 3000000000 | bytes 1000000 | tf_op jit(solution)/shard_map/block_states/pallas_call | solution.py:104
  1.9 2.1 %collective-permute-start.1 = (bf16[4,128,128]{2,1,0:T(8,128)(2,1)S(1)}, bf16[4,128,128]{2,1,0:T(8,128)(2,1)S(1)}, u32[]{:S(2)}, u32[]{:S(2)}) collective-permute-start(bf16[4,128,128]{2,1,0:T(8,128)(2,1)S(1)} %block_states.3.refs_0_.total_ref), channel_id=1, source_target_pairs={{0,4},{4,0},{8,12},{12,8},{16,20},{20,16},{24,28},{28,24},{1,5},{5... | collective-permute-start | bytes 393224 | tf_op jit(solution)/shard_map/ppermute | solution.py:468
  4.0 1.9 %block_states.4.refs_0_.total_ref = bf16[4,128,128]{2,1,0:T(8,128)(2,1)S(1)} custom-call(bf16[1024,2048]{1,0:T(8,128)(2,1)} %k_source.13, bf16[1024,2048]{1,0:T(8,128)(2,1)} %v_source.13, bf16[4,128,128]{2,1,0:T(8,128)(2,1)S(1)} %block_states.3.refs_0_.total_ref), custom_call_target="tpu_custom_call" | custom-call | flops 3000000000 | bytes 1000000 | tf_op jit(solution)/shard_map/block_states/pallas_call | solution.py:104
  6.0 0.1 collective-permute-start
  6.1 0.1 pad_add_fusion.place_ref
  6.1 1.1 %collective-permute-done.1.held_ref.refs_0_ = bf16[4,128,128]{2,1,0:T(8,128)(2,1)S(1)} collective-permute-done((bf16[4,128,128]{2,1,0:T(8,128)(2,1)S(1)}, bf16[4,128,128]{2,1,0:T(8,128)(2,1)S(1)}, u32[]{:S(2)}, u32[]{:S(2)}) %collective-permute-start.1) | collective-permute-done | bytes 131104 | tf_op jit(solution)/shard_map/ppermute | solution.py:468
  7.3 1.3 %collective-permute-start.2 = (bf16[4,128,128]{2,1,0:T(8,128)(2,1)S(1)}, bf16[4,128,128]{2,1,0:T(8,128)(2,1)S(1)}, u32[]{:S(2)}, u32[]{:S(2)}) collective-permute-start(bf16[4,128,128]{2,1,0:T(8,128)(2,1)S(1)} %add_states.6.refs_0_.total_ref), channel_id=1, source_target_pairs={{0,8},{4,12},{8,0},{12,4},{16,24},{20,28},{24,16},{28,20},{1,9},{5... | collective-permute-start | bytes 393224 | tf_op jit(solution)/shard_map/ppermute | solution.py:468
  8.6 2.9 %block_states.5.refs_0_.total_ref = bf16[8,128,128]{2,1,0:T(8,128)(2,1)S(1)} custom-call(bf16[1024,2048]{1,0:T(8,128)(2,1)} %k_source.13, bf16[1024,2048]{1,0:T(8,128)(2,1)} %v_source.13, bf16[4,128,128]{2,1,0:T(8,128)(2,1)S(1)} %add_states.6.refs_0_.total_ref), custom_call_target="tpu_custom_call" | custom-call | flops 3000000000 | bytes 1000000 | tf_op jit(solution)/shard_map/block_states/pallas_call | solution.py:104
  11.5 1.3 %collective-permute-start.5 = (bf16[8,128,128]{2,1,0:T(8,128)(2,1)S(1)}, bf16[8,128,128]{2,1,0:T(8,128)(2,1)S(1)}, u32[]{:S(2)}, u32[]{:S(2)}) collective-permute-start(bf16[8,128,128]{2,1,0:T(8,128)(2,1)S(1)} %block_states.5.refs_0_.total_ref), channel_id=1, source_target_pairs={{0,4},{4,0},{8,12},{12,8},{16,20},{20,16},{24,28},{28,24},{1,5},{5... | collective-permute-start | bytes 786440 | tf_op jit(solution)/shard_map/ppermute | solution.py:468
  12.8 0.0 copy-start
  12.8 2.4 %collective-permute-start.4 = (bf16[4,128,128]{2,1,0:T(8,128)(2,1)S(1)}, bf16[4,128,128]{2,1,0:T(8,128)(2,1)S(1)}, u32[]{:S(2)}, u32[]{:S(2)}) collective-permute-start(bf16[4,128,128]{2,1,0:T(8,128)(2,1)S(1)} %add_states.7.refs_0_), channel_id=1, source_target_pairs={{0,16},{4,20},{8,24},{12,28},{16,0},{20,4},{24,8},{28,12},{1,17},{... | collective-permute-start | bytes 393224 | tf_op jit(solution)/shard_map/ppermute | solution.py:468
  15.3 0.2 collective-permute-start.3
  15.5 4.2 %inner_part.7 = (f32[512,512]{1,0:T(8,128)S(1)}, bf16[512,512]{1,0:T(8,128)(2,1)S(1)}) custom-call(s32[4]{0:T(128)S(1)} %pad_add_fusion.place_ref, bf16[1024,2048]{1,0:T(8,128)(2,1)} %q_source.13, bf16[1024,2048]{1,0:T(8,128)(2,1)} %k_source.13, bf16[1024,2048]{1,0:T(8,128)(2,1)} %v_source.13, f32[1024,256]{1,0:T(8,128)S(1)} %copy-done, ...), custom_call_target="tpu_custom_call" | custom-call | flops 3000000000 | bytes 1000000 | tf_op jit(solution)/shard_map/inner_part/pallas_call | solution.py:306
  19.7 0.1 add_states.9.refs_3_.total_ref
  19.8 1.4 %collective-permute-start.7 = (bf16[8,128,128]{2,1,0:T(8,128)(2,1)S(1)}, bf16[8,128,128]{2,1,0:T(8,128)(2,1)S(1)}, u32[]{:S(2)}, u32[]{:S(2)}) collective-permute-start(bf16[8,128,128]{2,1,0:T(8,128)(2,1)S(1)} %add_states.9.refs_3_.total_ref), channel_id=1, source_target_pairs={{0,8},{4,12},{8,0},{12,4},{16,24},{20,28},{24,16},{28,20},{1,9},{5... | collective-permute-start | bytes 786440 | tf_op jit(solution)/shard_map/ppermute | solution.py:468
  21.2 1.8 %finish.7 = (bf16[256,512]{1,0:T(8,128)(2,1)S(1)}, bf16[256,512]{1,0:T(8,128)(2,1)S(1)}) custom-call(s32[4]{0:T(128)S(1)} %pad_add_fusion.place_ref, bf16[512,512]{1,0:T(8,128)(2,1)S(1)} %get-tuple-element.33.q_ref, f32[1024,256]{1,0:T(8,128)S(1)} %copy-done, f32[512,512]{1,0:T(8,128)S(1)} %get-tuple-element.34.refs_0_.inner_ref, ...), custom_call_target="tpu_custom_call" | custom-call | flops 3000000000 | bytes 1000000 | tf_op jit(solution)/shard_map/finish/pallas_call | solution.py:364
  22.9 4.7 %collective-permute-start.10 = (bf16[256,512]{1,0:T(8,128)(2,1)S(1)}, bf16[256,512]{1,0:T(8,128)(2,1)S(1)}, u32[]{:S(2)}, u32[]{:S(2)}) collective-permute-start(bf16[256,512]{1,0:T(8,128)(2,1)S(1)} %get-tuple-element.35.refs_0_), channel_id=1, source_target_pairs={{0,3},{1,2},{2,1},{3,0},{4,7},{5,6},{6,5},{7,4},{8,11},{9,10},{10,... | collective-permute-start | bytes 786440 | tf_op jit(solution)/shard_map/ppermute | solution.py:520
  27.6 0.1 collective-permute-start.6
  27.8 0.2 collective-permute-start.9
  28.0 4.2 %inner_part.8 = (f32[512,512]{1,0:T(8,128)S(1)}, bf16[512,512]{1,0:T(8,128)(2,1)S(1)}) custom-call(s32[4]{0:T(128)S(1)} %pad_add_fusion.place_ref, bf16[1024,2048]{1,0:T(8,128)(2,1)} %q_source.13, bf16[1024,2048]{1,0:T(8,128)(2,1)} %k_source.13, bf16[1024,2048]{1,0:T(8,128)(2,1)} %v_source.13, f32[1024,256]{1,0:T(8,128)S(1)} %copy-done, ...), custom_call_target="tpu_custom_call" | custom-call | flops 3000000000 | bytes 1000000 | tf_op jit(solution)/shard_map/inner_part/pallas_call | solution.py:306
  32.2 0.1 add_states.11.refs_3_
  32.3 2.4 %collective-permute-start.8 = (bf16[8,128,128]{2,1,0:T(8,128)(2,1)S(1)}, bf16[8,128,128]{2,1,0:T(8,128)(2,1)S(1)}, u32[]{:S(2)}, u32[]{:S(2)}) collective-permute-start(bf16[8,128,128]{2,1,0:T(8,128)(2,1)S(1)} %add_states.11.refs_3_), channel_id=1, source_target_pairs={{0,16},{4,20},{8,24},{12,28},{16,0},{20,4},{24,8},{28,12},{1,17},{... | collective-permute-start | bytes 786440 | tf_op jit(solution)/shard_map/ppermute | solution.py:468
  34.7 1.5 %collective-permute-done.6.refs_2_ = bf16[4,128,128]{2,1,0:T(8,128)(2,1)S(1)} collective-permute-done((bf16[4,128,128]{2,1,0:T(8,128)(2,1)S(1)}, bf16[4,128,128]{2,1,0:T(8,128)(2,1)S(1)}, u32[]{:S(2)}, u32[]{:S(2)}) %collective-permute-start.6) | collective-permute-done | bytes 131104 | tf_op jit(solution)/shard_map/ppermute | solution.py:468
  36.1 1.8 %finish.8 = (bf16[256,512]{1,0:T(8,128)(2,1)S(1)}, bf16[256,512]{1,0:T(8,128)(2,1)S(1)}) custom-call(s32[4]{0:T(128)S(1)} %pad_add_fusion.place_ref, bf16[512,512]{1,0:T(8,128)(2,1)S(1)} %get-tuple-element.36.q_ref, f32[1024,256]{1,0:T(8,128)S(1)} %copy-done, f32[512,512]{1,0:T(8,128)S(1)} %get-tuple-element.37.refs_0_.inner_ref, ...), custom_call_target="tpu_custom_call" | custom-call | flops 3000000000 | bytes 1000000 | tf_op jit(solution)/shard_map/finish/pallas_call | solution.py:364
  37.9 1.0 %collective-permute-start.11 = (bf16[256,512]{1,0:T(8,128)(2,1)S(1)}, bf16[256,512]{1,0:T(8,128)(2,1)S(1)}, u32[]{:S(2)}, u32[]{:S(2)}) collective-permute-start(bf16[256,512]{1,0:T(8,128)(2,1)S(1)} %get-tuple-element.51), channel_id=1, source_target_pairs={{0,2},{1,3},{2,0},{3,1},{4,6},{5,7},{6,4},{7,5},{8,10},{9,11},{10,... | collective-permute-start | bytes 786440 | tf_op jit(solution)/shard_map/ppermute | solution.py:520
  38.9 1.1 %collective-permute-start.12 = (bf16[256,512]{1,0:T(8,128)(2,1)S(1)}, bf16[256,512]{1,0:T(8,128)(2,1)S(1)}, u32[]{:S(2)}, u32[]{:S(2)}) collective-permute-start(bf16[256,512]{1,0:T(8,128)(2,1)S(1)} %get-tuple-element.38.refs_0_), channel_id=1, source_target_pairs={{0,3},{1,2},{2,1},{3,0},{4,7},{5,6},{6,5},{7,4},{8,11},{9,10},{10,... | collective-permute-start | bytes 786440 | tf_op jit(solution)/shard_map/ppermute | solution.py:520
  40.0 6.7 %inner_part.9 = (f32[512,1024]{1,0:T(8,128)S(1)}, bf16[512,1024]{1,0:T(8,128)(2,1)S(1)}) custom-call(s32[4]{0:T(128)S(1)} %pad_add_fusion.place_ref, bf16[1024,2048]{1,0:T(8,128)(2,1)} %q_source.13, bf16[1024,2048]{1,0:T(8,128)(2,1)} %k_source.13, bf16[1024,2048]{1,0:T(8,128)(2,1)} %v_source.13, f32[1024,256]{1,0:T(8,128)S(1)} %copy-done, ...), custom_call_target="tpu_custom_call" | custom-call | flops 3000000000 | bytes 1000000 | tf_op jit(solution)/shard_map/inner_part/pallas_call | solution.py:306
  46.7 4.2 %inner_part.10 = (f32[512,512]{1,0:T(8,128)S(1)}, bf16[512,512]{1,0:T(8,128)(2,1)S(1)}) custom-call(s32[4]{0:T(128)S(1)} %pad_add_fusion.place_ref, bf16[1024,2048]{1,0:T(8,128)(2,1)} %q_source.13, bf16[1024,2048]{1,0:T(8,128)(2,1)} %k_source.13, bf16[1024,2048]{1,0:T(8,128)(2,1)} %v_source.13, f32[1024,256]{1,0:T(8,128)S(1)} %copy-done, ...), custom_call_target="tpu_custom_call" | custom-call | flops 1024 | bytes 1024 | tf_op jit(solution)/shard_map/inner_part/pallas_call | solution.py:306
  50.9 1.8 %finish.9 = (bf16[256,512]{1,0:T(8,128)(2,1)S(1)}, bf16[256,512]{1,0:T(8,128)(2,1)S(1)}) custom-call(s32[4]{0:T(128)S(1)} %pad_add_fusion.place_ref, bf16[512,512]{1,0:T(8,128)(2,1)S(1)} %get-tuple-element.41.q_ref, f32[1024,256]{1,0:T(8,128)S(1)} %copy-done, f32[512,512]{1,0:T(8,128)S(1)} %get-tuple-element.42.inner_ref.refs_3_, ...), custom_call_target="tpu_custom_call" | custom-call | flops 1024 | bytes 1024 | tf_op jit(solution)/shard_map/finish/pallas_call | solution.py:364
  52.7 0.1 collective-permute-start.13
  52.8 3.0 %finish.10 = (bf16[256,1024]{1,0:T(8,128)(2,1)S(1)}, bf16[256,1024]{1,0:T(8,128)(2,1)S(1)}) custom-call(s32[4]{0:T(128)S(1)} %pad_add_fusion.place_ref, bf16[512,1024]{1,0:T(8,128)(2,1)S(1)} %get-tuple-element.39.q_ref, f32[1024,256]{1,0:T(8,128)S(1)} %copy-done, f32[512,1024]{1,0:T(8,128)S(1)} %get-tuple-element.40.refs_0_.inner_ref, ...), custom_call_target="tpu_custom_call" | custom-call | flops 3000000000 | bytes 1000000 | tf_op jit(solution)/shard_map/finish/pallas_call | solution.py:364
  55.9 1.0 %collective-permute-start.14 = (bf16[256,1024]{1,0:T(8,128)(2,1)S(1)}, bf16[256,1024]{1,0:T(8,128)(2,1)S(1)}, u32[]{:S(2)}, u32[]{:S(2)}) collective-permute-start(bf16[256,1024]{1,0:T(8,128)(2,1)S(1)} %get-tuple-element.57), channel_id=1, source_target_pairs={{0,2},{1,3},{2,0},{3,1},{4,6},{5,7},{6,4},{7,5},{8,10},{9,11},{10,... | collective-permute-start | bytes 1572872 | tf_op jit(solution)/shard_map/ppermute | solution.py:520
  56.9 1.2 %collective-permute-start.15 = (bf16[256,1024]{1,0:T(8,128)(2,1)S(1)}, bf16[256,1024]{1,0:T(8,128)(2,1)S(1)}, u32[]{:S(2)}, u32[]{:S(2)}) collective-permute-start(bf16[256,1024]{1,0:T(8,128)(2,1)S(1)} %get-tuple-element.45.refs_0_), channel_id=1, source_target_pairs={{0,3},{1,2},{2,1},{3,0},{4,7},{5,6},{6,5},{7,4},{8,11},{9,10},{10,... | collective-permute-start | bytes 1572872 | tf_op jit(solution)/shard_map/ppermute | solution.py:520
  58.1 4.2 %inner_part.11 = (f32[512,512]{1,0:T(8,128)S(1)}, bf16[512,512]{1,0:T(8,128)(2,1)S(1)}) custom-call(s32[4]{0:T(128)S(1)} %pad_add_fusion.place_ref, bf16[1024,2048]{1,0:T(8,128)(2,1)} %q_source.13, bf16[1024,2048]{1,0:T(8,128)(2,1)} %k_source.13, bf16[1024,2048]{1,0:T(8,128)(2,1)} %v_source.13, f32[1024,256]{1,0:T(8,128)S(1)} %copy-done, ...), custom_call_target="tpu_custom_call" | custom-call | flops 1024 | bytes 1024 | tf_op jit(solution)/shard_map/inner_part/pallas_call | solution.py:306
  62.3 1.8 %finish.11 = (bf16[256,512]{1,0:T(8,128)(2,1)S(1)}, bf16[256,512]{1,0:T(8,128)(2,1)S(1)}) custom-call(s32[4]{0:T(128)S(1)} %pad_add_fusion.place_ref, bf16[512,512]{1,0:T(8,128)(2,1)S(1)} %get-tuple-element.46.q_ref, f32[1024,256]{1,0:T(8,128)S(1)} %copy-done, f32[512,512]{1,0:T(8,128)S(1)} %get-tuple-element.47.inner_ref.refs_3_, ...), custom_call_target="tpu_custom_call" | custom-call | flops 1024 | bytes 1024 | tf_op jit(solution)/shard_map/finish/pallas_call | solution.py:364
  64.1 4.2 %inner_part.12 = (f32[512,512]{1,0:T(8,128)S(1)}, bf16[512,512]{1,0:T(8,128)(2,1)S(1)}) custom-call(s32[4]{0:T(128)S(1)} %pad_add_fusion.place_ref, bf16[1024,2048]{1,0:T(8,128)(2,1)} %q_source.13, bf16[1024,2048]{1,0:T(8,128)(2,1)} %k_source.13, bf16[1024,2048]{1,0:T(8,128)(2,1)} %v_source.13, f32[1024,256]{1,0:T(8,128)S(1)} %copy-done, ...), custom_call_target="tpu_custom_call" | custom-call | flops 1024 | bytes 1024 | tf_op jit(solution)/shard_map/inner_part/pallas_call | solution.py:306
  68.3 0.1 collective-permute-start.16
  68.4 1.8 %finish.12 = (bf16[256,512]{1,0:T(8,128)(2,1)S(1)}, bf16[256,512]{1,0:T(8,128)(2,1)S(1)}) custom-call(s32[4]{0:T(128)S(1)} %pad_add_fusion.place_ref, bf16[512,512]{1,0:T(8,128)(2,1)S(1)} %get-tuple-element.49.q_ref, f32[1024,256]{1,0:T(8,128)S(1)} %copy-done, f32[512,512]{1,0:T(8,128)S(1)} %get-tuple-element.50.inner_ref.refs_3_, ...), custom_call_target="tpu_custom_call" | custom-call | flops 1024 | bytes 1024 | tf_op jit(solution)/shard_map/finish/pallas_call | solution.py:364
  70.2 0.6 collective-permute-start.17
  70.7 4.2 %inner_part.13 = (f32[512,512]{1,0:T(8,128)S(1)}, bf16[512,512]{1,0:T(8,128)(2,1)S(1)}) custom-call(s32[4]{0:T(128)S(1)} %pad_add_fusion.place_ref, bf16[1024,2048]{1,0:T(8,128)(2,1)} %q_source.13, bf16[1024,2048]{1,0:T(8,128)(2,1)} %k_source.13, bf16[1024,2048]{1,0:T(8,128)(2,1)} %v_source.13, f32[1024,256]{1,0:T(8,128)S(1)} %copy-done, ...), custom_call_target="tpu_custom_call" | custom-call | flops 1024 | bytes 1024 | tf_op jit(solution)/shard_map/inner_part/pallas_call | solution.py:306
  74.9 0.0 copy-start.1
  75.0 0.0 copy-start.2
  75.0 1.8 %finish.13 = (bf16[256,512]{1,0:T(8,128)(2,1)S(1)}, bf16[256,512]{1,0:T(8,128)(2,1)S(1)}) custom-call(s32[4]{0:T(128)S(1)} %pad_add_fusion.place_ref, bf16[512,512]{1,0:T(8,128)(2,1)S(1)} %get-tuple-element.53.q_ref, f32[1024,256]{1,0:T(8,128)S(1)} %copy-done, f32[512,512]{1,0:T(8,128)S(1)} %get-tuple-element.54.inner_ref.refs_3_, ...), custom_call_target="tpu_custom_call" | custom-call | flops 1024 | bytes 1024 | tf_op jit(solution)/shard_map/finish/pallas_call | solution.py:364
  76.8 0.1 collective-permute-start.18
  76.9 0.3 copy-done.1
  77.1 1.7 %gating.1.gating_ref = f32[256,8192]{1,0:T(8,128)S(1)} custom-call(f32[1,8192]{1,0:T(1,128)S(1)} %bitcast.5, bf16[256,8192]{1,0:T(8,128)(2,1)S(1)} %copy-done.1, bf16[256,512]{1,0:T(8,128)(2,1)S(1)} %get-tuple-element.55.refs_0_), custom_call_target="tpu_custom_call" | custom-call | flops 1024 | bytes 1024 | tf_op jit(solution)/shard_map/gating/pallas_call | solution.py:395
  78.9 2.0 %collective-permute-done.15.refs_7_ = bf16[256,1024]{1,0:T(8,128)(2,1)S(1)} collective-permute-done((bf16[256,1024]{1,0:T(8,128)(2,1)S(1)}, bf16[256,1024]{1,0:T(8,128)(2,1)S(1)}, u32[]{:S(2)}, u32[]{:S(2)}) %collective-permute-start.15) | collective-permute-done | bytes 524320 | tf_op jit(solution)/shard_map/ppermute | solution.py:520
  80.8 4.2 %normalize.1 = bf16[256,8192]{1,0:T(8,128)(2,1)} custom-call(s32[4]{0:T(128)S(1)} %pad_add_fusion.place_ref, f32[256,8192]{1,0:T(8,128)S(1)} %gating.1.gating_ref, bf16[256,512]{1,0:T(8,128)(2,1)S(1)} %collective-permute-done.9.refs_4_.refs_0_, bf16[256,512]{1,0:T(8,128)(2,1)S(1)} %collective-permute-done.10.refs_5_.refs_1_, ...), custom_call_target="tpu_custom_call" | custom-call | flops 3000000000 | bytes 1000000 | tf_op jit(solution)/shard_map/normalize/pallas_call | solution.py:427
  (22 shorter events, 0.2 us)
Async XLA Ops:
  1.9 5.3 %collective-permute-start.1 = (bf16[4,128,128]{2,1,0:T(8,128)(2,1)S(1)}, bf16[4,128,128]{2,1,0:T(8,128)(2,1)S(1)}, u32[]{:S(2)}, u32[]{:S(2)}) collective-permute-start(bf16[4,128,128]{2,1,0:T(8,128)(2,1)S(1)} %block_states.3.refs_0_.total_ref), channel_id=1, source_target_pairs={{0,4},{4,0},{8,12},{12,8},{16,20},{20,16},{24,28},{28,24},{1,5},{5... | collective-permute-start | bytes 393224 | tf_op jit(solution)/shard_map/ppermute | solution.py:468
  6.0 9.2 %collective-permute-start = (bf16[4,128,128]{2,1,0:T(8,128)(2,1)S(1)}, bf16[4,128,128]{2,1,0:T(8,128)(2,1)S(1)}, u32[]{:S(2)}, u32[]{:S(2)}) collective-permute-start(bf16[4,128,128]{2,1,0:T(8,128)(2,1)S(1)} %block_states.4.refs_0_.total_ref), channel_id=1, source_target_pairs={{0,4},{4,0},{8,12},{12,8},{16,20},{20,16},{24,28},{28,24},{1,5},{5... | collective-permute-start | bytes 393224 | tf_op jit(solution)/shard_map/ppermute | solution.py:468
  7.3 5.5 %collective-permute-start.2 = (bf16[4,128,128]{2,1,0:T(8,128)(2,1)S(1)}, bf16[4,128,128]{2,1,0:T(8,128)(2,1)S(1)}, u32[]{:S(2)}, u32[]{:S(2)}) collective-permute-start(bf16[4,128,128]{2,1,0:T(8,128)(2,1)S(1)} %add_states.6.refs_0_.total_ref), channel_id=1, source_target_pairs={{0,8},{4,12},{8,0},{12,4},{16,24},{20,28},{24,16},{28,20},{1,9},{5... | collective-permute-start | bytes 393224 | tf_op jit(solution)/shard_map/ppermute | solution.py:468
  11.5 8.2 %collective-permute-start.5 = (bf16[8,128,128]{2,1,0:T(8,128)(2,1)S(1)}, bf16[8,128,128]{2,1,0:T(8,128)(2,1)S(1)}, u32[]{:S(2)}, u32[]{:S(2)}) collective-permute-start(bf16[8,128,128]{2,1,0:T(8,128)(2,1)S(1)} %block_states.5.refs_0_.total_ref), channel_id=1, source_target_pairs={{0,4},{4,0},{8,12},{12,8},{16,20},{20,16},{24,28},{28,24},{1,5},{5... | collective-permute-start | bytes 786440 | tf_op jit(solution)/shard_map/ppermute | solution.py:468
  12.8 2.7 %copy-start = (f32[1024,256]{1,0:T(8,128)S(1)}, f32[1024,256]{1,0:T(8,128)}, u32[]{:S(2)}) copy-start(f32[1024,256]{1,0:T(8,128)} %w_ref.27) | copy-start | bytes 3145732
  12.8 8.3 %collective-permute-start.4 = (bf16[4,128,128]{2,1,0:T(8,128)(2,1)S(1)}, bf16[4,128,128]{2,1,0:T(8,128)(2,1)S(1)}, u32[]{:S(2)}, u32[]{:S(2)}) collective-permute-start(bf16[4,128,128]{2,1,0:T(8,128)(2,1)S(1)} %add_states.7.refs_0_), channel_id=1, source_target_pairs={{0,16},{4,20},{8,24},{12,28},{16,0},{20,4},{24,8},{28,12},{1,17},{... | collective-permute-start | bytes 393224 | tf_op jit(solution)/shard_map/ppermute | solution.py:468
  15.3 12.3 %collective-permute-start.3 = (bf16[4,128,128]{2,1,0:T(8,128)(2,1)S(1)}, bf16[4,128,128]{2,1,0:T(8,128)(2,1)S(1)}, u32[]{:S(2)}, u32[]{:S(2)}) collective-permute-start(bf16[4,128,128]{2,1,0:T(8,128)(2,1)S(1)} %add_states.8.refs_0_.total_ref), channel_id=1, source_target_pairs={{0,8},{4,12},{8,0},{12,4},{16,24},{20,28},{24,16},{28,20},{1,9},{5... | collective-permute-start | bytes 393224 | tf_op jit(solution)/shard_map/ppermute | solution.py:468
  19.8 12.4 %collective-permute-start.7 = (bf16[8,128,128]{2,1,0:T(8,128)(2,1)S(1)}, bf16[8,128,128]{2,1,0:T(8,128)(2,1)S(1)}, u32[]{:S(2)}, u32[]{:S(2)}) collective-permute-start(bf16[8,128,128]{2,1,0:T(8,128)(2,1)S(1)} %add_states.9.refs_3_.total_ref), channel_id=1, source_target_pairs={{0,8},{4,12},{8,0},{12,4},{16,24},{20,28},{24,16},{28,20},{1,9},{5... | collective-permute-start | bytes 786440 | tf_op jit(solution)/shard_map/ppermute | solution.py:468
  22.9 29.9 %collective-permute-start.10 = (bf16[256,512]{1,0:T(8,128)(2,1)S(1)}, bf16[256,512]{1,0:T(8,128)(2,1)S(1)}, u32[]{:S(2)}, u32[]{:S(2)}) collective-permute-start(bf16[256,512]{1,0:T(8,128)(2,1)S(1)} %get-tuple-element.35.refs_0_), channel_id=1, source_target_pairs={{0,3},{1,2},{2,1},{3,0},{4,7},{5,6},{6,5},{7,4},{8,11},{9,10},{10,... | collective-permute-start | bytes 786440 | tf_op jit(solution)/shard_map/ppermute | solution.py:520
  27.6 8.5 %collective-permute-start.6 = (bf16[4,128,128]{2,1,0:T(8,128)(2,1)S(1)}, bf16[4,128,128]{2,1,0:T(8,128)(2,1)S(1)}, u32[]{:S(2)}, u32[]{:S(2)}) collective-permute-start(bf16[4,128,128]{2,1,0:T(8,128)(2,1)S(1)} %add_states.10.refs_0_), channel_id=1, source_target_pairs={{0,16},{4,20},{8,24},{12,28},{16,0},{20,4},{24,8},{28,12},{1,17},{... | collective-permute-start | bytes 393224 | tf_op jit(solution)/shard_map/ppermute | solution.py:468
  27.8 25.0 %collective-permute-start.9 = (bf16[256,512]{1,0:T(8,128)(2,1)S(1)}, bf16[256,512]{1,0:T(8,128)(2,1)S(1)}, u32[]{:S(2)}, u32[]{:S(2)}) collective-permute-start(bf16[256,512]{1,0:T(8,128)(2,1)S(1)} %get-tuple-element.44), channel_id=1, source_target_pairs={{0,2},{1,3},{2,0},{3,1},{4,6},{5,7},{6,4},{7,5},{8,10},{9,11},{10,... | collective-permute-start | bytes 786440 | tf_op jit(solution)/shard_map/ppermute | solution.py:520
  32.3 20.5 %collective-permute-start.8 = (bf16[8,128,128]{2,1,0:T(8,128)(2,1)S(1)}, bf16[8,128,128]{2,1,0:T(8,128)(2,1)S(1)}, u32[]{:S(2)}, u32[]{:S(2)}) collective-permute-start(bf16[8,128,128]{2,1,0:T(8,128)(2,1)S(1)} %add_states.11.refs_3_), channel_id=1, source_target_pairs={{0,16},{4,20},{8,24},{12,28},{16,0},{20,4},{24,8},{28,12},{1,17},{... | collective-permute-start | bytes 786440 | tf_op jit(solution)/shard_map/ppermute | solution.py:468
  37.9 30.4 %collective-permute-start.11 = (bf16[256,512]{1,0:T(8,128)(2,1)S(1)}, bf16[256,512]{1,0:T(8,128)(2,1)S(1)}, u32[]{:S(2)}, u32[]{:S(2)}) collective-permute-start(bf16[256,512]{1,0:T(8,128)(2,1)S(1)} %get-tuple-element.51), channel_id=1, source_target_pairs={{0,2},{1,3},{2,0},{3,1},{4,6},{5,7},{6,4},{7,5},{8,10},{9,11},{10,... | collective-permute-start | bytes 786440 | tf_op jit(solution)/shard_map/ppermute | solution.py:520
  38.9 29.5 %collective-permute-start.12 = (bf16[256,512]{1,0:T(8,128)(2,1)S(1)}, bf16[256,512]{1,0:T(8,128)(2,1)S(1)}, u32[]{:S(2)}, u32[]{:S(2)}) collective-permute-start(bf16[256,512]{1,0:T(8,128)(2,1)S(1)} %get-tuple-element.38.refs_0_), channel_id=1, source_target_pairs={{0,3},{1,2},{2,1},{3,0},{4,7},{5,6},{6,5},{7,4},{8,11},{9,10},{10,... | collective-permute-start | bytes 786440 | tf_op jit(solution)/shard_map/ppermute | solution.py:520
  52.7 24.0 %collective-permute-start.13 = (bf16[256,512]{1,0:T(8,128)(2,1)S(1)}, bf16[256,512]{1,0:T(8,128)(2,1)S(1)}, u32[]{:S(2)}, u32[]{:S(2)}) collective-permute-start(bf16[256,512]{1,0:T(8,128)(2,1)S(1)} %get-tuple-element.43.refs_3_), channel_id=1, source_target_pairs={{0,1},{1,0},{2,3},{3,2},{4,5},{5,4},{6,7},{7,6},{8,9},{9,8},{10,11... | collective-permute-start | bytes 786440 | tf_op jit(solution)/shard_map/ppermute | solution.py:520
  55.9 23.0 %collective-permute-start.14 = (bf16[256,1024]{1,0:T(8,128)(2,1)S(1)}, bf16[256,1024]{1,0:T(8,128)(2,1)S(1)}, u32[]{:S(2)}, u32[]{:S(2)}) collective-permute-start(bf16[256,1024]{1,0:T(8,128)(2,1)S(1)} %get-tuple-element.57), channel_id=1, source_target_pairs={{0,2},{1,3},{2,0},{3,1},{4,6},{5,7},{6,4},{7,5},{8,10},{9,11},{10,... | collective-permute-start | bytes 1572872 | tf_op jit(solution)/shard_map/ppermute | solution.py:520
  56.9 24.0 %collective-permute-start.15 = (bf16[256,1024]{1,0:T(8,128)(2,1)S(1)}, bf16[256,1024]{1,0:T(8,128)(2,1)S(1)}, u32[]{:S(2)}, u32[]{:S(2)}) collective-permute-start(bf16[256,1024]{1,0:T(8,128)(2,1)S(1)} %get-tuple-element.45.refs_0_), channel_id=1, source_target_pairs={{0,3},{1,2},{2,1},{3,0},{4,7},{5,6},{6,5},{7,4},{8,11},{9,10},{10,... | collective-permute-start | bytes 1572872 | tf_op jit(solution)/shard_map/ppermute | solution.py:520
  68.3 10.5 %collective-permute-start.16 = (bf16[256,512]{1,0:T(8,128)(2,1)S(1)}, bf16[256,512]{1,0:T(8,128)(2,1)S(1)}, u32[]{:S(2)}, u32[]{:S(2)}) collective-permute-start(bf16[256,512]{1,0:T(8,128)(2,1)S(1)} %get-tuple-element.48.refs_0_), channel_id=1, source_target_pairs={{0,1},{1,0},{2,3},{3,2},{4,5},{5,4},{6,7},{7,6},{8,9},{9,8},{10,11... | collective-permute-start | bytes 786440 | tf_op jit(solution)/shard_map/ppermute | solution.py:520
  70.2 8.7 %collective-permute-start.17 = (bf16[256,512]{1,0:T(8,128)(2,1)S(1)}, bf16[256,512]{1,0:T(8,128)(2,1)S(1)}, u32[]{:S(2)}, u32[]{:S(2)}) collective-permute-start(bf16[256,512]{1,0:T(8,128)(2,1)S(1)} %get-tuple-element.52.refs_0_), channel_id=1, source_target_pairs={{0,1},{1,0},{2,3},{3,2},{4,5},{5,4},{6,7},{7,6},{8,9},{9,8},{10,11... | collective-permute-start | bytes 786440 | tf_op jit(solution)/shard_map/ppermute | solution.py:520
  74.9 2.2 %copy-start.1 = (bf16[256,8192]{1,0:T(8,128)(2,1)S(1)}, bf16[256,8192]{1,0:T(8,128)(2,1)}, u32[]{:S(2)}) copy-start(bf16[256,8192]{1,0:T(8,128)(2,1)} %gate_ref.1) | copy-start | bytes 12582916
  75.0 2.2 %copy-start.2 = (f32[8192]{0:T(1024)S(1)}, f32[8192]{0:T(1024)}, u32[]{:S(2)}) copy-start(f32[8192]{0:T(1024)} %param.11) | copy-start | bytes 98308
  76.8 2.1 %collective-permute-start.18 = (bf16[256,512]{1,0:T(8,128)(2,1)S(1)}, bf16[256,512]{1,0:T(8,128)(2,1)S(1)}, u32[]{:S(2)}, u32[]{:S(2)}) collective-permute-start(bf16[256,512]{1,0:T(8,128)(2,1)S(1)} %get-tuple-element.55.refs_0_), channel_id=1, source_target_pairs={{0,1},{1,0},{2,3},{3,2},{4,5},{5,4},{6,7},{7,6},{8,9},{9,8},{10,11... | collective-permute-start | bytes 786440 | tf_op jit(solution)/shard_map/ppermute | solution.py:520

commit v3 on v2

--- a/solution.py
+++ b/solution.py
@@ -27,13 +27,13 @@
     ("A", 2),
     ("F", 0),
     ("A", 1),
-    ("I", 1),
+    ("W", 1),
     ("A", 2),
     ("F", 1),
     ("I", 2),
+    ("N", 1),
+    ("F", 2),
     ("N", 0),
-    ("F", 2),
-    ("N", 1),
     ("N", 2),
 )
 TINY = pl.CostEstimate(flops=1024, bytes_accessed=1024, transcendentals=0)
@@ -325,7 +325,9 @@
     )(place, in_hbm(queries), in_hbm(keys), in_hbm(values), weights, *after)
 
 
-def finish_kernel(first, start, heads, pairs, levels, place_ref, q_ref, w_ref, inner_ref, *refs):
+def finish_kernel(
+    first, start, heads, pairs, held, shift, levels, place_ref, q_ref, w_ref, inner_ref, *refs
+):
     tiers = refs[:levels]
     outs = refs[len(refs) - 2 * len(pairs) :]
     local_bits = w_ref.shape[0].bit_length() - 1
@@ -342,28 +344,41 @@
             weights = pltpu.roll(w_ref[here, pl.ds(lane, LANES)], (LANES - base) % LANES, 1)
             for i in range(GROUP):
                 cols = pl.ds(pl.multiple_of((step * GROUP + i) * HEAD_DIM, HEAD_DIM), HEAD_DIM)
-                own = slice(2 * n * rows, 2 * (n + 1) * rows)
-                q = q_ref[own, cols]
-                total = inner_ref[own, cols]
+                spot_held = held.index(pair)
+                own = slice(2 * spot_held * rows, 2 * (spot_held + 1) * rows)
+                source = (shift + step * GROUP + i) * HEAD_DIM
+                source = pl.ds(pl.multiple_of(source, HEAD_DIM), HEAD_DIM)
+                q = q_ref[own, source]
+                total = inner_ref[own, source]
                 for m in range(levels):
                     level = i * LEVELS + local_bits + 1 + m
-                    held = place_ref[1 + m].astype(jnp.float32)
+                    upper = place_ref[1 + m].astype(jnp.float32)
                     tier = tiers[m][start + step * GROUP + i]
-                    total += (weights[:, level : level + 1] * held) * dot(q, tier)
-                upper, lower = total[:rows], total[rows:]
-                outs[2 * n][:, cols] = jnp.where(flip, lower, upper).astype(jnp.bfloat16)
-                outs[2 * n + 1][:, cols] = jnp.where(flip, upper, lower).astype(jnp.bfloat16)
+                    total += (weights[:, level : level + 1] * upper) * dot(q, tier)
+                top, bottom = total[:rows], total[rows:]
+                outs[2 * n][:, cols] = jnp.where(flip, bottom, top).astype(jnp.bfloat16)
+                outs[2 * n + 1][:, cols] = jnp.where(flip, top, bottom).astype(jnp.bfloat16)
         return carry
 
     lax.fori_loop(0, heads // GROUP, group, 0)
 
 
-def finish(place, tiers, queries, inner, weights, chunk_first, start, heads, pairs, parts, after):
+def finish(
+    place, tiers, inner, weights, chunk_first, start, heads, pairs, parts, after
+):
+    total, queries, held, begin = inner
     rows = weights.shape[0] // parts
     outs = 2 * len(pairs)
     return pl.pallas_call(
         functools.partial(
-            finish_kernel, chunk_first + start, start, heads, tuple(pairs), len(tiers)
+            finish_kernel,
+            chunk_first + start,
+            start,
+            heads,
+            tuple(pairs),
+            held,
+            start - begin,
+            len(tiers),
         ),
         in_specs=[pl.BlockSpec(memory_space=pltpu.SMEM)]
         + [local()] * (3 + len(tiers))
@@ -375,7 +390,7 @@
         compiler_params=params(8),
         cost_estimate=cost(pairs),
         name="finish",
-    )(place, queries, weights, inner, *tiers, *after)
+    )(place, queries, weights, total, *tiers, *after)
 
 
 def gate_kernel(gain_ref, gate_ref, *refs):
@@ -482,7 +497,7 @@
             hop(g)
 
     def inner_step(g, pairs, start, size):
-        inner[g] = inner_part(
+        total, held = inner_part(
             place,
             queries,
             key_vectors,
@@ -495,17 +510,16 @@
             parts,
             tuple(last.values()),
         )
-        last["kernel"] = inner[g][0]
+        inner[g] = total, held, tuple(pairs), start
+        last["kernel"] = total
 
     def finish_step(g, pairs, start, size):
-        part, q_part = inner[g]
         behind = g - 2 if pairs[0] else g - 1 if g == len(sizes) - 1 else -1
         before = tuple(arrived.get(behind, ()))
         outs = finish(
             place,
             tiers[g],
-            q_part,
-            part,
+            inner[g],
             level_weight,
             firsts[g],
             start,
@@ -523,7 +537,7 @@
             if pairs[0]:
                 arrived.setdefault(g, []).append(out)
 
-    far, near = range(1, parts // 2), range(1)
+    far, near = list(range(1, parts // 2)), [0]
     for kind, g in ORDER:
         if g >= len(sizes):
             continue
@@ -533,14 +547,17 @@
             add_step(g)
         if kind == "I":
             inner_step(g, far, 0, sizes[g])
+        if kind == "W":
+            inner_step(g, far + near, 0, sizes[g])
         if kind == "F":
             for _ in range(seq_bits):
                 add_step(g)
             finish_step(g, far, 0, sizes[g])
         if kind == "N":
+            if 0 not in inner[g][2]:
+                inner_step(g, near, 0, sizes[g])
             for start in range(0, sizes[g], SIZES[0]):
                 size = min(SIZES[0], sizes[g] - start)
-                inner_step(g, near, start, size)
                 finish_step(g, near, start, size)
     gated = gating(norm_gain, gate_values, tuple(last.values()))
     return normalize(place, gated, layout, pieces, width)

time: 85.3 us -> 81.8 us (0.959)
  Pallas kernels: 58.6 us -> 54.6 us
    pallas_call x7 -> x5, Pallas kernels: 31.9 us -> 27.9 us  [inner_part(): pl.pallas_call(functools.partial(inner_kernel, first, heads, tuple(pairs)...]
    ppermute x10, waiting for transfers between devices: 1.98 us -> 3.95 us  [finish_step(): out = lax.ppermute(out, 'head', [(i, i ^ step) for i in range(parts)])]
    ppermute x9, waiting for transfers between devices: 2.61 us -> 1.14 us  [hop(): tiers[g].append(lax.ppermute(sends[g], 'seq', pairs))]
  transfers between devices with their start and end apart: 19 -> 19, of which waited for: 3 -> 2; matrix products, arithmetic and copies ran while one was open for 0% -> 0% of each run, Pallas kernels for 62% -> 59%
where the time goes in v3:
time: 81.8 us; the launch traced here: 81.6 us
  Pallas kernels  54.6 us (67%)
  starting transfers between devices  21.5 us (26%)
  waiting for transfers between devices  5.09 us (6%)
    pallas_call x5, Pallas kernels, inner_part(): pl.pallas_call(functools.partial(inner_kernel, first, heads, tuple(pairs)...  27.9 us
    pallas_call x7, Pallas kernels, finish(): pl.pallas_call(functools.partial(finish_kernel, chunk_first + start, star...  13.8 us
    ppermute x9, starting transfers between devices, hop(): tiers[g].append(lax.ppermute(sends[g], 'seq', pairs))  11.2 us
    ppermute x10, starting transfers between devices, finish_step(): out = lax.ppermute(out, 'head', [(i, i ^ step) for i in range(parts)])  10.3 us
    pallas_call x3, Pallas kernels, block_states(): pl.pallas_call(functools.partial(state_kernel, first, heads), in_specs=[h...  6.77 us
    pallas_call x1, Pallas kernels, normalize(): pl.pallas_call(functools.partial(norm_kernel, layout, width), grid=(rows...  4.17 us
    ppermute x10, waiting for transfers between devices, finish_step(): out = lax.ppermute(out, 'head', [(i, i ^ step) for i in range(parts)])  3.95 us
    pallas_call x1, Pallas kernels, gating(): pl.pallas_call(gate_kernel, in_specs=[local()] * 2 + [anywhere() for _ in...  1.69 us
  transfers between devices with their start and end apart: 19, of which 2 were waited for; matrix products, arithmetic and copies ran while one was open for 0% of the time, Pallas kernels for 59%

profile of v3, /device:TPU:1, one launch (start us, length us, event | category | flops | bytes accessed | tf_op | source)
XLA Modules:
  0.0 81.6 jit_solution(11044819930386492871)
XLA Ops:
  0.0 1.9 %block_states.3.refs_0_.total_ref = bf16[4,128,128]{2,1,0:T(8,128)(2,1)S(1)} custom-call(bf16[1024,2048]{1,0:T(8,128)(2,1)} %k_source.9, bf16[1024,2048]{1,0:T(8,128)(2,1)} %v_source.9), custom_call_target="tpu_custom_call" | custom-call | flops 3000000000 | bytes 1000000 | tf_op jit(solution)/shard_map/block_states/pallas_call | solution.py:104
  1.9 2.1 %collective-permute-start.1 = (bf16[4,128,128]{2,1,0:T(8,128)(2,1)S(1)}, bf16[4,128,128]{2,1,0:T(8,128)(2,1)S(1)}, u32[]{:S(2)}, u32[]{:S(2)}) collective-permute-start(bf16[4,128,128]{2,1,0:T(8,128)(2,1)S(1)} %block_states.3.refs_0_.total_ref), channel_id=1, source_target_pairs={{0,4},{4,0},{8,12},{12,8},{16,20},{20,16},{24,28},{28,24},{1,5},{5... | collective-permute-start | bytes 393224 | tf_op jit(solution)/shard_map/ppermute | solution.py:483
  4.0 1.9 %block_states.4.refs_0_.total_ref = bf16[4,128,128]{2,1,0:T(8,128)(2,1)S(1)} custom-call(bf16[1024,2048]{1,0:T(8,128)(2,1)} %k_source.9, bf16[1024,2048]{1,0:T(8,128)(2,1)} %v_source.9, bf16[4,128,128]{2,1,0:T(8,128)(2,1)S(1)} %block_states.3.refs_0_.total_ref), custom_call_target="tpu_custom_call" | custom-call | flops 3000000000 | bytes 1000000 | tf_op jit(solution)/shard_map/block_states/pallas_call | solution.py:104
  6.0 0.1 collective-permute-start
  6.1 0.1 pad_add_fusion.place_ref
  6.1 1.1 %collective-permute-done.1.held_ref.refs_0_ = bf16[4,128,128]{2,1,0:T(8,128)(2,1)S(1)} collective-permute-done((bf16[4,128,128]{2,1,0:T(8,128)(2,1)S(1)}, bf16[4,128,128]{2,1,0:T(8,128)(2,1)S(1)}, u32[]{:S(2)}, u32[]{:S(2)}) %collective-permute-start.1) | collective-permute-done | bytes 131104 | tf_op jit(solution)/shard_map/ppermute | solution.py:483
  7.3 1.3 %collective-permute-start.2 = (bf16[4,128,128]{2,1,0:T(8,128)(2,1)S(1)}, bf16[4,128,128]{2,1,0:T(8,128)(2,1)S(1)}, u32[]{:S(2)}, u32[]{:S(2)}) collective-permute-start(bf16[4,128,128]{2,1,0:T(8,128)(2,1)S(1)} %add_states.6.refs_0_.total_ref), channel_id=1, source_target_pairs={{0,8},{4,12},{8,0},{12,4},{16,24},{20,28},{24,16},{28,20},{1,9},{5... | collective-permute-start | bytes 393224 | tf_op jit(solution)/shard_map/ppermute | solution.py:483
  8.6 2.9 %block_states.5.refs_0_.total_ref = bf16[8,128,128]{2,1,0:T(8,128)(2,1)S(1)} custom-call(bf16[1024,2048]{1,0:T(8,128)(2,1)} %k_source.9, bf16[1024,2048]{1,0:T(8,128)(2,1)} %v_source.9, bf16[4,128,128]{2,1,0:T(8,128)(2,1)S(1)} %add_states.6.refs_0_.total_ref), custom_call_target="tpu_custom_call" | custom-call | flops 3000000000 | bytes 1000000 | tf_op jit(solution)/shard_map/block_states/pallas_call | solution.py:104
  11.5 1.3 %collective-permute-start.5 = (bf16[8,128,128]{2,1,0:T(8,128)(2,1)S(1)}, bf16[8,128,128]{2,1,0:T(8,128)(2,1)S(1)}, u32[]{:S(2)}, u32[]{:S(2)}) collective-permute-start(bf16[8,128,128]{2,1,0:T(8,128)(2,1)S(1)} %block_states.5.refs_0_.total_ref), channel_id=1, source_target_pairs={{0,4},{4,0},{8,12},{12,8},{16,20},{20,16},{24,28},{28,24},{1,5},{5... | collective-permute-start | bytes 786440 | tf_op jit(solution)/shard_map/ppermute | solution.py:483
  12.8 0.0 copy-start
  12.8 2.4 %collective-permute-start.4 = (bf16[4,128,128]{2,1,0:T(8,128)(2,1)S(1)}, bf16[4,128,128]{2,1,0:T(8,128)(2,1)S(1)}, u32[]{:S(2)}, u32[]{:S(2)}) collective-permute-start(bf16[4,128,128]{2,1,0:T(8,128)(2,1)S(1)} %add_states.7.refs_0_), channel_id=1, source_target_pairs={{0,16},{4,20},{8,24},{12,28},{16,0},{20,4},{24,8},{28,12},{1,17},{... | collective-permute-start | bytes 393224 | tf_op jit(solution)/shard_map/ppermute | solution.py:483
  15.2 0.0 collective-permute-done.held_ref.refs_0_
  15.3 0.2 collective-permute-start.3
  15.5 4.2 %inner_part.5 = (f32[512,512]{1,0:T(8,128)S(1)}, bf16[512,512]{1,0:T(8,128)(2,1)S(1)}) custom-call(s32[4]{0:T(128)S(1)} %pad_add_fusion.place_ref, bf16[1024,2048]{1,0:T(8,128)(2,1)} %q_source.9, bf16[1024,2048]{1,0:T(8,128)(2,1)} %k_source.9, bf16[1024,2048]{1,0:T(8,128)(2,1)} %v_source.9, f32[1024,256]{1,0:T(8,128)S(1)} %copy-done, ...), custom_call_target="tpu_custom_call" | custom-call | flops 3000000000 | bytes 1000000 | tf_op jit(solution)/shard_map/inner_part/pallas_call | solution.py:306
  19.7 0.0 collective-permute-done.5.held_ref.refs_0_
  19.7 0.1 add_states.9.refs_3_.total_ref
  19.8 1.4 %collective-permute-start.7 = (bf16[8,128,128]{2,1,0:T(8,128)(2,1)S(1)}, bf16[8,128,128]{2,1,0:T(8,128)(2,1)S(1)}, u32[]{:S(2)}, u32[]{:S(2)}) collective-permute-start(bf16[8,128,128]{2,1,0:T(8,128)(2,1)S(1)} %add_states.9.refs_3_.total_ref), channel_id=1, source_target_pairs={{0,8},{4,12},{8,0},{12,4},{16,24},{20,28},{24,16},{28,20},{1,9},{5... | collective-permute-start | bytes 786440 | tf_op jit(solution)/shard_map/ppermute | solution.py:483
  21.2 1.8 %finish.7 = (bf16[256,512]{1,0:T(8,128)(2,1)S(1)}, bf16[256,512]{1,0:T(8,128)(2,1)S(1)}) custom-call(s32[4]{0:T(128)S(1)} %pad_add_fusion.place_ref, bf16[512,512]{1,0:T(8,128)(2,1)S(1)} %get-tuple-element.29.q_ref, f32[1024,256]{1,0:T(8,128)S(1)} %copy-done, f32[512,512]{1,0:T(8,128)S(1)} %get-tuple-element.30.refs_0_.inner_ref, ...), custom_call_target="tpu_custom_call" | custom-call | flops 3000000000 | bytes 1000000 | tf_op jit(solution)/shard_map/finish/pallas_call | solution.py:372
  22.9 4.7 %collective-permute-start.10 = (bf16[256,512]{1,0:T(8,128)(2,1)S(1)}, bf16[256,512]{1,0:T(8,128)(2,1)S(1)}, u32[]{:S(2)}, u32[]{:S(2)}) collective-permute-start(bf16[256,512]{1,0:T(8,128)(2,1)S(1)} %get-tuple-element.31.refs_0_), channel_id=1, source_target_pairs={{0,3},{1,2},{2,1},{3,0},{4,7},{5,6},{6,5},{7,4},{8,11},{9,10},{10,... | collective-permute-start | bytes 786440 | tf_op jit(solution)/shard_map/ppermute | solution.py:534
  27.6 0.0 collective-permute-done.3.held_ref.refs_1_
  27.6 0.1 collective-permute-start.6
  27.8 0.2 collective-permute-start.9
  28.0 6.1 %inner_part.6 = (f32[1024,512]{1,0:T(8,128)S(1)}, bf16[1024,512]{1,0:T(8,128)(2,1)S(1)}) custom-call(s32[4]{0:T(128)S(1)} %pad_add_fusion.place_ref, bf16[1024,2048]{1,0:T(8,128)(2,1)} %q_source.9, bf16[1024,2048]{1,0:T(8,128)(2,1)} %k_source.9, bf16[1024,2048]{1,0:T(8,128)(2,1)} %v_source.9, f32[1024,256]{1,0:T(8,128)S(1)} %copy-done, ...), custom_call_target="tpu_custom_call" | custom-call | flops 3000000000 | bytes 1000000 | tf_op jit(solution)/shard_map/inner_part/pallas_call | solution.py:306
  34.1 0.0 collective-permute-done.7.held_ref.refs_1_
  34.1 0.1 add_states.11.refs_3_
  34.2 2.4 %collective-permute-start.8 = (bf16[8,128,128]{2,1,0:T(8,128)(2,1)S(1)}, bf16[8,128,128]{2,1,0:T(8,128)(2,1)S(1)}, u32[]{:S(2)}, u32[]{:S(2)}) collective-permute-start(bf16[8,128,128]{2,1,0:T(8,128)(2,1)S(1)} %add_states.11.refs_3_), channel_id=1, source_target_pairs={{0,16},{4,20},{8,24},{12,28},{16,0},{20,4},{24,8},{28,12},{1,17},{... | collective-permute-start | bytes 786440 | tf_op jit(solution)/shard_map/ppermute | solution.py:483
  36.5 1.8 %finish.8 = (bf16[256,512]{1,0:T(8,128)(2,1)S(1)}, bf16[256,512]{1,0:T(8,128)(2,1)S(1)}) custom-call(s32[4]{0:T(128)S(1)} %pad_add_fusion.place_ref, bf16[1024,512]{1,0:T(8,128)(2,1)S(1)} %get-tuple-element.32.q_ref, f32[1024,256]{1,0:T(8,128)S(1)} %copy-done, f32[1024,512]{1,0:T(8,128)S(1)} %get-tuple-element.33.refs_0_.inner_ref, ...), custom_call_target="tpu_custom_call" | custom-call | flops 3000000000 | bytes 1000000 | tf_op jit(solution)/shard_map/finish/pallas_call | solution.py:372
  38.4 1.3 %collective-permute-start.11 = (bf16[256,512]{1,0:T(8,128)(2,1)S(1)}, bf16[256,512]{1,0:T(8,128)(2,1)S(1)}, u32[]{:S(2)}, u32[]{:S(2)}) collective-permute-start(bf16[256,512]{1,0:T(8,128)(2,1)S(1)} %get-tuple-element.45), channel_id=1, source_target_pairs={{0,2},{1,3},{2,0},{3,1},{4,6},{5,7},{6,4},{7,5},{8,10},{9,11},{10,... | collective-permute-start | bytes 786440 | tf_op jit(solution)/shard_map/ppermute | solution.py:534
  39.7 1.1 %collective-permute-start.12 = (bf16[256,512]{1,0:T(8,128)(2,1)S(1)}, bf16[256,512]{1,0:T(8,128)(2,1)S(1)}, u32[]{:S(2)}, u32[]{:S(2)}) collective-permute-start(bf16[256,512]{1,0:T(8,128)(2,1)S(1)} %get-tuple-element.34.refs_0_), channel_id=1, source_target_pairs={{0,3},{1,2},{2,1},{3,0},{4,7},{5,6},{6,5},{7,4},{8,11},{9,10},{10,... | collective-permute-start | bytes 786440 | tf_op jit(solution)/shard_map/ppermute | solution.py:534
  40.8 6.7 %inner_part.7 = (f32[512,1024]{1,0:T(8,128)S(1)}, bf16[512,1024]{1,0:T(8,128)(2,1)S(1)}) custom-call(s32[4]{0:T(128)S(1)} %pad_add_fusion.place_ref, bf16[1024,2048]{1,0:T(8,128)(2,1)} %q_source.9, bf16[1024,2048]{1,0:T(8,128)(2,1)} %k_source.9, bf16[1024,2048]{1,0:T(8,128)(2,1)} %v_source.9, f32[1024,256]{1,0:T(8,128)S(1)} %copy-done, ...), custom_call_target="tpu_custom_call" | custom-call | flops 3000000000 | bytes 1000000 | tf_op jit(solution)/shard_map/inner_part/pallas_call | solution.py:306
  47.5 1.8 %finish.9 = (bf16[256,512]{1,0:T(8,128)(2,1)S(1)}, bf16[256,512]{1,0:T(8,128)(2,1)S(1)}) custom-call(s32[4]{0:T(128)S(1)} %pad_add_fusion.place_ref, bf16[1024,512]{1,0:T(8,128)(2,1)S(1)} %get-tuple-element.32.q_ref, f32[1024,256]{1,0:T(8,128)S(1)} %copy-done, f32[1024,512]{1,0:T(8,128)S(1)} %get-tuple-element.33.refs_0_.inner_ref, ...), custom_call_target="tpu_custom_call" | custom-call | flops 1024 | bytes 1024 | tf_op jit(solution)/shard_map/finish/pallas_call | solution.py:372
  49.3 0.1 collective-permute-start.13
  49.4 3.0 %finish.10 = (bf16[256,1024]{1,0:T(8,128)(2,1)S(1)}, bf16[256,1024]{1,0:T(8,128)(2,1)S(1)}) custom-call(s32[4]{0:T(128)S(1)} %pad_add_fusion.place_ref, bf16[512,1024]{1,0:T(8,128)(2,1)S(1)} %get-tuple-element.35.q_ref, f32[1024,256]{1,0:T(8,128)S(1)} %copy-done, f32[512,1024]{1,0:T(8,128)S(1)} %get-tuple-element.36.refs_3_.inner_ref, ...), custom_call_target="tpu_custom_call" | custom-call | flops 3000000000 | bytes 1000000 | tf_op jit(solution)/shard_map/finish/pallas_call | solution.py:372
  52.5 0.7 collective-permute-start.14
  53.2 1.4 %collective-permute-start.15 = (bf16[256,1024]{1,0:T(8,128)(2,1)S(1)}, bf16[256,1024]{1,0:T(8,128)(2,1)S(1)}, u32[]{:S(2)}, u32[]{:S(2)}) collective-permute-start(bf16[256,1024]{1,0:T(8,128)(2,1)S(1)} %get-tuple-element.39.refs_0_), channel_id=1, source_target_pairs={{0,3},{1,2},{2,1},{3,0},{4,7},{5,6},{6,5},{7,4},{8,11},{9,10},{10,... | collective-permute-start | bytes 1572872 | tf_op jit(solution)/shard_map/ppermute | solution.py:534
  54.6 4.2 %inner_part.8 = (f32[512,512]{1,0:T(8,128)S(1)}, bf16[512,512]{1,0:T(8,128)(2,1)S(1)}) custom-call(s32[4]{0:T(128)S(1)} %pad_add_fusion.place_ref, bf16[1024,2048]{1,0:T(8,128)(2,1)} %q_source.9, bf16[1024,2048]{1,0:T(8,128)(2,1)} %k_source.9, bf16[1024,2048]{1,0:T(8,128)(2,1)} %v_source.9, f32[1024,256]{1,0:T(8,128)S(1)} %copy-done, ...), custom_call_target="tpu_custom_call" | custom-call | flops 1024 | bytes 1024 | tf_op jit(solution)/shard_map/inner_part/pallas_call | solution.py:306
  58.9 1.8 %finish.11 = (bf16[256,512]{1,0:T(8,128)(2,1)S(1)}, bf16[256,512]{1,0:T(8,128)(2,1)S(1)}) custom-call(s32[4]{0:T(128)S(1)} %pad_add_fusion.place_ref, bf16[512,512]{1,0:T(8,128)(2,1)S(1)} %get-tuple-element.40.q_ref, f32[1024,256]{1,0:T(8,128)S(1)} %copy-done, f32[512,512]{1,0:T(8,128)S(1)} %get-tuple-element.41.inner_ref.refs_3_, ...), custom_call_target="tpu_custom_call" | custom-call | flops 1024 | bytes 1024 | tf_op jit(solution)/shard_map/finish/pallas_call | solution.py:372
  60.6 6.7 %inner_part.9 = (f32[512,1024]{1,0:T(8,128)S(1)}, bf16[512,1024]{1,0:T(8,128)(2,1)S(1)}) custom-call(s32[4]{0:T(128)S(1)} %pad_add_fusion.place_ref, bf16[1024,2048]{1,0:T(8,128)(2,1)} %q_source.9, bf16[1024,2048]{1,0:T(8,128)(2,1)} %k_source.9, bf16[1024,2048]{1,0:T(8,128)(2,1)} %v_source.9, f32[1024,256]{1,0:T(8,128)S(1)} %copy-done, ...), custom_call_target="tpu_custom_call" | custom-call | flops 1024 | bytes 1024 | tf_op jit(solution)/shard_map/inner_part/pallas_call | solution.py:306
  67.4 0.1 collective-permute-start.16
  67.5 1.8 %finish.12 = (bf16[256,512]{1,0:T(8,128)(2,1)S(1)}, bf16[256,512]{1,0:T(8,128)(2,1)S(1)}) custom-call(s32[4]{0:T(128)S(1)} %pad_add_fusion.place_ref, bf16[512,1024]{1,0:T(8,128)(2,1)S(1)} %get-tuple-element.43.q_ref, f32[1024,256]{1,0:T(8,128)S(1)} %copy-done, f32[512,1024]{1,0:T(8,128)S(1)} %get-tuple-element.44.inner_ref.refs_3_, ...), custom_call_target="tpu_custom_call" | custom-call | flops 1024 | bytes 1024 | tf_op jit(solution)/shard_map/finish/pallas_call | solution.py:372
  69.3 0.0 copy-start.1
  69.3 0.0 copy-start.2
  69.3 1.8 %finish.13 = (bf16[256,512]{1,0:T(8,128)(2,1)S(1)}, bf16[256,512]{1,0:T(8,128)(2,1)S(1)}) custom-call(s32[4]{0:T(128)S(1)} %pad_add_fusion.place_ref, bf16[512,1024]{1,0:T(8,128)(2,1)S(1)} %get-tuple-element.43.q_ref, f32[1024,256]{1,0:T(8,128)S(1)} %copy-done, f32[512,1024]{1,0:T(8,128)S(1)} %get-tuple-element.44.inner_ref.refs_3_, ...), custom_call_target="tpu_custom_call" | custom-call | flops 1024 | bytes 1024 | tf_op jit(solution)/shard_map/finish/pallas_call | solution.py:372
  71.1 0.6 collective-permute-start.18
  71.7 0.1 collective-permute-start.17
  71.8 1.7 %gating.1.gating_ref = f32[256,8192]{1,0:T(8,128)S(1)} custom-call(f32[1,8192]{1,0:T(1,128)S(1)} %bitcast.5, bf16[256,8192]{1,0:T(8,128)(2,1)S(1)} %copy-done.1, bf16[256,512]{1,0:T(8,128)(2,1)S(1)} %get-tuple-element.47.refs_0_), custom_call_target="tpu_custom_call" | custom-call | flops 1024 | bytes 1024 | tf_op jit(solution)/shard_map/gating/pallas_call | solution.py:410
  73.5 3.9 %collective-permute-done.15.refs_7_ = bf16[256,1024]{1,0:T(8,128)(2,1)S(1)} collective-permute-done((bf16[256,1024]{1,0:T(8,128)(2,1)S(1)}, bf16[256,1024]{1,0:T(8,128)(2,1)S(1)}, u32[]{:S(2)}, u32[]{:S(2)}) %collective-permute-start.15) | collective-permute-done | bytes 524320 | tf_op jit(solution)/shard_map/ppermute | solution.py:534
  77.4 4.2 %normalize.1 = bf16[256,8192]{1,0:T(8,128)(2,1)} custom-call(s32[4]{0:T(128)S(1)} %pad_add_fusion.place_ref, f32[256,8192]{1,0:T(8,128)S(1)} %gating.1.gating_ref, bf16[256,512]{1,0:T(8,128)(2,1)S(1)} %collective-permute-done.9.refs_4_.refs_0_, bf16[256,512]{1,0:T(8,128)(2,1)S(1)} %collective-permute-done.10.refs_5_.refs_1_, ...), custom_call_target="tpu_custom_call" | custom-call | flops 3000000000 | bytes 1000000 | tf_op jit(solution)/shard_map/normalize/pallas_call | solution.py:442
  (20 shorter events, 0.2 us)
Async XLA Ops:
  1.9 5.3 %collective-permute-start.1 = (bf16[4,128,128]{2,1,0:T(8,128)(2,1)S(1)}, bf16[4,128,128]{2,1,0:T(8,128)(2,1)S(1)}, u32[]{:S(2)}, u32[]{:S(2)}) collective-permute-start(bf16[4,128,128]{2,1,0:T(8,128)(2,1)S(1)} %block_states.3.refs_0_.total_ref), channel_id=1, source_target_pairs={{0,4},{4,0},{8,12},{12,8},{16,20},{20,16},{24,28},{28,24},{1,5},{5... | collective-permute-start | bytes 393224 | tf_op jit(solution)/shard_map/ppermute | solution.py:483
  6.0 9.2 %collective-permute-start = (bf16[4,128,128]{2,1,0:T(8,128)(2,1)S(1)}, bf16[4,128,128]{2,1,0:T(8,128)(2,1)S(1)}, u32[]{:S(2)}, u32[]{:S(2)}) collective-permute-start(bf16[4,128,128]{2,1,0:T(8,128)(2,1)S(1)} %block_states.4.refs_0_.total_ref), channel_id=1, source_target_pairs={{0,4},{4,0},{8,12},{12,8},{16,20},{20,16},{24,28},{28,24},{1,5},{5... | collective-permute-start | bytes 393224 | tf_op jit(solution)/shard_map/ppermute | solution.py:483
  7.3 5.5 %collective-permute-start.2 = (bf16[4,128,128]{2,1,0:T(8,128)(2,1)S(1)}, bf16[4,128,128]{2,1,0:T(8,128)(2,1)S(1)}, u32[]{:S(2)}, u32[]{:S(2)}) collective-permute-start(bf16[4,128,128]{2,1,0:T(8,128)(2,1)S(1)} %add_states.6.refs_0_.total_ref), channel_id=1, source_target_pairs={{0,8},{4,12},{8,0},{12,4},{16,24},{20,28},{24,16},{28,20},{1,9},{5... | collective-permute-start | bytes 393224 | tf_op jit(solution)/shard_map/ppermute | solution.py:483
  11.5 8.2 %collective-permute-start.5 = (bf16[8,128,128]{2,1,0:T(8,128)(2,1)S(1)}, bf16[8,128,128]{2,1,0:T(8,128)(2,1)S(1)}, u32[]{:S(2)}, u32[]{:S(2)}) collective-permute-start(bf16[8,128,128]{2,1,0:T(8,128)(2,1)S(1)} %block_states.5.refs_0_.total_ref), channel_id=1, source_target_pairs={{0,4},{4,0},{8,12},{12,8},{16,20},{20,16},{24,28},{28,24},{1,5},{5... | collective-permute-start | bytes 786440 | tf_op jit(solution)/shard_map/ppermute | solution.py:483
  12.8 2.7 %copy-start = (f32[1024,256]{1,0:T(8,128)S(1)}, f32[1024,256]{1,0:T(8,128)}, u32[]{:S(2)}) copy-start(f32[1024,256]{1,0:T(8,128)} %w_ref.23) | copy-start | bytes 3145732
  12.8 8.3 %collective-permute-start.4 = (bf16[4,128,128]{2,1,0:T(8,128)(2,1)S(1)}, bf16[4,128,128]{2,1,0:T(8,128)(2,1)S(1)}, u32[]{:S(2)}, u32[]{:S(2)}) collective-permute-start(bf16[4,128,128]{2,1,0:T(8,128)(2,1)S(1)} %add_states.7.refs_0_), channel_id=1, source_target_pairs={{0,16},{4,20},{8,24},{12,28},{16,0},{20,4},{24,8},{28,12},{1,17},{... | collective-permute-start | bytes 393224 | tf_op jit(solution)/shard_map/ppermute | solution.py:483
  15.3 12.3 %collective-permute-start.3 = (bf16[4,128,128]{2,1,0:T(8,128)(2,1)S(1)}, bf16[4,128,128]{2,1,0:T(8,128)(2,1)S(1)}, u32[]{:S(2)}, u32[]{:S(2)}) collective-permute-start(bf16[4,128,128]{2,1,0:T(8,128)(2,1)S(1)} %add_states.8.refs_0_.total_ref), channel_id=1, source_target_pairs={{0,8},{4,12},{8,0},{12,4},{16,24},{20,28},{24,16},{28,20},{1,9},{5... | collective-permute-start | bytes 393224 | tf_op jit(solution)/shard_map/ppermute | solution.py:483
  19.8 14.3 %collective-permute-start.7 = (bf16[8,128,128]{2,1,0:T(8,128)(2,1)S(1)}, bf16[8,128,128]{2,1,0:T(8,128)(2,1)S(1)}, u32[]{:S(2)}, u32[]{:S(2)}) collective-permute-start(bf16[8,128,128]{2,1,0:T(8,128)(2,1)S(1)} %add_states.9.refs_3_.total_ref), channel_id=1, source_target_pairs={{0,8},{4,12},{8,0},{12,4},{16,24},{20,28},{24,16},{28,20},{1,9},{5... | collective-permute-start | bytes 786440 | tf_op jit(solution)/shard_map/ppermute | solution.py:483
  22.9 26.5 %collective-permute-start.10 = (bf16[256,512]{1,0:T(8,128)(2,1)S(1)}, bf16[256,512]{1,0:T(8,128)(2,1)S(1)}, u32[]{:S(2)}, u32[]{:S(2)}) collective-permute-start(bf16[256,512]{1,0:T(8,128)(2,1)S(1)} %get-tuple-element.31.refs_0_), channel_id=1, source_target_pairs={{0,3},{1,2},{2,1},{3,0},{4,7},{5,6},{6,5},{7,4},{8,11},{9,10},{10,... | collective-permute-start | bytes 786440 | tf_op jit(solution)/shard_map/ppermute | solution.py:534
  27.6 8.9 %collective-permute-start.6 = (bf16[4,128,128]{2,1,0:T(8,128)(2,1)S(1)}, bf16[4,128,128]{2,1,0:T(8,128)(2,1)S(1)}, u32[]{:S(2)}, u32[]{:S(2)}) collective-permute-start(bf16[4,128,128]{2,1,0:T(8,128)(2,1)S(1)} %add_states.10.refs_0_), channel_id=1, source_target_pairs={{0,16},{4,20},{8,24},{12,28},{16,0},{20,4},{24,8},{28,12},{1,17},{... | collective-permute-start | bytes 393224 | tf_op jit(solution)/shard_map/ppermute | solution.py:483
  27.8 21.6 %collective-permute-start.9 = (bf16[256,512]{1,0:T(8,128)(2,1)S(1)}, bf16[256,512]{1,0:T(8,128)(2,1)S(1)}, u32[]{:S(2)}, u32[]{:S(2)}) collective-permute-start(bf16[256,512]{1,0:T(8,128)(2,1)S(1)} %get-tuple-element.38), channel_id=1, source_target_pairs={{0,2},{1,3},{2,0},{3,1},{4,6},{5,7},{6,4},{7,5},{8,10},{9,11},{10,... | collective-permute-start | bytes 786440 | tf_op jit(solution)/shard_map/ppermute | solution.py:534
  34.2 15.2 %collective-permute-start.8 = (bf16[8,128,128]{2,1,0:T(8,128)(2,1)S(1)}, bf16[8,128,128]{2,1,0:T(8,128)(2,1)S(1)}, u32[]{:S(2)}, u32[]{:S(2)}) collective-permute-start(bf16[8,128,128]{2,1,0:T(8,128)(2,1)S(1)} %add_states.11.refs_3_), channel_id=1, source_target_pairs={{0,16},{4,20},{8,24},{12,28},{16,0},{20,4},{24,8},{28,12},{1,17},{... | collective-permute-start | bytes 786440 | tf_op jit(solution)/shard_map/ppermute | solution.py:483
  38.4 29.0 %collective-permute-start.11 = (bf16[256,512]{1,0:T(8,128)(2,1)S(1)}, bf16[256,512]{1,0:T(8,128)(2,1)S(1)}, u32[]{:S(2)}, u32[]{:S(2)}) collective-permute-start(bf16[256,512]{1,0:T(8,128)(2,1)S(1)} %get-tuple-element.45), channel_id=1, source_target_pairs={{0,2},{1,3},{2,0},{3,1},{4,6},{5,7},{6,4},{7,5},{8,10},{9,11},{10,... | collective-permute-start | bytes 786440 | tf_op jit(solution)/shard_map/ppermute | solution.py:534
  39.7 27.8 %collective-permute-start.12 = (bf16[256,512]{1,0:T(8,128)(2,1)S(1)}, bf16[256,512]{1,0:T(8,128)(2,1)S(1)}, u32[]{:S(2)}, u32[]{:S(2)}) collective-permute-start(bf16[256,512]{1,0:T(8,128)(2,1)S(1)} %get-tuple-element.34.refs_0_), channel_id=1, source_target_pairs={{0,3},{1,2},{2,1},{3,0},{4,7},{5,6},{6,5},{7,4},{8,11},{9,10},{10,... | collective-permute-start | bytes 786440 | tf_op jit(solution)/shard_map/ppermute | solution.py:534
  49.3 22.3 %collective-permute-start.13 = (bf16[256,512]{1,0:T(8,128)(2,1)S(1)}, bf16[256,512]{1,0:T(8,128)(2,1)S(1)}, u32[]{:S(2)}, u32[]{:S(2)}) collective-permute-start(bf16[256,512]{1,0:T(8,128)(2,1)S(1)} %get-tuple-element.37.refs_3_), channel_id=1, source_target_pairs={{0,1},{1,0},{2,3},{3,2},{4,5},{5,4},{6,7},{7,6},{8,9},{9,8},{10,11... | collective-permute-start | bytes 786440 | tf_op jit(solution)/shard_map/ppermute | solution.py:534
  52.5 21.0 %collective-permute-start.14 = (bf16[256,1024]{1,0:T(8,128)(2,1)S(1)}, bf16[256,1024]{1,0:T(8,128)(2,1)S(1)}, u32[]{:S(2)}, u32[]{:S(2)}) collective-permute-start(bf16[256,1024]{1,0:T(8,128)(2,1)S(1)} %get-tuple-element.49), channel_id=1, source_target_pairs={{0,2},{1,3},{2,0},{3,1},{4,6},{5,7},{6,4},{7,5},{8,10},{9,11},{10,... | collective-permute-start | bytes 1572872 | tf_op jit(solution)/shard_map/ppermute | solution.py:534
  53.2 24.2 %collective-permute-start.15 = (bf16[256,1024]{1,0:T(8,128)(2,1)S(1)}, bf16[256,1024]{1,0:T(8,128)(2,1)S(1)}, u32[]{:S(2)}, u32[]{:S(2)}) collective-permute-start(bf16[256,1024]{1,0:T(8,128)(2,1)S(1)} %get-tuple-element.39.refs_0_), channel_id=1, source_target_pairs={{0,3},{1,2},{2,1},{3,0},{4,7},{5,6},{6,5},{7,4},{8,11},{9,10},{10,... | collective-permute-start | bytes 1572872 | tf_op jit(solution)/shard_map/ppermute | solution.py:534
  67.4 6.1 %collective-permute-start.16 = (bf16[256,512]{1,0:T(8,128)(2,1)S(1)}, bf16[256,512]{1,0:T(8,128)(2,1)S(1)}, u32[]{:S(2)}, u32[]{:S(2)}) collective-permute-start(bf16[256,512]{1,0:T(8,128)(2,1)S(1)} %get-tuple-element.42.refs_0_), channel_id=1, source_target_pairs={{0,1},{1,0},{2,3},{3,2},{4,5},{5,4},{6,7},{7,6},{8,9},{9,8},{10,11... | collective-permute-start | bytes 786440 | tf_op jit(solution)/shard_map/ppermute | solution.py:534
  69.3 2.5 %copy-start.1 = (bf16[256,8192]{1,0:T(8,128)(2,1)S(1)}, bf16[256,8192]{1,0:T(8,128)(2,1)}, u32[]{:S(2)}) copy-start(bf16[256,8192]{1,0:T(8,128)(2,1)} %gate_ref.1) | copy-start | bytes 12582916
  69.3 2.5 %copy-start.2 = (f32[8192]{0:T(1024)S(1)}, f32[8192]{0:T(1024)}, u32[]{:S(2)}) copy-start(f32[8192]{0:T(1024)} %param.11) | copy-start | bytes 98308
  71.1 2.4 %collective-permute-start.18 = (bf16[256,512]{1,0:T(8,128)(2,1)S(1)}, bf16[256,512]{1,0:T(8,128)(2,1)S(1)}, u32[]{:S(2)}, u32[]{:S(2)}) collective-permute-start(bf16[256,512]{1,0:T(8,128)(2,1)S(1)} %get-tuple-element.47.refs_0_), channel_id=1, source_target_pairs={{0,1},{1,0},{2,3},{3,2},{4,5},{5,4},{6,7},{7,6},{8,9},{9,8},{10,11... | collective-permute-start | bytes 786440 | tf_op jit(solution)/shard_map/ppermute | solution.py:534
  71.7 1.8 %collective-permute-start.17 = (bf16[256,512]{1,0:T(8,128)(2,1)S(1)}, bf16[256,512]{1,0:T(8,128)(2,1)S(1)}, u32[]{:S(2)}, u32[]{:S(2)}) collective-permute-start(bf16[256,512]{1,0:T(8,128)(2,1)S(1)} %get-tuple-element.46.refs_3_), channel_id=1, source_target_pairs={{0,1},{1,0},{2,3},{3,2},{4,5},{5,4},{6,7},{7,6},{8,9},{9,8},{10,11... | collective-permute-start | bytes 786440 | tf_op jit(solution)/shard_map/ppermute | solution.py:534

commit v4 on v3

--- a/solution.py
+++ b/solution.py
@@ -24,9 +24,9 @@
     ("A", 0),
     ("A", 1),
     ("I", 0),
-    ("A", 2),
     ("F", 0),
     ("A", 1),
+    ("A", 2),
     ("W", 1),
     ("A", 2),
     ("F", 1),

time: 81.8 us -> 84.2 us (1.029)
  waiting for transfers between devices: 5.09 us -> 7.76 us
    ppermute x9, waiting for transfers between devices: 1.14 us -> 4.25 us  [hop(): tiers[g].append(lax.ppermute(sends[g], 'seq', pairs))]
  transfers between devices with their start and end apart: 19 -> 19, of which waited for: 2 -> 4; matrix products, arithmetic and copies ran while one was open for 0% -> 0% of each run, Pallas kernels for 59% -> 58%
where the time goes in v4:
time: 84.2 us; the launch traced here: 84 us
  Pallas kernels  54.6 us (65%)
  starting transfers between devices  21.3 us (25%)
  waiting for transfers between devices  7.76 us (9%)
    pallas_call x5, Pallas kernels, inner_part(): pl.pallas_call(functools.partial(inner_kernel, first, heads, tuple(pairs)...  27.9 us
    pallas_call x7, Pallas kernels, finish(): pl.pallas_call(functools.partial(finish_kernel, chunk_first + start, star...  13.8 us
    ppermute x9, starting transfers between devices, hop(): tiers[g].append(lax.ppermute(sends[g], 'seq', pairs))  11.3 us
    ppermute x10, starting transfers between devices, finish_step(): out = lax.ppermute(out, 'head', [(i, i ^ step) for i in range(parts)])  10 us
    pallas_call x3, Pallas kernels, block_states(): pl.pallas_call(functools.partial(state_kernel, first, heads), in_specs=[h...  6.78 us
    ppermute x9, waiting for transfers between devices, hop(): tiers[g].append(lax.ppermute(sends[g], 'seq', pairs))  4.25 us
    pallas_call x1, Pallas kernels, normalize(): pl.pallas_call(functools.partial(norm_kernel, layout, width), grid=(rows...  4.17 us
    ppermute x10, waiting for transfers between devices, finish_step(): out = lax.ppermute(out, 'head', [(i, i ^ step) for i in range(parts)])  3.51 us
  transfers between devices with their start and end apart: 19, of which 4 were waited for; matrix products, arithmetic and copies ran while one was open for 0% of the time, Pallas kernels for 58%

profile of v4, /device:TPU:1, one launch (start us, length us, event | category | flops | bytes accessed | tf_op | source)
XLA Modules:
  0.0 84.0 jit_solution(1895156867604617406)
XLA Ops:
  0.0 1.9 %block_states.3.refs_0_.total_ref = bf16[4,128,128]{2,1,0:T(8,128)(2,1)S(1)} custom-call(bf16[1024,2048]{1,0:T(8,128)(2,1)} %k_source.9, bf16[1024,2048]{1,0:T(8,128)(2,1)} %v_source.9), custom_call_target="tpu_custom_call" | custom-call | flops 3000000000 | bytes 1000000 | tf_op jit(solution)/shard_map/block_states/pallas_call | solution.py:104
  1.9 2.1 %collective-permute-start = (bf16[4,128,128]{2,1,0:T(8,128)(2,1)S(1)}, bf16[4,128,128]{2,1,0:T(8,128)(2,1)S(1)}, u32[]{:S(2)}, u32[]{:S(2)}) collective-permute-start(bf16[4,128,128]{2,1,0:T(8,128)(2,1)S(1)} %block_states.3.refs_0_.total_ref), channel_id=1, source_target_pairs={{0,4},{4,0},{8,12},{12,8},{16,20},{20,16},{24,28},{28,24},{1,5},{5... | collective-permute-start | bytes 393224 | tf_op jit(solution)/shard_map/ppermute | solution.py:483
  4.0 1.9 %block_states.4.refs_0_.total_ref = bf16[4,128,128]{2,1,0:T(8,128)(2,1)S(1)} custom-call(bf16[1024,2048]{1,0:T(8,128)(2,1)} %k_source.9, bf16[1024,2048]{1,0:T(8,128)(2,1)} %v_source.9, bf16[4,128,128]{2,1,0:T(8,128)(2,1)S(1)} %block_states.3.refs_0_.total_ref), custom_call_target="tpu_custom_call" | custom-call | flops 3000000000 | bytes 1000000 | tf_op jit(solution)/shard_map/block_states/pallas_call | solution.py:104
  6.0 0.1 collective-permute-start.2
  6.1 0.1 pad_add_fusion.place_ref
  6.1 1.1 %collective-permute-done.held_ref.refs_0_ = bf16[4,128,128]{2,1,0:T(8,128)(2,1)S(1)} collective-permute-done((bf16[4,128,128]{2,1,0:T(8,128)(2,1)S(1)}, bf16[4,128,128]{2,1,0:T(8,128)(2,1)S(1)}, u32[]{:S(2)}, u32[]{:S(2)}) %collective-permute-start) | collective-permute-done | bytes 131104 | tf_op jit(solution)/shard_map/ppermute | solution.py:483
  7.3 1.3 %collective-permute-start.3 = (bf16[4,128,128]{2,1,0:T(8,128)(2,1)S(1)}, bf16[4,128,128]{2,1,0:T(8,128)(2,1)S(1)}, u32[]{:S(2)}, u32[]{:S(2)}) collective-permute-start(bf16[4,128,128]{2,1,0:T(8,128)(2,1)S(1)} %add_states.6.refs_0_.total_ref), channel_id=1, source_target_pairs={{0,8},{4,12},{8,0},{12,4},{16,24},{20,28},{24,16},{28,20},{1,9},{5... | collective-permute-start | bytes 393224 | tf_op jit(solution)/shard_map/ppermute | solution.py:483
  8.6 2.9 %block_states.5.refs_0_.total_ref = bf16[8,128,128]{2,1,0:T(8,128)(2,1)S(1)} custom-call(bf16[1024,2048]{1,0:T(8,128)(2,1)} %k_source.9, bf16[1024,2048]{1,0:T(8,128)(2,1)} %v_source.9, bf16[4,128,128]{2,1,0:T(8,128)(2,1)S(1)} %add_states.6.refs_0_.total_ref), custom_call_target="tpu_custom_call" | custom-call | flops 3000000000 | bytes 1000000 | tf_op jit(solution)/shard_map/block_states/pallas_call | solution.py:104
  11.5 1.3 %collective-permute-start.1 = (bf16[8,128,128]{2,1,0:T(8,128)(2,1)S(1)}, bf16[8,128,128]{2,1,0:T(8,128)(2,1)S(1)}, u32[]{:S(2)}, u32[]{:S(2)}) collective-permute-start(bf16[8,128,128]{2,1,0:T(8,128)(2,1)S(1)} %block_states.5.refs_0_.total_ref), channel_id=1, source_target_pairs={{0,4},{4,0},{8,12},{12,8},{16,20},{20,16},{24,28},{28,24},{1,5},{5... | collective-permute-start | bytes 786440 | tf_op jit(solution)/shard_map/ppermute | solution.py:483
  12.8 0.0 collective-permute-done.3.held_ref.refs_1_
  12.8 0.0 copy-start
  12.8 2.4 %collective-permute-start.5 = (bf16[4,128,128]{2,1,0:T(8,128)(2,1)S(1)}, bf16[4,128,128]{2,1,0:T(8,128)(2,1)S(1)}, u32[]{:S(2)}, u32[]{:S(2)}) collective-permute-start(bf16[4,128,128]{2,1,0:T(8,128)(2,1)S(1)} %add_states.7.refs_0_), channel_id=1, source_target_pairs={{0,16},{4,20},{8,24},{12,28},{16,0},{20,4},{24,8},{28,12},{1,17},{... | collective-permute-start | bytes 393224 | tf_op jit(solution)/shard_map/ppermute | solution.py:483
  15.3 0.2 collective-permute-start.4
  15.5 4.2 %inner_part.5 = (f32[512,512]{1,0:T(8,128)S(1)}, bf16[512,512]{1,0:T(8,128)(2,1)S(1)}) custom-call(s32[4]{0:T(128)S(1)} %pad_add_fusion.place_ref, bf16[1024,2048]{1,0:T(8,128)(2,1)} %q_source.9, bf16[1024,2048]{1,0:T(8,128)(2,1)} %k_source.9, bf16[1024,2048]{1,0:T(8,128)(2,1)} %v_source.9, f32[1024,256]{1,0:T(8,128)S(1)} %copy-done, ...), custom_call_target="tpu_custom_call" | custom-call | flops 3000000000 | bytes 1000000 | tf_op jit(solution)/shard_map/inner_part/pallas_call | solution.py:306
  19.7 0.0 collective-permute-done.5.refs_2_
  19.7 1.8 %finish.7 = (bf16[256,512]{1,0:T(8,128)(2,1)S(1)}, bf16[256,512]{1,0:T(8,128)(2,1)S(1)}) custom-call(s32[4]{0:T(128)S(1)} %pad_add_fusion.place_ref, bf16[512,512]{1,0:T(8,128)(2,1)S(1)} %get-tuple-element.29.q_ref, f32[1024,256]{1,0:T(8,128)S(1)} %copy-done, f32[512,512]{1,0:T(8,128)S(1)} %get-tuple-element.30.inner_ref.refs_3_, ...), custom_call_target="tpu_custom_call" | custom-call | flops 3000000000 | bytes 1000000 | tf_op jit(solution)/shard_map/finish/pallas_call | solution.py:372
  21.5 4.4 %collective-permute-start.10 = (bf16[256,512]{1,0:T(8,128)(2,1)S(1)}, bf16[256,512]{1,0:T(8,128)(2,1)S(1)}, u32[]{:S(2)}, u32[]{:S(2)}) collective-permute-start(bf16[256,512]{1,0:T(8,128)(2,1)S(1)} %get-tuple-element.31.refs_0_), channel_id=1, source_target_pairs={{0,3},{1,2},{2,1},{3,0},{4,7},{5,6},{6,5},{7,4},{8,11},{9,10},{10,... | collective-permute-start | bytes 786440 | tf_op jit(solution)/shard_map/ppermute | solution.py:534
  25.9 1.0 %collective-permute-start.6 = (bf16[4,128,128]{2,1,0:T(8,128)(2,1)S(1)}, bf16[4,128,128]{2,1,0:T(8,128)(2,1)S(1)}, u32[]{:S(2)}, u32[]{:S(2)}) collective-permute-start(bf16[4,128,128]{2,1,0:T(8,128)(2,1)S(1)} %add_states.9.refs_0_), channel_id=1, source_target_pairs={{0,16},{4,20},{8,24},{12,28},{16,0},{20,4},{24,8},{28,12},{1,17},{... | collective-permute-start | bytes 393224 | tf_op jit(solution)/shard_map/ppermute | solution.py:483
  26.9 0.1 add_states.10.refs_0_.total_ref
  27.0 1.5 %collective-permute-start.7 = (bf16[8,128,128]{2,1,0:T(8,128)(2,1)S(1)}, bf16[8,128,128]{2,1,0:T(8,128)(2,1)S(1)}, u32[]{:S(2)}, u32[]{:S(2)}) collective-permute-start(bf16[8,128,128]{2,1,0:T(8,128)(2,1)S(1)} %add_states.10.refs_0_.total_ref), channel_id=1, source_target_pairs={{0,8},{4,12},{8,0},{12,4},{16,24},{20,28},{24,16},{28,20},{1,9},{5... | collective-permute-start | bytes 786440 | tf_op jit(solution)/shard_map/ppermute | solution.py:483
  28.5 0.3 collective-permute-start.9
  28.8 6.1 %inner_part.6 = (f32[1024,512]{1,0:T(8,128)S(1)}, bf16[1024,512]{1,0:T(8,128)(2,1)S(1)}) custom-call(s32[4]{0:T(128)S(1)} %pad_add_fusion.place_ref, bf16[1024,2048]{1,0:T(8,128)(2,1)} %q_source.9, bf16[1024,2048]{1,0:T(8,128)(2,1)} %k_source.9, bf16[1024,2048]{1,0:T(8,128)(2,1)} %v_source.9, f32[1024,256]{1,0:T(8,128)S(1)} %copy-done, ...), custom_call_target="tpu_custom_call" | custom-call | flops 3000000000 | bytes 1000000 | tf_op jit(solution)/shard_map/inner_part/pallas_call | solution.py:306
  34.9 2.5 %collective-permute-done.7.held_ref.refs_1_ = bf16[8,128,128]{2,1,0:T(8,128)(2,1)S(1)} collective-permute-done((bf16[8,128,128]{2,1,0:T(8,128)(2,1)S(1)}, bf16[8,128,128]{2,1,0:T(8,128)(2,1)S(1)}, u32[]{:S(2)}, u32[]{:S(2)}) %collective-permute-start.7) | collective-permute-done | bytes 262176 | tf_op jit(solution)/shard_map/ppermute | solution.py:483
  37.4 0.1 add_states.11.refs_3_
  37.5 1.4 %collective-permute-start.8 = (bf16[8,128,128]{2,1,0:T(8,128)(2,1)S(1)}, bf16[8,128,128]{2,1,0:T(8,128)(2,1)S(1)}, u32[]{:S(2)}, u32[]{:S(2)}) collective-permute-start(bf16[8,128,128]{2,1,0:T(8,128)(2,1)S(1)} %add_states.11.refs_3_), channel_id=1, source_target_pairs={{0,16},{4,20},{8,24},{12,28},{16,0},{20,4},{24,8},{28,12},{1,17},{... | collective-permute-start | bytes 786440 | tf_op jit(solution)/shard_map/ppermute | solution.py:483
  38.9 1.8 %finish.8 = (bf16[256,512]{1,0:T(8,128)(2,1)S(1)}, bf16[256,512]{1,0:T(8,128)(2,1)S(1)}) custom-call(s32[4]{0:T(128)S(1)} %pad_add_fusion.place_ref, bf16[1024,512]{1,0:T(8,128)(2,1)S(1)} %get-tuple-element.32.q_ref, f32[1024,256]{1,0:T(8,128)S(1)} %copy-done, f32[1024,512]{1,0:T(8,128)S(1)} %get-tuple-element.33.refs_0_.inner_ref, ...), custom_call_target="tpu_custom_call" | custom-call | flops 3000000000 | bytes 1000000 | tf_op jit(solution)/shard_map/finish/pallas_call | solution.py:372
  40.7 0.6 collective-permute-start.11
  41.3 1.1 %collective-permute-start.12 = (bf16[256,512]{1,0:T(8,128)(2,1)S(1)}, bf16[256,512]{1,0:T(8,128)(2,1)S(1)}, u32[]{:S(2)}, u32[]{:S(2)}) collective-permute-start(bf16[256,512]{1,0:T(8,128)(2,1)S(1)} %get-tuple-element.34.refs_0_), channel_id=1, source_target_pairs={{0,3},{1,2},{2,1},{3,0},{4,7},{5,6},{6,5},{7,4},{8,11},{9,10},{10,... | collective-permute-start | bytes 786440 | tf_op jit(solution)/shard_map/ppermute | solution.py:534
  42.5 6.7 %inner_part.7 = (f32[512,1024]{1,0:T(8,128)S(1)}, bf16[512,1024]{1,0:T(8,128)(2,1)S(1)}) custom-call(s32[4]{0:T(128)S(1)} %pad_add_fusion.place_ref, bf16[1024,2048]{1,0:T(8,128)(2,1)} %q_source.9, bf16[1024,2048]{1,0:T(8,128)(2,1)} %k_source.9, bf16[1024,2048]{1,0:T(8,128)(2,1)} %v_source.9, f32[1024,256]{1,0:T(8,128)S(1)} %copy-done, ...), custom_call_target="tpu_custom_call" | custom-call | flops 3000000000 | bytes 1000000 | tf_op jit(solution)/shard_map/inner_part/pallas_call | solution.py:306
  49.2 1.8 %finish.9 = (bf16[256,512]{1,0:T(8,128)(2,1)S(1)}, bf16[256,512]{1,0:T(8,128)(2,1)S(1)}) custom-call(s32[4]{0:T(128)S(1)} %pad_add_fusion.place_ref, bf16[1024,512]{1,0:T(8,128)(2,1)S(1)} %get-tuple-element.32.q_ref, f32[1024,256]{1,0:T(8,128)S(1)} %copy-done, f32[1024,512]{1,0:T(8,128)S(1)} %get-tuple-element.33.refs_0_.inner_ref, ...), custom_call_target="tpu_custom_call" | custom-call | flops 1024 | bytes 1024 | tf_op jit(solution)/shard_map/finish/pallas_call | solution.py:372
  51.0 0.2 collective-permute-start.13
  51.2 0.6 collective-permute-done.8.refs_2_
  51.8 3.0 %finish.10 = (bf16[256,1024]{1,0:T(8,128)(2,1)S(1)}, bf16[256,1024]{1,0:T(8,128)(2,1)S(1)}) custom-call(s32[4]{0:T(128)S(1)} %pad_add_fusion.place_ref, bf16[512,1024]{1,0:T(8,128)(2,1)S(1)} %get-tuple-element.35.q_ref, f32[1024,256]{1,0:T(8,128)S(1)} %copy-done, f32[512,1024]{1,0:T(8,128)S(1)} %get-tuple-element.36.refs_3_.inner_ref, ...), custom_call_target="tpu_custom_call" | custom-call | flops 3000000000 | bytes 1000000 | tf_op jit(solution)/shard_map/finish/pallas_call | solution.py:372
  54.9 1.0 %collective-permute-start.14 = (bf16[256,1024]{1,0:T(8,128)(2,1)S(1)}, bf16[256,1024]{1,0:T(8,128)(2,1)S(1)}, u32[]{:S(2)}, u32[]{:S(2)}) collective-permute-start(bf16[256,1024]{1,0:T(8,128)(2,1)S(1)} %get-tuple-element.49), channel_id=1, source_target_pairs={{0,2},{1,3},{2,0},{3,1},{4,6},{5,7},{6,4},{7,5},{8,10},{9,11},{10,... | collective-permute-start | bytes 1572872 | tf_op jit(solution)/shard_map/ppermute | solution.py:534
  55.9 1.6 %collective-permute-start.15 = (bf16[256,1024]{1,0:T(8,128)(2,1)S(1)}, bf16[256,1024]{1,0:T(8,128)(2,1)S(1)}, u32[]{:S(2)}, u32[]{:S(2)}) collective-permute-start(bf16[256,1024]{1,0:T(8,128)(2,1)S(1)} %get-tuple-element.39.refs_0_), channel_id=1, source_target_pairs={{0,3},{1,2},{2,1},{3,0},{4,7},{5,6},{6,5},{7,4},{8,11},{9,10},{10,... | collective-permute-start | bytes 1572872 | tf_op jit(solution)/shard_map/ppermute | solution.py:534
  57.5 4.2 %inner_part.8 = (f32[512,512]{1,0:T(8,128)S(1)}, bf16[512,512]{1,0:T(8,128)(2,1)S(1)}) custom-call(s32[4]{0:T(128)S(1)} %pad_add_fusion.place_ref, bf16[1024,2048]{1,0:T(8,128)(2,1)} %q_source.9, bf16[1024,2048]{1,0:T(8,128)(2,1)} %k_source.9, bf16[1024,2048]{1,0:T(8,128)(2,1)} %v_source.9, f32[1024,256]{1,0:T(8,128)S(1)} %copy-done, ...), custom_call_target="tpu_custom_call" | custom-call | flops 1024 | bytes 1024 | tf_op jit(solution)/shard_map/inner_part/pallas_call | solution.py:306
  61.7 1.8 %finish.11 = (bf16[256,512]{1,0:T(8,128)(2,1)S(1)}, bf16[256,512]{1,0:T(8,128)(2,1)S(1)}) custom-call(s32[4]{0:T(128)S(1)} %pad_add_fusion.place_ref, bf16[512,512]{1,0:T(8,128)(2,1)S(1)} %get-tuple-element.40.q_ref, f32[1024,256]{1,0:T(8,128)S(1)} %copy-done, f32[512,512]{1,0:T(8,128)S(1)} %get-tuple-element.41.inner_ref.refs_3_, ...), custom_call_target="tpu_custom_call" | custom-call | flops 1024 | bytes 1024 | tf_op jit(solution)/shard_map/finish/pallas_call | solution.py:372
  63.5 6.7 %inner_part.9 = (f32[512,1024]{1,0:T(8,128)S(1)}, bf16[512,1024]{1,0:T(8,128)(2,1)S(1)}) custom-call(s32[4]{0:T(128)S(1)} %pad_add_fusion.place_ref, bf16[1024,2048]{1,0:T(8,128)(2,1)} %q_source.9, bf16[1024,2048]{1,0:T(8,128)(2,1)} %k_source.9, bf16[1024,2048]{1,0:T(8,128)(2,1)} %v_source.9, f32[1024,256]{1,0:T(8,128)S(1)} %copy-done, ...), custom_call_target="tpu_custom_call" | custom-call | flops 1024 | bytes 1024 | tf_op jit(solution)/shard_map/inner_part/pallas_call | solution.py:306
  70.2 0.1 collective-permute-start.16
  70.3 1.8 %finish.12 = (bf16[256,512]{1,0:T(8,128)(2,1)S(1)}, bf16[256,512]{1,0:T(8,128)(2,1)S(1)}) custom-call(s32[4]{0:T(128)S(1)} %pad_add_fusion.place_ref, bf16[512,1024]{1,0:T(8,128)(2,1)S(1)} %get-tuple-element.43.q_ref, f32[1024,256]{1,0:T(8,128)S(1)} %copy-done, f32[512,1024]{1,0:T(8,128)S(1)} %get-tuple-element.44.inner_ref.refs_3_, ...), custom_call_target="tpu_custom_call" | custom-call | flops 1024 | bytes 1024 | tf_op jit(solution)/shard_map/finish/pallas_call | solution.py:372
  72.1 0.0 copy-start.1
  72.1 0.0 copy-start.2
  72.1 1.8 %finish.13 = (bf16[256,512]{1,0:T(8,128)(2,1)S(1)}, bf16[256,512]{1,0:T(8,128)(2,1)S(1)}) custom-call(s32[4]{0:T(128)S(1)} %pad_add_fusion.place_ref, bf16[512,1024]{1,0:T(8,128)(2,1)S(1)} %get-tuple-element.43.q_ref, f32[1024,256]{1,0:T(8,128)S(1)} %copy-done, f32[512,1024]{1,0:T(8,128)S(1)} %get-tuple-element.44.inner_ref.refs_3_, ...), custom_call_target="tpu_custom_call" | custom-call | flops 1024 | bytes 1024 | tf_op jit(solution)/shard_map/finish/pallas_call | solution.py:372
  73.9 0.6 collective-permute-start.18
  74.5 0.1 collective-permute-start.17
  74.6 1.7 %gating.1.gating_ref = f32[256,8192]{1,0:T(8,128)S(1)} custom-call(f32[1,8192]{1,0:T(1,128)S(1)} %bitcast.5, bf16[256,8192]{1,0:T(8,128)(2,1)S(1)} %copy-done.1, bf16[256,512]{1,0:T(8,128)(2,1)S(1)} %get-tuple-element.47.refs_0_), custom_call_target="tpu_custom_call" | custom-call | flops 1024 | bytes 1024 | tf_op jit(solution)/shard_map/gating/pallas_call | solution.py:410
  76.3 3.5 %collective-permute-done.15.refs_7_ = bf16[256,1024]{1,0:T(8,128)(2,1)S(1)} collective-permute-done((bf16[256,1024]{1,0:T(8,128)(2,1)S(1)}, bf16[256,1024]{1,0:T(8,128)(2,1)S(1)}, u32[]{:S(2)}, u32[]{:S(2)}) %collective-permute-start.15) | collective-permute-done | bytes 524320 | tf_op jit(solution)/shard_map/ppermute | solution.py:534
  79.8 4.2 %normalize.1 = bf16[256,8192]{1,0:T(8,128)(2,1)} custom-call(s32[4]{0:T(128)S(1)} %pad_add_fusion.place_ref, f32[256,8192]{1,0:T(8,128)S(1)} %gating.1.gating_ref, bf16[256,512]{1,0:T(8,128)(2,1)S(1)} %collective-permute-done.9.refs_4_.refs_0_, bf16[256,512]{1,0:T(8,128)(2,1)S(1)} %collective-permute-done.10.refs_5_.refs_1_, ...), custom_call_target="tpu_custom_call" | custom-call | flops 3000000000 | bytes 1000000 | tf_op jit(solution)/shard_map/normalize/pallas_call | solution.py:442
  (20 shorter events, 0.2 us)
Async XLA Ops:
  1.9 5.3 %collective-permute-start = (bf16[4,128,128]{2,1,0:T(8,128)(2,1)S(1)}, bf16[4,128,128]{2,1,0:T(8,128)(2,1)S(1)}, u32[]{:S(2)}, u32[]{:S(2)}) collective-permute-start(bf16[4,128,128]{2,1,0:T(8,128)(2,1)S(1)} %block_states.3.refs_0_.total_ref), channel_id=1, source_target_pairs={{0,4},{4,0},{8,12},{12,8},{16,20},{20,16},{24,28},{28,24},{1,5},{5... | collective-permute-start | bytes 393224 | tf_op jit(solution)/shard_map/ppermute | solution.py:483
  6.0 9.2 %collective-permute-start.2 = (bf16[4,128,128]{2,1,0:T(8,128)(2,1)S(1)}, bf16[4,128,128]{2,1,0:T(8,128)(2,1)S(1)}, u32[]{:S(2)}, u32[]{:S(2)}) collective-permute-start(bf16[4,128,128]{2,1,0:T(8,128)(2,1)S(1)} %block_states.4.refs_0_.total_ref), channel_id=1, source_target_pairs={{0,4},{4,0},{8,12},{12,8},{16,20},{20,16},{24,28},{28,24},{1,5},{5... | collective-permute-start | bytes 393224 | tf_op jit(solution)/shard_map/ppermute | solution.py:483
  7.3 5.5 %collective-permute-start.3 = (bf16[4,128,128]{2,1,0:T(8,128)(2,1)S(1)}, bf16[4,128,128]{2,1,0:T(8,128)(2,1)S(1)}, u32[]{:S(2)}, u32[]{:S(2)}) collective-permute-start(bf16[4,128,128]{2,1,0:T(8,128)(2,1)S(1)} %add_states.6.refs_0_.total_ref), channel_id=1, source_target_pairs={{0,8},{4,12},{8,0},{12,4},{16,24},{20,28},{24,16},{28,20},{1,9},{5... | collective-permute-start | bytes 393224 | tf_op jit(solution)/shard_map/ppermute | solution.py:483
  11.5 15.4 %collective-permute-start.1 = (bf16[8,128,128]{2,1,0:T(8,128)(2,1)S(1)}, bf16[8,128,128]{2,1,0:T(8,128)(2,1)S(1)}, u32[]{:S(2)}, u32[]{:S(2)}) collective-permute-start(bf16[8,128,128]{2,1,0:T(8,128)(2,1)S(1)} %block_states.5.refs_0_.total_ref), channel_id=1, source_target_pairs={{0,4},{4,0},{8,12},{12,8},{16,20},{20,16},{24,28},{28,24},{1,5},{5... | collective-permute-start | bytes 786440 | tf_op jit(solution)/shard_map/ppermute | solution.py:483
  12.8 2.7 %copy-start = (f32[1024,256]{1,0:T(8,128)S(1)}, f32[1024,256]{1,0:T(8,128)}, u32[]{:S(2)}) copy-start(f32[1024,256]{1,0:T(8,128)} %w_ref.23) | copy-start | bytes 3145732
  12.8 6.9 %collective-permute-start.5 = (bf16[4,128,128]{2,1,0:T(8,128)(2,1)S(1)}, bf16[4,128,128]{2,1,0:T(8,128)(2,1)S(1)}, u32[]{:S(2)}, u32[]{:S(2)}) collective-permute-start(bf16[4,128,128]{2,1,0:T(8,128)(2,1)S(1)} %add_states.7.refs_0_), channel_id=1, source_target_pairs={{0,16},{4,20},{8,24},{12,28},{16,0},{20,4},{24,8},{28,12},{1,17},{... | collective-permute-start | bytes 393224 | tf_op jit(solution)/shard_map/ppermute | solution.py:483
  15.3 10.6 %collective-permute-start.4 = (bf16[4,128,128]{2,1,0:T(8,128)(2,1)S(1)}, bf16[4,128,128]{2,1,0:T(8,128)(2,1)S(1)}, u32[]{:S(2)}, u32[]{:S(2)}) collective-permute-start(bf16[4,128,128]{2,1,0:T(8,128)(2,1)S(1)} %add_states.8.refs_0_.total_ref), channel_id=1, source_target_pairs={{0,8},{4,12},{8,0},{12,4},{16,24},{20,28},{24,16},{28,20},{1,9},{5... | collective-permute-start | bytes 393224 | tf_op jit(solution)/shard_map/ppermute | solution.py:483
  21.5 29.7 %collective-permute-start.10 = (bf16[256,512]{1,0:T(8,128)(2,1)S(1)}, bf16[256,512]{1,0:T(8,128)(2,1)S(1)}, u32[]{:S(2)}, u32[]{:S(2)}) collective-permute-start(bf16[256,512]{1,0:T(8,128)(2,1)S(1)} %get-tuple-element.31.refs_0_), channel_id=1, source_target_pairs={{0,3},{1,2},{2,1},{3,0},{4,7},{5,6},{6,5},{7,4},{8,11},{9,10},{10,... | collective-permute-start | bytes 786440 | tf_op jit(solution)/shard_map/ppermute | solution.py:534
  25.9 12.9 %collective-permute-start.6 = (bf16[4,128,128]{2,1,0:T(8,128)(2,1)S(1)}, bf16[4,128,128]{2,1,0:T(8,128)(2,1)S(1)}, u32[]{:S(2)}, u32[]{:S(2)}) collective-permute-start(bf16[4,128,128]{2,1,0:T(8,128)(2,1)S(1)} %add_states.9.refs_0_), channel_id=1, source_target_pairs={{0,16},{4,20},{8,24},{12,28},{16,0},{20,4},{24,8},{28,12},{1,17},{... | collective-permute-start | bytes 393224 | tf_op jit(solution)/shard_map/ppermute | solution.py:483
  27.0 10.4 %collective-permute-start.7 = (bf16[8,128,128]{2,1,0:T(8,128)(2,1)S(1)}, bf16[8,128,128]{2,1,0:T(8,128)(2,1)S(1)}, u32[]{:S(2)}, u32[]{:S(2)}) collective-permute-start(bf16[8,128,128]{2,1,0:T(8,128)(2,1)S(1)} %add_states.10.refs_0_.total_ref), channel_id=1, source_target_pairs={{0,8},{4,12},{8,0},{12,4},{16,24},{20,28},{24,16},{28,20},{1,9},{5... | collective-permute-start | bytes 786440 | tf_op jit(solution)/shard_map/ppermute | solution.py:483
  28.5 22.5 %collective-permute-start.9 = (bf16[256,512]{1,0:T(8,128)(2,1)S(1)}, bf16[256,512]{1,0:T(8,128)(2,1)S(1)}, u32[]{:S(2)}, u32[]{:S(2)}) collective-permute-start(bf16[256,512]{1,0:T(8,128)(2,1)S(1)} %get-tuple-element.38), channel_id=1, source_target_pairs={{0,2},{1,3},{2,0},{3,1},{4,6},{5,7},{6,4},{7,5},{8,10},{9,11},{10,... | collective-permute-start | bytes 786440 | tf_op jit(solution)/shard_map/ppermute | solution.py:534
  37.5 14.4 %collective-permute-start.8 = (bf16[8,128,128]{2,1,0:T(8,128)(2,1)S(1)}, bf16[8,128,128]{2,1,0:T(8,128)(2,1)S(1)}, u32[]{:S(2)}, u32[]{:S(2)}) collective-permute-start(bf16[8,128,128]{2,1,0:T(8,128)(2,1)S(1)} %add_states.11.refs_3_), channel_id=1, source_target_pairs={{0,16},{4,20},{8,24},{12,28},{16,0},{20,4},{24,8},{28,12},{1,17},{... | collective-permute-start | bytes 786440 | tf_op jit(solution)/shard_map/ppermute | solution.py:483
  40.7 29.5 %collective-permute-start.11 = (bf16[256,512]{1,0:T(8,128)(2,1)S(1)}, bf16[256,512]{1,0:T(8,128)(2,1)S(1)}, u32[]{:S(2)}, u32[]{:S(2)}) collective-permute-start(bf16[256,512]{1,0:T(8,128)(2,1)S(1)} %get-tuple-element.45), channel_id=1, source_target_pairs={{0,2},{1,3},{2,0},{3,1},{4,6},{5,7},{6,4},{7,5},{8,10},{9,11},{10,... | collective-permute-start | bytes 786440 | tf_op jit(solution)/shard_map/ppermute | solution.py:534
  41.3 29.0 %collective-permute-start.12 = (bf16[256,512]{1,0:T(8,128)(2,1)S(1)}, bf16[256,512]{1,0:T(8,128)(2,1)S(1)}, u32[]{:S(2)}, u32[]{:S(2)}) collective-permute-start(bf16[256,512]{1,0:T(8,128)(2,1)S(1)} %get-tuple-element.34.refs_0_), channel_id=1, source_target_pairs={{0,3},{1,2},{2,1},{3,0},{4,7},{5,6},{6,5},{7,4},{8,11},{9,10},{10,... | collective-permute-start | bytes 786440 | tf_op jit(solution)/shard_map/ppermute | solution.py:534
  51.0 23.5 %collective-permute-start.13 = (bf16[256,512]{1,0:T(8,128)(2,1)S(1)}, bf16[256,512]{1,0:T(8,128)(2,1)S(1)}, u32[]{:S(2)}, u32[]{:S(2)}) collective-permute-start(bf16[256,512]{1,0:T(8,128)(2,1)S(1)} %get-tuple-element.37.refs_3_), channel_id=1, source_target_pairs={{0,1},{1,0},{2,3},{3,2},{4,5},{5,4},{6,7},{7,6},{8,9},{9,8},{10,11... | collective-permute-start | bytes 786440 | tf_op jit(solution)/shard_map/ppermute | solution.py:534
  54.9 21.5 %collective-permute-start.14 = (bf16[256,1024]{1,0:T(8,128)(2,1)S(1)}, bf16[256,1024]{1,0:T(8,128)(2,1)S(1)}, u32[]{:S(2)}, u32[]{:S(2)}) collective-permute-start(bf16[256,1024]{1,0:T(8,128)(2,1)S(1)} %get-tuple-element.49), channel_id=1, source_target_pairs={{0,2},{1,3},{2,0},{3,1},{4,6},{5,7},{6,4},{7,5},{8,10},{9,11},{10,... | collective-permute-start | bytes 1572872 | tf_op jit(solution)/shard_map/ppermute | solution.py:534
  55.9 23.9 %collective-permute-start.15 = (bf16[256,1024]{1,0:T(8,128)(2,1)S(1)}, bf16[256,1024]{1,0:T(8,128)(2,1)S(1)}, u32[]{:S(2)}, u32[]{:S(2)}) collective-permute-start(bf16[256,1024]{1,0:T(8,128)(2,1)S(1)} %get-tuple-element.39.refs_0_), channel_id=1, source_target_pairs={{0,3},{1,2},{2,1},{3,0},{4,7},{5,6},{6,5},{7,4},{8,11},{9,10},{10,... | collective-permute-start | bytes 1572872 | tf_op jit(solution)/shard_map/ppermute | solution.py:534
  70.2 6.1 %collective-permute-start.16 = (bf16[256,512]{1,0:T(8,128)(2,1)S(1)}, bf16[256,512]{1,0:T(8,128)(2,1)S(1)}, u32[]{:S(2)}, u32[]{:S(2)}) collective-permute-start(bf16[256,512]{1,0:T(8,128)(2,1)S(1)} %get-tuple-element.42.refs_0_), channel_id=1, source_target_pairs={{0,1},{1,0},{2,3},{3,2},{4,5},{5,4},{6,7},{7,6},{8,9},{9,8},{10,11... | collective-permute-start | bytes 786440 | tf_op jit(solution)/shard_map/ppermute | solution.py:534
  72.1 2.5 %copy-start.1 = (bf16[256,8192]{1,0:T(8,128)(2,1)S(1)}, bf16[256,8192]{1,0:T(8,128)(2,1)}, u32[]{:S(2)}) copy-start(bf16[256,8192]{1,0:T(8,128)(2,1)} %gate_ref.1) | copy-start | bytes 12582916
  72.1 2.5 %copy-start.2 = (f32[8192]{0:T(1024)S(1)}, f32[8192]{0:T(1024)}, u32[]{:S(2)}) copy-start(f32[8192]{0:T(1024)} %param.11) | copy-start | bytes 98308
  73.9 2.4 %collective-permute-start.18 = (bf16[256,512]{1,0:T(8,128)(2,1)S(1)}, bf16[256,512]{1,0:T(8,128)(2,1)S(1)}, u32[]{:S(2)}, u32[]{:S(2)}) collective-permute-start(bf16[256,512]{1,0:T(8,128)(2,1)S(1)} %get-tuple-element.47.refs_0_), channel_id=1, source_target_pairs={{0,1},{1,0},{2,3},{3,2},{4,5},{5,4},{6,7},{7,6},{8,9},{9,8},{10,11... | collective-permute-start | bytes 786440 | tf_op jit(solution)/shard_map/ppermute | solution.py:534
  74.5 1.8 %collective-permute-start.17 = (bf16[256,512]{1,0:T(8,128)(2,1)S(1)}, bf16[256,512]{1,0:T(8,128)(2,1)S(1)}, u32[]{:S(2)}, u32[]{:S(2)}) collective-permute-start(bf16[256,512]{1,0:T(8,128)(2,1)S(1)} %get-tuple-element.46.refs_3_), channel_id=1, source_target_pairs={{0,1},{1,0},{2,3},{3,2},{4,5},{5,4},{6,7},{7,6},{8,9},{9,8},{10,11... | collective-permute-start | bytes 786440 | tf_op jit(solution)/shard_map/ppermute | solution.py:534
